TPU v7x, 32 devices: a whole 2x2x4 slice. The times are simulated.
32 devices in a mesh: pairs: 8 (over z, x), ints: 4 (over y, core).
Axes of the slice: x: 2, y: 2, z: 4, core: 2. Of those that a mesh axis runs over, the one named last changes fastest.
Arguments:
- amps: float32 [16, 256, 256], P('pairs', 'ints'), may hold values from -0.8 to 0.8
- resid_rest: float32 [16, 256, 256], P('pairs', 'ints'), may hold values from -6 to 6
- int_blocks: bfloat16 [8, 256, 256], P('pairs'), may hold values from -0.375 to 0.375
- virt_energy: float32 [16, 256], P('pairs'), may hold values from 0.5 to 3
- pair_energy: float32 [16], P('pairs'), may hold values from -2 to -0.5
- item_block: int32 [2048, 1], P(('pairs', 'ints')), may hold values from 0 to 7; in each aligned block of 64 rows (0 to 63, 64 to 127, ...) at most 12 rows name the same one
- share_owner: int32 [768, 1], P('pairs'), may hold values from 0 to 7; in each aligned block of 96 rows (0 to 95, 96 to 191, ...) at most 18 rows name the same one
- share_pair: int32 [768, 1], P('pairs'), may hold values from 0 to 1
- share_amp: int32 [768, 1], P('pairs'), may hold values from 0 to 1
- transpose_pair: int32 [16], P('pairs'), may hold values from 0 to 15, as said below
Outputs:
- update: float32 [16, 256, 256], P('pairs', 'ints')
Inputs may be any that keep to these rules, and one draw needn't show every extreme that they name: `item_block`: within each aligned block of 64 rows no value occurs more than 12 times, and some value occurs exactly 12 times. `share_owner`: within each aligned block of 96 rows no value occurs more than 18 times, and some value occurs exactly 18 times. `transpose_pair`: A permutation equal to its own inverse; pair p maps into the block of 2 consecutive pairs whose block number is (p // 2 + 16 // 4) modulo 16 // 2.
All inputs are finite; a program needn't handle non-finite values.
Results may differ from a plain program's by a relative error of at most 0.008.
Values may be sent and summed in bfloat16 or wider, within the bound.
No kernel may reach another device: no remote copies, remote signals or barrier semaphores. Data moves between devices by JAX's collectives and lax.ppermute only.
A program may use at most 64 MiB of HBM per device.

v0:
```python
import jax
import jax.numpy as jnp
from jax import lax
from jax.sharding import PartitionSpec as P


def from_behind(value, axis, steps):
    count = lax.axis_size(axis)
    pairs = [(source, (source + steps) % count) for source in range(count)]
    return lax.ppermute(value, axis, pairs)


def slot_ranks(targets, n_groups):
    match_hits = (targets[:, None] == jnp.arange(n_groups, dtype=jnp.int32)[None, :]).astype(
        jnp.int32
    )
    before = jnp.cumsum(match_hits, axis=0) - match_hits
    return jnp.sum(before * match_hits, axis=1)


def body(
    amps,
    resid_rest,
    int_blocks,
    virt_energy,
    pair_energy,
    item_block,
    share_owner,
    share_pair,
    share_amp,
    transpose_pair,
):
    n_pairs = lax.axis_size("pairs")
    pair_index = lax.axis_index("pairs")
    quarter = lax.axis_index("ints")
    pair_count, row_count, domain = amps.shape
    amp_half = amps.astype(jnp.bfloat16)
    n_items = item_block.shape[0]
    item_height = pair_count * row_count // n_items
    item_rows = amp_half.reshape(n_items, item_height, domain)
    block_targets = item_block[:, 0]
    cap_items = max(2, 3 * n_items // (2 * n_pairs))
    item_slot = block_targets * cap_items + slot_ranks(block_targets, n_pairs)
    outgoing = (
        jnp.zeros((n_pairs * cap_items, item_height, domain), jnp.bfloat16)
        .at[item_slot]
        .set(item_rows)
    )
    outgoing = outgoing.reshape(n_pairs, cap_items, item_height, domain)
    resident = int_blocks[0]
    arrived = lax.all_to_all(outgoing, "pairs", split_axis=0, concat_axis=0, tiled=True)
    leading = arrived.shape[:3]
    product = jnp.dot(arrived.reshape(-1, domain), resident, preferred_element_type=jnp.float32)
    product = product.astype(jnp.bfloat16).reshape(leading + (domain,))
    returned = lax.all_to_all(product, "pairs", split_axis=0, concat_axis=0, tiled=True)
    x_rows = returned.reshape(n_pairs * cap_items, item_height, domain)[item_slot]
    x_rows = x_rows.reshape(pair_count, row_count, domain)
    partial_value = jnp.einsum("pac,pad->pcd", amp_half, x_rows, preferred_element_type=jnp.float32)
    intermed = lax.psum_scatter(
        partial_value.astype(jnp.bfloat16), "ints", scatter_dimension=1, tiled=True
    )
    amp_full = lax.all_gather(amp_half, "ints", axis=1, tiled=True)
    owners = share_owner[:, 0]
    wanted = share_pair[:, 0]
    n_req = owners.shape[0]
    per_pair = n_req // pair_count
    source_global = owners * pair_count + wanted
    empty_rows = jnp.zeros((n_req, row_count, domain), jnp.bfloat16)
    piece = lax.all_gather(intermed, "pairs", axis=0, tiled=True)
    start = jnp.int32(0)
    local = jnp.clip(source_global, 0, piece.shape[0] - 1)
    inside = (source_global >= start) & (source_global < start + piece.shape[0])
    picked = jnp.where(inside[:, None, None], piece[local], empty_rows)
    picked = picked.reshape(pair_count, per_pair, row_count, domain)
    partners = share_amp[:, 0].reshape(pair_count, per_pair)

    def cycle_one(packed):
        w_req, amp_index = packed
        return jnp.einsum(
            "kac,kcb->ab", w_req, amp_full[amp_index], preferred_element_type=jnp.float32
        )

    cycle_term = lax.map(cycle_one, (picked, partners))
    energies_rows = lax.dynamic_slice_in_dim(virt_energy, quarter * row_count, row_count, 1)
    divisor = energies_rows[:, :, None] + virt_energy[:, None, :] - pair_energy[:, None, None]
    scaled = (resid_rest + cycle_term) / divisor
    mirror_part = from_behind(scaled.astype(jnp.bfloat16), "pairs", n_pairs // 2).astype(
        scaled.dtype
    )
    turned = lax.all_to_all(
        mirror_part.astype(jnp.bfloat16), "ints", split_axis=2, concat_axis=1, tiled=True
    ).astype(mirror_part.dtype)
    partner_dev = (pair_index + n_pairs // 2) % n_pairs
    local_swap = transpose_pair - partner_dev * pair_count
    mirrored = jnp.transpose(turned[local_swap], (0, 2, 1))
    return -0.5 * (scaled + mirrored)


def solution(mesh):
    placed = (
        P("pairs", "ints", None),
        P("pairs", "ints", None),
        P("pairs", None, None),
        P("pairs", None),
        P("pairs"),
        P(("pairs", "ints"), None),
        P("pairs", None),
        P("pairs", None),
        P("pairs", None),
        P("pairs"),
    )
    return jax.shard_map(
        body, mesh=mesh, in_specs=placed, out_specs=P("pairs", "ints", None), check_vma=False
    )
```

profile of v0, /device:TPU:0, one launch (start us, length us, event | category | flops | bytes accessed | tf_op | source)
XLA Modules:
  0.0 157.2 jit_solution(7218802619027532439)
XLA Ops:
  6.5 0.8 fusion.15
  7.4 0.8 select_reduce_fusion
  8.9 0.9 convert_element_type.33
  9.9 0.7 broadcast_in_dim.35
  10.6 7.7 %scatter_fusion = bf16[96,2,256]{2,1,0:T(2,128)(2,1)} fusion(bf16[96,2,256]{2,1,0:T(2,128)(2,1)} %broadcast_in_dim.35, s32[64]{0:T(128)S(1)} %fusion.16, bf16[64,2,256]{2,1,0:T(2,128)(2,1)S(1)} %reshape.123), kind=kCustom, calls=%fused_computation.4 | custom fusion | bytes 196864 | tf_op jit(solution)/shard_map/scatter | solution.py:47
  18.3 7.3 %all-to-all-start = ((bf16[8,12,2,256]{3,2,1,0:T(2,128)(2,1)}), bf16[8,12,2,256]{3,2,1,0:T(2,128)(2,1)S(1)}, u32[]{:S(2)}, u32[]{:S(2)}) async-start(bf16[8,12,2,256]{3,2,1,0:T(2,128)(2,1)} %bitcast.8), calls=%async_computation | async-start | bytes 196608 | tf_op jit(solution)/shard_map/all_to_all | solution.py:51
  25.6 0.8 constant_dynamic-slice_fusion.2
  26.3 0.7 and_reduce_fusion
  27.0 5.7 %all-to-all-done = bf16[8,12,2,256]{3,2,1,0:T(2,128)(2,1)S(1)} async-done(((bf16[8,12,2,256]{3,2,1,0:T(2,128)(2,1)}), bf16[8,12,2,256]{3,2,1,0:T(2,128)(2,1)S(1)}, u32[]{:S(2)}, u32[]{:S(2)}) %all-to-all-start) | async-done | bytes 98336 | tf_op jit(solution)/shard_map/all_to_all | solution.py:51
  32.9 0.7 reshape.82
  33.6 3.4 %all-to-all-start.1 = ((bf16[8,12,2,256]{3,2,1,0:T(2,128)(2,1)}), bf16[8,12,2,256]{3,2,1,0:T(2,128)(2,1)S(1)}, u32[]{:S(2)}, u32[]{:S(2)}) async-start(bf16[8,12,2,256]{3,2,1,0:T(2,128)(2,1)} %reshape.82), calls=%async_computation.1 | async-start | bytes 196608 | tf_op jit(solution)/shard_map/all_to_all | solution.py:55
  37.7 6.3 %all-to-all-done.1 = bf16[8,12,2,256]{3,2,1,0:T(2,128)(2,1)S(1)} async-done(((bf16[8,12,2,256]{3,2,1,0:T(2,128)(2,1)}), bf16[8,12,2,256]{3,2,1,0:T(2,128)(2,1)S(1)}, u32[]{:S(2)}, u32[]{:S(2)}) %all-to-all-start.1) | async-done | bytes 98336 | tf_op jit(solution)/shard_map/all_to_all | solution.py:55
  44.0 0.7 gather_fusion.1
  45.1 0.9 copy.14
  46.0 5.8 %all_gather.7 = bf16[2,256,256]{2,1,0:T(8,128)(2,1)S(1)} all-gather(bf16[2,64,256]{2,1,0:T(8,128)(2,1)S(1)} %convert_element_type.33), channel_id=1, replica_groups=mesh['pairs'=8,'ints'=4] {'ints'}, dimensions={1}, use_global_device_ids=true | all-gather | bytes 327680 | tf_op jit(solution)/shard_map/all_gather | solution.py:62
  52.4 0.7 reduce.7
  55.1 20.6 %all-reduce.3.cloned.1.call-done = bf16[2,256,256]{2,0,1:T(2,128)(2,1)} async-done(((bf16[2,256,256]{2,0,1:T(2,128)(2,1)}), bf16[2,256,256]{2,0,1:T(2,128)(2,1)}) %all-reduce.3.cloned.1.call-update) | async-done | bytes 262160
  75.8 0.9 constant_dynamic-slice_fusion.1
  76.7 31.4 %all_gather.6 = bf16[16,64,256]{2,1,0:T(8,128)(2,1)S(1)} all-gather(bf16[2,64,256]{2,1,0:T(8,128)(2,1)S(1)} %copy.15), channel_id=1, replica_groups=mesh['pairs'=8,'ints'=4] {'pairs'}, dimensions={0}, use_global_device_ids=true | all-gather | bytes 589824 | tf_op jit(solution)/shard_map/all_gather | solution.py:69
  108.1 2.6 %gather_fusion.2 = bf16[96,64,256]{2,1,0:T(8,128)(2,1)} fusion(bf16[16,64,256]{2,1,0:T(8,128)(2,1)S(1)} %all_gather.6, s32[1024]{0:T(1024)S(1)} %pad_clamp_fusion.2), kind=kCustom, calls=%fused_computation.2 | custom fusion | bytes 6291840 | tf_op jit(solution)/shard_map/gather | solution.py:73
  110.7 2.2 %broadcast_select_fusion = bf16[2,48,64,256]{3,2,1,0:T(8,128)(2,1)S(1)} fusion(bf16[2,48,64,256]{3,2,1,0:T(8,128)(2,1)} %bitcast.66, pred[2,48]{1,0:T(4,128)(4,1)S(1)} %and.18), kind=kLoop, calls=%fused_computation.16 | loop fusion | flops 1572864 | bytes 6291552 | tf_op jit(solution)/shard_map/jit(_where)/select_n | solution.py:73
  112.9 20.1 %while.10 = (s32[]{:T(128)}, f32[2,64,256]{2,1,0:T(8,128)}, bf16[2,48,64,256]{3,2,1,0:T(8,128)(2,1)S(1)}, s32[2,48]{1,0:T(2,128)}, bf16[2,256,256]{2,1,0:T(8,128)(2,1)S(1)}, /*index=5*/s32[]{:T(128)}) while((s32[]{:T(128)}, f32[2,64,256]{2,1,0:T(8,128)}, bf16[2,48,64,256]{3,2,1,0:T(8,128)(2,1)S(1)}, s32[2,48]{1,0:T(2,128)}, ...), condition=%wide.region_5.6_spmd, body=%wide.region_4.5_spmd.sunk | while | flops 402654368 | bytes 20518736 | solution.py:83
  113.5 4.8 %gather_fusion = bf16[48,256,256]{2,1,0:T(8,128)(2,1)} fusion(bf16[2,256,256]{2,1,0:T(8,128)(2,1)S(1)} %get-tuple-element.90, s32[1024]{0:T(1024)S(1)} %pad_clamp_fusion.5), kind=kCustom, calls=%fused_computation.clone.1 | custom fusion | bytes 12583104 | tf_op jit(solution)/shard_map/while/body/eval_jaxpr/gather | solution.py:80
  118.3 4.6 %fusion.30 = f32[2,64,256]{2,1,0:T(8,128)} fusion(f32[2,64,256]{2,1,0:T(8,128)} %get-tuple-element.81, s32[]{:T(128)S(6)} %copy.25, bf16[48,256,256]{2,1,0:T(8,128)(2,1)} %gather_fusion, bf16[2,48,64,256]{3,2,1,0:T(8,128)(2,1)S(1)} %get-tuple-element.88), kind=kOutput, calls=%fused_computation.9.clone.1 | convolution fusion | flops 402653184 | bytes 7930880 | tf_op jit(solution)/shard_map/while/body/eval_jaxpr/kac,kcb->ab/dot_general | solution.py:79
  123.6 4.8 %gather_fusion = bf16[48,256,256]{2,1,0:T(8,128)(2,1)} fusion(bf16[2,256,256]{2,1,0:T(8,128)(2,1)S(1)} %get-tuple-element.90, s32[1024]{0:T(1024)S(1)} %pad_clamp_fusion.5), kind=kCustom, calls=%fused_computation.clone.1 | custom fusion | bytes 12583104 | tf_op jit(solution)/shard_map/while/body/eval_jaxpr/gather | solution.py:80
  128.3 4.6 %fusion.30 = f32[2,64,256]{2,1,0:T(8,128)} fusion(f32[2,64,256]{2,1,0:T(8,128)} %get-tuple-element.81, s32[]{:T(128)S(6)} %copy.25, bf16[48,256,256]{2,1,0:T(8,128)(2,1)} %gather_fusion, bf16[2,48,64,256]{3,2,1,0:T(8,128)(2,1)S(1)} %get-tuple-element.88), kind=kOutput, calls=%fused_computation.9.clone.1 | convolution fusion | flops 402653184 | bytes 7930880 | tf_op jit(solution)/shard_map/while/body/eval_jaxpr/kac,kcb->ab/dot_general | solution.py:79
  133.0 1.1 fusion.18
  134.8 4.5 %collective-permute-done = bf16[2,64,256]{2,1,0:T(8,128)(2,1)S(1)} collective-permute-done((bf16[2,64,256]{2,1,0:T(8,128)(2,1)S(1)}, bf16[2,64,256]{2,1,0:T(8,128)(2,1)S(1)}, u32[]{:S(2)}, u32[]{:S(2)}) %collective-permute-start) | collective-permute-done | bytes 65568 | tf_op jit(solution)/shard_map/ppermute | solution.py:10
  139.4 0.8 reshape.146
  140.2 3.3 %all-to-all-start.2 = ((bf16[4,2,4096]{2,1,0:T(2,128)(2,1)}), bf16[4,2,4096]{2,1,0:T(2,128)(2,1)S(1)}, u32[]{:S(2)}, u32[]{:S(2)}) async-start(bf16[4,2,4096]{2,1,0:T(2,128)(2,1)} %reshape.146), calls=%async_computation.2 | async-start | bytes 131072 | tf_op jit(solution)/shard_map/all_to_all | solution.py:90
  143.5 4.1 %all-to-all-done.2 = bf16[4,2,4096]{2,1,0:T(2,128)(2,1)S(1)} async-done(((bf16[4,2,4096]{2,1,0:T(2,128)(2,1)}), bf16[4,2,4096]{2,1,0:T(2,128)(2,1)S(1)}, u32[]{:S(2)}, u32[]{:S(2)}) %all-to-all-start.2) | async-done | bytes 65568 | tf_op jit(solution)/shard_map/all_to_all | solution.py:90
  148.6 1.7 %fusion.13 = f32[2,64,256]{2,1,0:T(8,128)} fusion(f32[2,256,64]{1,2,0:T(8,128)S(1)} %gather_fusion.3, f32[2]{0:T(128)S(1)} %copy-done.2, f32[2,256]{1,0:T(2,128)S(1)} %copy-done.1, f32[2,64]{1,0:T(2,128)S(1)} %constant_dynamic-slice_fusion.2, f32[2,64,256]{2,1,0:T(8,128)} %param.13, f32[2,64,256]{2,1,0:T(8,128)} %get-tuple-element.32), kind=kLoop, calls=%fused_computation.22 | loop fusion | flops 196608 | bytes 526856 | tf_op jit(solution)/shard_map/mul | solution.py:96
  (40 shorter events, 7.2 us)
Async XLA Ops:
  6.5 26.2 %copy-start = (bf16[1,256,256]{2,1,0:T(8,128)(2,1)S(1)}, bf16[1,256,256]{2,1,0:T(8,128)(2,1)}, u32[]{:S(2)}) copy-start(bf16[1,256,256]{2,1,0:T(8,128)(2,1)} %param.14) | copy-start | bytes 393220
  6.5 47.2 %copy-start.4 = (u32[32]{0:T(128)S(1)}, u32[32]{0:T(128)}, u32[]{:S(2)}) copy-start(u32[32]{0:T(128)} %constant.77) | copy-start | bytes 388
  6.5 45.9 %copy-start.3 = (s32[96,1]{0,1:T(1,128)S(1)}, s32[96,1]{0,1:T(1,128)}, u32[]{:S(2)}) copy-start(s32[96,1]{0,1:T(1,128)} %param.20) | copy-start | bytes 1156
  18.3 14.4 %all-to-all-start = ((bf16[8,12,2,256]{3,2,1,0:T(2,128)(2,1)}), bf16[8,12,2,256]{3,2,1,0:T(2,128)(2,1)S(1)}, u32[]{:S(2)}, u32[]{:S(2)}) async-start(bf16[8,12,2,256]{3,2,1,0:T(2,128)(2,1)} %bitcast.8), calls=%async_computation | async-start | bytes 196608 | tf_op jit(solution)/shard_map/all_to_all | solution.py:51
  33.6 10.4 %all-to-all-start.1 = ((bf16[8,12,2,256]{3,2,1,0:T(2,128)(2,1)}), bf16[8,12,2,256]{3,2,1,0:T(2,128)(2,1)S(1)}, u32[]{:S(2)}, u32[]{:S(2)}) async-start(bf16[8,12,2,256]{3,2,1,0:T(2,128)(2,1)} %reshape.82), calls=%async_computation.1 | async-start | bytes 196608 | tf_op jit(solution)/shard_map/all_to_all | solution.py:55
  37.0 38.8 %all-reduce.3.cloned.1.call-start = ((), (), s32[]{:S(2)}) async-start(), calls=%async_computation.3 | async-start | bytes 524288
  112.8 20.1 %copy-start.1 = (f32[2,256]{1,0:T(2,128)S(1)}, f32[2,256]{1,0:T(2,128)}, u32[]{:S(2)}) copy-start(f32[2,256]{1,0:T(2,128)} %param.15) | copy-start | bytes 6148
  112.8 20.1 %copy-start.2 = (f32[2]{0:T(128)S(1)}, f32[2]{0:T(128)}, u32[]{:S(2)}) copy-start(f32[2]{0:T(128)} %param.16) | copy-start | bytes 28
  134.0 5.2 %collective-permute-start = (bf16[2,64,256]{2,1,0:T(8,128)(2,1)S(1)}, bf16[2,64,256]{2,1,0:T(8,128)(2,1)S(1)}, u32[]{:S(2)}, u32[]{:S(2)}) collective-permute-start(bf16[2,64,256]{2,1,0:T(8,128)(2,1)S(1)} %fusion.18), channel_id=1, source_target_pairs={{0,16},{4,20},{8,24},{12,28},{16,0},{20,4},{24,8},{28,12},{1,17},{... | collective-permute-start | bytes 196616 | tf_op jit(solution)/shard_map/ppermute | solution.py:10
  140.2 7.4 %all-to-all-start.2 = ((bf16[4,2,4096]{2,1,0:T(2,128)(2,1)}), bf16[4,2,4096]{2,1,0:T(2,128)(2,1)S(1)}, u32[]{:S(2)}, u32[]{:S(2)}) async-start(bf16[4,2,4096]{2,1,0:T(2,128)(2,1)} %reshape.146), calls=%async_computation.2 | async-start | bytes 131072 | tf_op jit(solution)/shard_map/all_to_all | solution.py:90
Sparse Core Ops, SparseCore 0:
  46.1 29.6 all-reduce.2
where the time goes:
time: 158 us; the launch traced here: 157 us
  waiting for transfers between devices  41.2 us (26%)
  blocking collectives  37.2 us (24%)
  local copies, waits for them, and re-layouts  28.5 us (18%)
  between operations  14.3 us (9%)
  starting transfers between devices  14 us (9%)
  other arithmetic  12.3 us (8%)
  matrix products  9.67 us (6%)
    all_gather x1, blocking collectives, body(): piece = lax.all_gather(intermed, 'pairs', axis=0, tiled=True)  31.4 us
    unnamed x2, waiting for transfers between devices  20.6 us
    gather x2, local copies, waits for them, and re-layouts, cycle_one(): amp_full[amp_index]  9.61 us
    dot_general x2, matrix products, cycle_one(): jnp.einsum('kac,kcb->ab', w_req, amp_full[amp_index], preferred_element_t...  9.23 us
    scatter x1, local copies, waits for them, and re-layouts, body(): outgoing = jnp.zeros((n_pairs * cap_items, item_height, domain), jnp.bflo...  7.74 us
    all_to_all x1, starting transfers between devices, body(): lax.all_to_all(outgoing, 'pairs', split_axis=0, concat_axis=0, tiled=True)  7.25 us
    all_to_all x1, waiting for transfers between devices, body(): lax.all_to_all(product, 'pairs', split_axis=0, concat_axis=0, tiled=True)  6.33 us
    all_gather x1, blocking collectives, body(): amp_full = lax.all_gather(amp_half, 'ints', axis=1, tiled=True)  5.79 us
  transfers between devices with their start and end apart: 5, of which 5 were waited for; matrix products, arithmetic and copies ran while one was open for 3% of the time, Pallas kernels for 0%

commit v1 on v0

v1 whole, which is shorter than its diff:
```python
import functools

import jax
import jax.numpy as jnp
from jax import lax
from jax.experimental import pallas as pl
from jax.experimental.pallas import tpu as pltpu
from jax.sharding import PartitionSpec as P

F32, BF16 = jnp.float32, jnp.bfloat16
DIRECT = 16
NT = (((1,), (1,)), ((), ()))
TN = (((0,), (0,)), ((), ()))


def dot(a, b, dims=(((1,), (0,)), ((), ()))):
    return lax.dot_general(a, b, dims, preferred_element_type=F32)


def iota(shape, dim):
    return lax.broadcasted_iota(jnp.int32, shape, dim)


def partner(value, axis, offset):
    count = lax.axis_size(axis)
    return lax.ppermute(value, axis, [(source, source ^ offset) for source in range(count)])


def gathered(value, axis):
    count = lax.axis_size(axis)
    if count > DIRECT:
        return [lax.all_gather(value, axis, axis=0, tiled=False)]
    return [value] + [partner(value, axis, offset) for offset in range(1, count)]


def prepare(amps, resid, block, virt, pair, items, owners, wanted, share, rows_out, bt_out, far_out):
    pairs, height, domain = amps.shape
    quarter = lax.axis_index("ints")
    rows = pairs * height
    amp_half = amps[...].astype(BF16)
    rows_out[:, :, :domain] = amp_half
    n_items = items.shape[1]
    lanes = rows_out.shape[2] - domain
    spread = (iota((rows, n_items), 0) * n_items // rows == iota((rows, n_items), 1)).astype(BF16)
    named = jnp.broadcast_to(items[...].astype(F32), (lanes, n_items)).astype(BF16)
    rows_out[:, :, domain:] = dot(spread, named, NT).astype(BF16).reshape(pairs, height, lanes)

    chosen = (iota((height, domain), 1) == iota((height, domain), 0) + quarter * height).astype(BF16)
    bt_out[...] = dot(chosen, block[0], NT).astype(BF16)

    far_out[:rows, :] = amp_half.reshape(rows, domain)
    far_out[rows : 2 * rows, :] = resid[...].astype(BF16).reshape(rows, domain)
    n_req = owners.shape[1]
    source = owners[...] * pairs + wanted[...]
    hits = (source == iota((domain, n_req), 0)).astype(BF16)
    row, col = iota((8, n_req), 0), iota((8, n_req), 1)
    into = ((col // (n_req // pairs) == row // pairs) & (share[...] == row % pairs)).astype(BF16)
    counts = dot(into, hits, NT)
    row = iota((8, domain), 0)
    energy = jnp.zeros((8, domain), F32)
    for p in range(pairs):
        energy = jnp.where(row == p, virt[p : p + 1, :], energy)
        energy = jnp.where(row == pairs + p, pair[p], energy)
    high = energy.astype(BF16).astype(F32)
    middle = (energy - high).astype(BF16).astype(F32)
    low = energy - high - middle
    far_out[2 * rows :, :] = jnp.concatenate([counts, high, middle, low], axis=0).astype(BF16)


def intermediate(n_rows, *refs):
    pieces, blocks, out = refs[:n_rows], refs[n_rows:-1], refs[-1]
    pairs, height, _ = pieces[0].shape
    domain = blocks[0].shape[-1]
    group = lax.axis_index("pairs")
    x = [jnp.concatenate([piece[p, :, :domain] for piece in pieces], axis=0) for p in range(pairs)]
    x_all = jnp.concatenate(x, axis=0)
    ids = jnp.concatenate([piece[p, :, domain:] for p in range(pairs) for piece in pieces], axis=0)
    ids = ids.astype(F32).astype(jnp.int32)
    total, lanes = x_all.shape[0], 2 * height
    first = iota((total, lanes), 1) < height

    def chosen(two, low, high):
        return jnp.where(ids == jnp.where(first, low, high), dot(x_all, two, NT), 0.0)

    if len(blocks) > 1:
        product = sum(
            chosen(jnp.concatenate([blocks[k][...], blocks[k + 1][...]], axis=0), group ^ k, group ^ (k + 1))
            for k in range(0, len(blocks), 2)
        )
    else:

        def step(k, sofar):
            two = blocks[0][pl.ds(2 * k, 2)].reshape(lanes, domain)
            return sofar + chosen(two, 2 * k, 2 * k + 1)

        product = lax.fori_loop(0, blocks[0].shape[0] // 2, step, jnp.zeros((total, lanes), F32))
    product = product.astype(BF16)
    for p in range(pairs):
        both = dot(product[p * domain : (p + 1) * domain], x[p], TN)
        out[p * height : (p + 1) * height, :] = (both[:height] + both[height:]).astype(BF16)


def cycle(n_sends, rows_own, resid, near, far, swap, *refs):
    units, (own_out, *sends), (here, there) = refs[: -n_sends - 3], refs[-n_sends - 3 : -2], refs[-2:]
    pairs, height, domain = resid.shape
    rows = pairs * height
    group, quarter = lax.axis_index("pairs"), lax.axis_index("ints")
    n_pairs = lax.axis_size("pairs")
    terms = pairs * pairs
    lanes = -(-n_pairs * pairs // 128) * 128
    counts = jnp.concatenate([near[2 * rows : 2 * rows + 8, :lanes], far[2 * rows : 2 * rows + 8, :lanes]], axis=0)
    tall = 2 * terms * height
    which = iota((tall, 16), 0) // height
    which = jnp.where(which < terms, which, which - terms + 8)
    spread = dot((which == iota((tall, 16), 1)).astype(BF16), counts).astype(BF16)
    same = iota((tall, rows), 0) % height == iota((tall, rows), 1) % height

    def weights(source_group):
        place = iota((lanes, rows), 0) == source_group * pairs + iota((lanes, rows), 1) // height
        return jnp.where(same, dot(spread, place.astype(BF16)), 0.0).astype(BF16)

    if len(units) > 1:
        mixed = sum(dot(weights(group ^ k), unit[...]) for k, unit in enumerate(units))
    else:
        mixed = lax.fori_loop(
            0,
            units[0].shape[0],
            lambda k, sofar: sofar + dot(weights(k), units[0][k]),
            jnp.zeros((tall, domain), F32),
        )
    mixed = mixed.astype(BF16)

    start = pl.multiple_of(quarter * height, height)
    amps_near = rows_own[:, :, :domain].reshape(rows, domain)
    amps_far = far[:rows, :]

    def fill(target, side, amps, packed, terms_of):
        parts = packed[2 * rows + 8 : 2 * rows + 32, :].astype(F32)
        energy = parts[:8] + parts[8:16] + parts[16:24]
        tall_energy = energy.T
        for p in range(pairs):
            at = (side * pairs + p) * rows
            target[p] = dot(mixed[at : at + rows], amps, TN)
            target[p, pl.ds(start, height), :] += terms_of(p)
            divisor = tall_energy[:, p : p + 1] + energy[p : p + 1] - energy[pairs + p : pairs + p + 1]
            target[p] = target[p] / divisor

    fill(there, 1, amps_far, far, lambda p: far[rows + p * height : rows + (p + 1) * height, :].astype(F32))
    fill(here, 0, amps_near, near, lambda p: resid[p])
    base = (group ^ (n_pairs // 2)) * pairs
    for p in range(pairs):
        here[p] += there[swap[p] - base].T
    own_out[...] = here[:, pl.ds(start, height), :]
    for offset, send in enumerate(sends, 1):
        to = pl.multiple_of((quarter ^ offset) * height, height)
        send[...] = here[:, pl.ds(to, height), :].astype(BF16)


VM = pl.BlockSpec(memory_space=pltpu.VMEM)
SM = pl.BlockSpec(memory_space=pltpu.SMEM)


def call(kernel, outs, in_specs, name, scratch=()):
    return pl.pallas_call(
        kernel,
        out_shape=outs,
        in_specs=in_specs,
        out_specs=jax.tree.map(lambda _: VM, outs),
        scratch_shapes=scratch,
        name=name,
        compiler_params=pltpu.CompilerParams(vmem_limit_bytes=48 * 1024 * 1024),
    )


def body(
    amps,
    resid_rest,
    int_blocks,
    virt_energy,
    pair_energy,
    item_block,
    share_owner,
    share_pair,
    share_amp,
    transpose_pair,
):
    n_pairs, n_ints = lax.axis_size("pairs"), lax.axis_size("ints")
    pairs, height, domain = amps.shape
    rows = pairs * height
    shape = jax.ShapeDtypeStruct
    rows_own, bt, near = call(
        prepare,
        [
            shape((pairs, height, domain + 128), BF16),
            shape((height, domain), BF16),
            shape((2 * rows + 32, domain), BF16),
        ],
        [VM, VM, VM, VM, SM, VM, VM, VM, VM],
        "prepare",
    )(
        amps,
        resid_rest,
        int_blocks,
        virt_energy,
        pair_energy,
        item_block.reshape(1, -1),
        share_owner.reshape(1, -1),
        share_pair.reshape(1, -1),
        share_amp.reshape(1, -1),
    )
    blocks = gathered(bt, "pairs")
    pieces = [rows_own] + [partner(rows_own, "ints", k) for k in range(1, n_ints)]
    far = partner(near, "pairs", n_pairs // 2)
    inter = call(
        functools.partial(intermediate, n_ints),
        shape((rows, domain), BF16),
        [VM] * (n_ints + len(blocks)),
        "intermediate",
    )(*pieces, *blocks)
    units = gathered(inter, "pairs")
    own, *sends = call(
        functools.partial(cycle, n_ints - 1),
        [shape((pairs, height, domain), F32)] + [shape((pairs, height, domain), BF16)] * (n_ints - 1),
        [VM, VM, VM, VM, SM] + [VM] * len(units),
        "cycle",
        [pltpu.VMEM((pairs, domain, domain), F32)] * 2,
    )(rows_own, resid_rest, near, far, transpose_pair, *units)
    for offset, send in enumerate(sends, 1):
        own = own + partner(send, "ints", offset).astype(F32)
    return -0.5 * own


def solution(mesh):
    placed = (
        P("pairs", "ints", None),
        P("pairs", "ints", None),
        P("pairs", None, None),
        P("pairs", None),
        P("pairs"),
        P(("pairs", "ints"), None),
        P("pairs", None),
        P("pairs", None),
        P("pairs", None),
        P("pairs"),
    )
    return jax.shard_map(
        body, mesh=mesh, in_specs=placed, out_specs=P("pairs", "ints", None), check_vma=False
    )
```

time: 158 us -> 54.5 us (0.34)
  blocking collectives: 37.2 us -> 0 us
  waiting for transfers between devices: 41.2 us -> 14.8 us
  local copies, waits for them, and re-layouts: 28.5 us -> 3.44 us
  starting transfers between devices: 14 us -> 31.1 us
  between operations: 14.3 us -> 0.09 us
  other arithmetic: 12.3 us -> 0.69 us
  matrix products: 9.67 us -> 0 us
  Pallas kernels: 0 us -> 4.11 us
    all_gather x2 -> x0, blocking collectives: 37.2 us -> none  [the longest x1 31.4 us: body(): piece = lax.all_gather(intermed, 'pairs', axis=0, tiled=True)]
    ppermute x1 -> x21, starting transfers between devices: 0.07 us -> 31.1 us  [partner(): lax.ppermute(value, axis, [(source, source ^ offset) for source in range(...]
    unnamed x2 -> x0, waiting for transfers between devices: 20.6 us -> none
    all_to_all x3 -> x0, waiting for transfers between devices: 16.1 us -> none  [the longest x1 6.33 us: body(): lax.all_to_all(product, 'pairs', split_axis=0, concat_axis=0, tiled=True)]
    all_to_all x3 -> x0, starting transfers between devices: 13.9 us -> none  [the longest x1 7.25 us: body(): lax.all_to_all(outgoing, 'pairs', split_axis=0, concat_axis=0, tiled=True)]
    gather x5 -> x0, local copies, waits for them, and re-layouts: 13.4 us -> none  [the longest x2 9.61 us: cycle_one(): amp_full[amp_index]]
    ppermute x1 -> x21, waiting for transfers between devices: 4.49 us -> 14.8 us  [partner(): lax.ppermute(value, axis, [(source, source ^ offset) for source in range(...]
    dot_general x4 -> x0, matrix products: 9.67 us -> none  [the longest x2 9.23 us: cycle_one(): jnp.einsum('kac,kcb->ab', w_req, amp_full[amp_index], preferred_element_t...]
  transfers between devices with their start and end apart: 5 -> 21, of which waited for: 5 -> 9; matrix products, arithmetic and copies ran while one was open for 3% -> 0% of each run, Pallas kernels for 0% -> 1%
where the time goes in v1:
time: 54.5 us; the launch traced here: 54.3 us
  starting transfers between devices  31.1 us (57%)
  waiting for transfers between devices  14.8 us (27%)
  Pallas kernels  4.11 us (8%)
  local copies, waits for them, and re-layouts  3.44 us (6%)
  other arithmetic  0.69 us (1%)
    ppermute x21, starting transfers between devices, partner(): lax.ppermute(value, axis, [(source, source ^ offset) for source in range(...  31.1 us
    ppermute x21, waiting for transfers between devices, partner(): lax.ppermute(value, axis, [(source, source ^ offset) for source in range(...  14.8 us
    unnamed x22, local copies, waits for them, and re-layouts  3.44 us
    pallas_call x1, Pallas kernels, body(): call(functools.partial(cycle, n_ints - 1), [shape((pairs, height, domain)...  2.73 us
  transfers between devices with their start and end apart: 21, of which 9 were waited for; matrix products, arithmetic and copies ran while one was open for 0% of the time, Pallas kernels for 1%

profile of v1, /device:TPU:0, one launch (start us, length us, event | category | flops | bytes accessed | tf_op | source)
XLA Modules:
  0.0 54.3 jit_solution(18345307033733569478)
XLA Ops:
  0.0 0.6 %copy-done.8 = s32[96,1]{0,1:T(1,128)S(1)} copy-done((s32[96,1]{0,1:T(1,128)S(1)}, s32[96,1]{0,1:T(1,128)}, u32[]{:S(2)}) %copy-start.8) | copy-done | bytes 408
  0.7 0.9 %copy-done = f32[2,64,256]{2,1,0:T(8,128)S(1)} copy-done((f32[2,64,256]{2,1,0:T(8,128)S(1)}, f32[2,64,256]{2,1,0:T(8,128)}, u32[]{:S(2)}) %copy-start) | copy-done | bytes 131096
  1.6 0.9 %copy-done.2 = f32[2,64,256]{2,1,0:T(8,128)S(1)} copy-done((f32[2,64,256]{2,1,0:T(8,128)S(1)}, f32[2,64,256]{2,1,0:T(8,128)}, u32[]{:S(2)}) %copy-start.2) | copy-done | bytes 131096
  2.5 0.9 %copy-done.3 = bf16[1,256,256]{2,1,0:T(8,128)(2,1)S(1)} copy-done((bf16[1,256,256]{2,1,0:T(8,128)(2,1)S(1)}, bf16[1,256,256]{2,1,0:T(8,128)(2,1)}, u32[]{:S(2)}) %copy-start.3) | copy-done | bytes 131096
  3.4 0.7 %prepare.1 = (bf16[2,64,384]{2,1,0:T(8,128)(2,1)S(1)}, bf16[64,256]{1,0:T(8,128)(2,1)S(1)}, bf16[288,256]{1,0:T(8,128)(2,1)S(1)}) custom-call(f32[2,64,256]{2,1,0:T(8,128)S(1)} %copy-done.2, f32[2,64,256]{2,1,0:T(8,128)S(1)} %copy-done, bf16[1,256,256]{2,1,0:T(8,128)(2,1)S(1)} %copy-done.3, f32[2,256]{1,0:T(2,128)S(1)} %copy-done.4, f32[2]{0:T(128)S(1)} %copy-done.5, ...), custom_call_target="tpu_custom_call" | custom-call | tf_op jit(solution)/shard_map/prepare/pallas_call | solution.py:191
  4.2 6.0 %collective-permute-start.10 = (bf16[64,256]{1,0:T(8,128)(2,1)S(1)}, bf16[64,256]{1,0:T(8,128)(2,1)S(1)}, u32[]{:S(2)}, u32[]{:S(2)}) collective-permute-start(bf16[64,256]{1,0:T(8,128)(2,1)S(1)} %get-tuple-element.14.refs_4_), channel_id=1, source_target_pairs={{0,28},{4,24},{8,20},{12,16},{16,12},{20,8},{24,4},{28,0},{1,29},{... | collective-permute-start | bytes 98312 | tf_op jit(solution)/shard_map/ppermute | solution.py:26
  10.5 0.8 %collective-permute-start.8 = (bf16[64,256]{1,0:T(8,128)(2,1)S(1)}, bf16[64,256]{1,0:T(8,128)(2,1)S(1)}, u32[]{:S(2)}, u32[]{:S(2)}) collective-permute-start(bf16[64,256]{1,0:T(8,128)(2,1)S(1)} %get-tuple-element.14.refs_4_), channel_id=1, source_target_pairs={{0,20},{4,16},{8,28},{12,24},{16,4},{20,0},{24,12},{28,8},{1,21},{... | collective-permute-start | bytes 98312 | tf_op jit(solution)/shard_map/ppermute | solution.py:26
  11.2 2.0 %collective-permute-start.7 = (bf16[64,256]{1,0:T(8,128)(2,1)S(1)}, bf16[64,256]{1,0:T(8,128)(2,1)S(1)}, u32[]{:S(2)}, u32[]{:S(2)}) collective-permute-start(bf16[64,256]{1,0:T(8,128)(2,1)S(1)} %get-tuple-element.14.refs_4_), channel_id=1, source_target_pairs={{0,16},{4,20},{8,24},{12,28},{16,0},{20,4},{24,8},{28,12},{1,17},{... | collective-permute-start | bytes 98312 | tf_op jit(solution)/shard_map/ppermute | solution.py:26
  13.2 2.3 %collective-permute-start.6 = (bf16[64,256]{1,0:T(8,128)(2,1)S(1)}, bf16[64,256]{1,0:T(8,128)(2,1)S(1)}, u32[]{:S(2)}, u32[]{:S(2)}) collective-permute-start(bf16[64,256]{1,0:T(8,128)(2,1)S(1)} %get-tuple-element.14.refs_4_), channel_id=1, source_target_pairs={{0,12},{4,8},{8,4},{12,0},{16,28},{20,24},{24,20},{28,16},{1,13},{... | collective-permute-start | bytes 98312 | tf_op jit(solution)/shard_map/ppermute | solution.py:26
  15.5 0.5 collective-permute-done.9.refs_10_
  16.0 1.5 %collective-permute-start.2 = (bf16[2,64,384]{2,1,0:T(8,128)(2,1)S(1)}, bf16[2,64,384]{2,1,0:T(8,128)(2,1)S(1)}, u32[]{:S(2)}, u32[]{:S(2)}) collective-permute-start(bf16[2,64,384]{2,1,0:T(8,128)(2,1)S(1)} %get-tuple-element.12.refs_0_.rows_own), channel_id=1, source_target_pairs={{0,2},{1,3},{2,0},{3,1},{4,6},{5,7},{6,4},{7,5},{8,10},{9,11},{10,... | collective-permute-start | bytes 294920 | tf_op jit(solution)/shard_map/ppermute | solution.py:26
  17.6 2.8 %collective-permute-start = (bf16[288,256]{1,0:T(8,128)(2,1)S(1)}, bf16[288,256]{1,0:T(8,128)(2,1)S(1)}, u32[]{:S(2)}, u32[]{:S(2)}) collective-permute-start(bf16[288,256]{1,0:T(8,128)(2,1)S(1)} %get-tuple-element.13.near), channel_id=1, source_target_pairs={{0,16},{4,20},{8,24},{12,28},{16,0},{20,4},{24,8},{28,12},{1,17},{... | collective-permute-start | bytes 442376 | tf_op jit(solution)/shard_map/ppermute | solution.py:26
  20.8 3.8 %collective-permute-done.5.refs_6_ = bf16[64,256]{1,0:T(8,128)(2,1)S(1)} collective-permute-done((bf16[64,256]{1,0:T(8,128)(2,1)S(1)}, bf16[64,256]{1,0:T(8,128)(2,1)S(1)}, u32[]{:S(2)}, u32[]{:S(2)}) %collective-permute-start.5) | collective-permute-done | bytes 32800 | tf_op jit(solution)/shard_map/ppermute | solution.py:26
  24.6 0.7 %collective-permute-start.4 = (bf16[64,256]{1,0:T(8,128)(2,1)S(1)}, bf16[64,256]{1,0:T(8,128)(2,1)S(1)}, u32[]{:S(2)}, u32[]{:S(2)}) collective-permute-start(bf16[64,256]{1,0:T(8,128)(2,1)S(1)} %get-tuple-element.14.refs_4_), channel_id=1, source_target_pairs={{0,4},{4,0},{8,12},{12,8},{16,20},{20,16},{24,28},{28,24},{1,5},{5... | collective-permute-start | bytes 98312 | tf_op jit(solution)/shard_map/ppermute | solution.py:26
  25.3 3.2 %collective-permute-done.4.refs_5_ = bf16[64,256]{1,0:T(8,128)(2,1)S(1)} collective-permute-done((bf16[64,256]{1,0:T(8,128)(2,1)S(1)}, bf16[64,256]{1,0:T(8,128)(2,1)S(1)}, u32[]{:S(2)}, u32[]{:S(2)}) %collective-permute-start.4) | collective-permute-done | bytes 32800 | tf_op jit(solution)/shard_map/ppermute | solution.py:26
  28.5 0.6 %intermediate.1.refs_0_ = bf16[128,256]{1,0:T(8,128)(2,1)S(1)} custom-call(bf16[2,64,384]{2,1,0:T(8,128)(2,1)S(1)} %get-tuple-element.12.refs_0_.rows_own, bf16[2,64,384]{2,1,0:T(8,128)(2,1)S(1)} %collective-permute-done.1.refs_1_, bf16[2,64,384]{2,1,0:T(8,128)(2,1)S(1)} %collective-permute-done.2.refs_2_, ...), custom_call_target="tpu_custom_call" | custom-call | tf_op jit(solution)/shard_map/intermediate/pallas_call | solution.py:214
  29.2 2.1 %collective-permute-start.17 = (bf16[128,256]{1,0:T(8,128)(2,1)S(1)}, bf16[128,256]{1,0:T(8,128)(2,1)S(1)}, u32[]{:S(2)}, u32[]{:S(2)}) collective-permute-start(bf16[128,256]{1,0:T(8,128)(2,1)S(1)} %intermediate.1.refs_0_), channel_id=1, source_target_pairs={{0,28},{4,24},{8,20},{12,16},{16,12},{20,8},{24,4},{28,0},{1,29},{... | collective-permute-start | bytes 196616 | tf_op jit(solution)/shard_map/ppermute | solution.py:26
  31.3 2.0 %collective-permute-start.16 = (bf16[128,256]{1,0:T(8,128)(2,1)S(1)}, bf16[128,256]{1,0:T(8,128)(2,1)S(1)}, u32[]{:S(2)}, u32[]{:S(2)}) collective-permute-start(bf16[128,256]{1,0:T(8,128)(2,1)S(1)} %intermediate.1.refs_0_), channel_id=1, source_target_pairs={{0,24},{4,28},{8,16},{12,20},{16,8},{20,12},{24,0},{28,4},{1,25},{... | collective-permute-start | bytes 196616 | tf_op jit(solution)/shard_map/ppermute | solution.py:26
  33.2 0.9 %collective-permute-start.15 = (bf16[128,256]{1,0:T(8,128)(2,1)S(1)}, bf16[128,256]{1,0:T(8,128)(2,1)S(1)}, u32[]{:S(2)}, u32[]{:S(2)}) collective-permute-start(bf16[128,256]{1,0:T(8,128)(2,1)S(1)} %intermediate.1.refs_0_), channel_id=1, source_target_pairs={{0,20},{4,16},{8,28},{12,24},{16,4},{20,0},{24,12},{28,8},{1,21},{... | collective-permute-start | bytes 196616 | tf_op jit(solution)/shard_map/ppermute | solution.py:26
  34.1 2.8 %collective-permute-start.14 = (bf16[128,256]{1,0:T(8,128)(2,1)S(1)}, bf16[128,256]{1,0:T(8,128)(2,1)S(1)}, u32[]{:S(2)}, u32[]{:S(2)}) collective-permute-start(bf16[128,256]{1,0:T(8,128)(2,1)S(1)} %intermediate.1.refs_0_), channel_id=1, source_target_pairs={{0,16},{4,20},{8,24},{12,28},{16,0},{20,4},{24,8},{28,12},{1,17},{... | collective-permute-start | bytes 196616 | tf_op jit(solution)/shard_map/ppermute | solution.py:26
  36.9 0.7 %collective-permute-start.13 = (bf16[128,256]{1,0:T(8,128)(2,1)S(1)}, bf16[128,256]{1,0:T(8,128)(2,1)S(1)}, u32[]{:S(2)}, u32[]{:S(2)}) collective-permute-start(bf16[128,256]{1,0:T(8,128)(2,1)S(1)} %intermediate.1.refs_0_), channel_id=1, source_target_pairs={{0,12},{4,8},{8,4},{12,0},{16,28},{20,24},{24,20},{28,16},{1,13},{... | collective-permute-start | bytes 196616 | tf_op jit(solution)/shard_map/ppermute | solution.py:26
  37.5 3.4 %collective-permute-start.12 = (bf16[128,256]{1,0:T(8,128)(2,1)S(1)}, bf16[128,256]{1,0:T(8,128)(2,1)S(1)}, u32[]{:S(2)}, u32[]{:S(2)}) collective-permute-start(bf16[128,256]{1,0:T(8,128)(2,1)S(1)} %intermediate.1.refs_0_), channel_id=1, source_target_pairs={{0,8},{4,12},{8,0},{12,4},{16,24},{20,28},{24,16},{28,20},{1,9},{5... | collective-permute-start | bytes 196616 | tf_op jit(solution)/shard_map/ppermute | solution.py:26
  40.9 0.7 %collective-permute-start.11 = (bf16[128,256]{1,0:T(8,128)(2,1)S(1)}, bf16[128,256]{1,0:T(8,128)(2,1)S(1)}, u32[]{:S(2)}, u32[]{:S(2)}) collective-permute-start(bf16[128,256]{1,0:T(8,128)(2,1)S(1)} %intermediate.1.refs_0_), channel_id=1, source_target_pairs={{0,4},{4,0},{8,12},{12,8},{16,20},{20,16},{24,28},{28,24},{1,5},{5... | collective-permute-start | bytes 196616 | tf_op jit(solution)/shard_map/ppermute | solution.py:26
  41.6 1.7 %collective-permute-done.15.refs_5_ = bf16[128,256]{1,0:T(8,128)(2,1)S(1)} collective-permute-done((bf16[128,256]{1,0:T(8,128)(2,1)S(1)}, bf16[128,256]{1,0:T(8,128)(2,1)S(1)}, u32[]{:S(2)}, u32[]{:S(2)}) %collective-permute-start.15) | collective-permute-done | bytes 65568 | tf_op jit(solution)/shard_map/ppermute | solution.py:26
  43.3 0.7 %collective-permute-done.13.refs_3_ = bf16[128,256]{1,0:T(8,128)(2,1)S(1)} collective-permute-done((bf16[128,256]{1,0:T(8,128)(2,1)S(1)}, bf16[128,256]{1,0:T(8,128)(2,1)S(1)}, u32[]{:S(2)}, u32[]{:S(2)}) %collective-permute-start.13) | collective-permute-done | bytes 65568 | tf_op jit(solution)/shard_map/ppermute | solution.py:26
  44.0 1.1 %collective-permute-done.11.refs_1_ = bf16[128,256]{1,0:T(8,128)(2,1)S(1)} collective-permute-done((bf16[128,256]{1,0:T(8,128)(2,1)S(1)}, bf16[128,256]{1,0:T(8,128)(2,1)S(1)}, u32[]{:S(2)}, u32[]{:S(2)}) %collective-permute-start.11) | collective-permute-done | bytes 65568 | tf_op jit(solution)/shard_map/ppermute | solution.py:26
  45.2 2.7 %cycle.1 = (f32[2,64,256]{2,1,0:T(8,128)S(1)}, bf16[2,64,256]{2,1,0:T(8,128)(2,1)S(1)}, bf16[2,64,256]{2,1,0:T(8,128)(2,1)S(1)}, bf16[2,64,256]{2,1,0:T(8,128)(2,1)S(1)}) custom-call(bf16[2,64,384]{2,1,0:T(8,128)(2,1)S(1)} %get-tuple-element.12.refs_0_.rows_own, f32[2,64,256]{2,1,0:T(8,128)S(1)} %copy-done.1, bf16[288,256]{1,0:T(8,128)(2,1)S(1)} %get-tuple-element.13.near, ...), custom_call_target="tpu_custom_call" | custom-call | tf_op jit(solution)/shard_map/cycle/pallas_call | solution.py:221
  48.0 1.3 %collective-permute-start.19 = (bf16[2,64,256]{2,1,0:T(8,128)(2,1)S(1)}, bf16[2,64,256]{2,1,0:T(8,128)(2,1)S(1)}, u32[]{:S(2)}, u32[]{:S(2)}) collective-permute-start(bf16[2,64,256]{2,1,0:T(8,128)(2,1)S(1)} %get-tuple-element.17), channel_id=1, source_target_pairs={{0,2},{1,3},{2,0},{3,1},{4,6},{5,7},{6,4},{7,5},{8,10},{9,11},{10,... | collective-permute-start | bytes 196616 | tf_op jit(solution)/shard_map/ppermute | solution.py:26
  49.2 0.6 %collective-permute-start.20 = (bf16[2,64,256]{2,1,0:T(8,128)(2,1)S(1)}, bf16[2,64,256]{2,1,0:T(8,128)(2,1)S(1)}, u32[]{:S(2)}, u32[]{:S(2)}) collective-permute-start(bf16[2,64,256]{2,1,0:T(8,128)(2,1)S(1)} %get-tuple-element.18), channel_id=1, source_target_pairs={{0,3},{1,2},{2,1},{3,0},{4,7},{5,6},{6,5},{7,4},{8,11},{9,10},{10,... | collective-permute-start | bytes 196616 | tf_op jit(solution)/shard_map/ppermute | solution.py:26
  49.9 3.0 %collective-permute-done.19 = bf16[2,64,256]{2,1,0:T(8,128)(2,1)S(1)} collective-permute-done((bf16[2,64,256]{2,1,0:T(8,128)(2,1)S(1)}, bf16[2,64,256]{2,1,0:T(8,128)(2,1)S(1)}, u32[]{:S(2)}, u32[]{:S(2)}) %collective-permute-start.19) | collective-permute-done | bytes 65568 | tf_op jit(solution)/shard_map/ppermute | solution.py:26
  52.8 0.8 %collective-permute-done.20 = bf16[2,64,256]{2,1,0:T(8,128)(2,1)S(1)} collective-permute-done((bf16[2,64,256]{2,1,0:T(8,128)(2,1)S(1)}, bf16[2,64,256]{2,1,0:T(8,128)(2,1)S(1)}, u32[]{:S(2)}, u32[]{:S(2)}) %collective-permute-start.20) | collective-permute-done | bytes 65568 | tf_op jit(solution)/shard_map/ppermute | solution.py:26
  53.6 0.7 %add_multiply_fusion = f32[2,64,256]{2,1,0:T(8,128)} fusion(bf16[2,64,256]{2,1,0:T(8,128)(2,1)S(1)} %collective-permute-done.20, bf16[2,64,256]{2,1,0:T(8,128)(2,1)S(1)} %collective-permute-done.19, f32[2,64,256]{2,1,0:T(8,128)S(1)} %get-tuple-element.15, bf16[2,64,256]{2,1,0:T(8,128)(2,1)S(1)} %collective-permute-done.18), kind=kLoop, calls=%fused_computation | loop fusion | flops 229376 | bytes 458752 | tf_op jit(solution)/shard_map/mul | solution.py:230
  (36 shorter events, 1.0 us)
Async XLA Ops:
  0.0 0.7 %copy-start.8 = (s32[96,1]{0,1:T(1,128)S(1)}, s32[96,1]{0,1:T(1,128)}, u32[]{:S(2)}) copy-start(s32[96,1]{0,1:T(1,128)} %param.17) | copy-start | bytes 1156
  0.0 0.7 %copy-start.9 = (s32[96,1]{0,1:T(1,128)S(1)}, s32[96,1]{0,1:T(1,128)}, u32[]{:S(2)}) copy-start(s32[96,1]{0,1:T(1,128)} %param.18) | copy-start | bytes 1156
  0.0 0.7 %copy-start.4 = (f32[2,256]{1,0:T(2,128)S(1)}, f32[2,256]{1,0:T(2,128)}, u32[]{:S(2)}) copy-start(f32[2,256]{1,0:T(2,128)} %virt.1) | copy-start | bytes 6148
  0.0 0.7 %copy-start.5 = (f32[2]{0:T(128)S(1)}, f32[2]{0:T(128)}, u32[]{:S(2)}) copy-start(f32[2]{0:T(128)} %pair.1) | copy-start | bytes 28
  0.0 0.7 %copy-start.6 = (s32[64,1]{0,1:T(1,128)S(1)}, s32[64,1]{0,1:T(1,128)}, u32[]{:S(2)}) copy-start(s32[64,1]{0,1:T(1,128)} %param.15) | copy-start | bytes 772
  0.0 0.7 %copy-start.7 = (s32[96,1]{0,1:T(1,128)S(1)}, s32[96,1]{0,1:T(1,128)}, u32[]{:S(2)}) copy-start(s32[96,1]{0,1:T(1,128)} %param.16) | copy-start | bytes 1156
  0.7 0.9 %copy-start = (f32[2,64,256]{2,1,0:T(8,128)S(1)}, f32[2,64,256]{2,1,0:T(8,128)}, u32[]{:S(2)}) copy-start(f32[2,64,256]{2,1,0:T(8,128)} %resid.3) | copy-start | bytes 393220
  1.6 0.9 %copy-start.2 = (f32[2,64,256]{2,1,0:T(8,128)S(1)}, f32[2,64,256]{2,1,0:T(8,128)}, u32[]{:S(2)}) copy-start(f32[2,64,256]{2,1,0:T(8,128)} %amps.1) | copy-start | bytes 393220
  2.5 0.9 %copy-start.3 = (bf16[1,256,256]{2,1,0:T(8,128)(2,1)S(1)}, bf16[1,256,256]{2,1,0:T(8,128)(2,1)}, u32[]{:S(2)}) copy-start(bf16[1,256,256]{2,1,0:T(8,128)(2,1)} %block.1) | copy-start | bytes 393220
  4.2 11.3 %collective-permute-start.10 = (bf16[64,256]{1,0:T(8,128)(2,1)S(1)}, bf16[64,256]{1,0:T(8,128)(2,1)S(1)}, u32[]{:S(2)}, u32[]{:S(2)}) collective-permute-start(bf16[64,256]{1,0:T(8,128)(2,1)S(1)} %get-tuple-element.14.refs_4_), channel_id=1, source_target_pairs={{0,28},{4,24},{8,20},{12,16},{16,12},{20,8},{24,4},{28,0},{1,29},{... | collective-permute-start | bytes 98312 | tf_op jit(solution)/shard_map/ppermute | solution.py:26
  10.2 5.8 %collective-permute-start.9 = (bf16[64,256]{1,0:T(8,128)(2,1)S(1)}, bf16[64,256]{1,0:T(8,128)(2,1)S(1)}, u32[]{:S(2)}, u32[]{:S(2)}) collective-permute-start(bf16[64,256]{1,0:T(8,128)(2,1)S(1)} %get-tuple-element.14.refs_4_), channel_id=1, source_target_pairs={{0,24},{4,28},{8,16},{12,20},{16,8},{20,12},{24,0},{28,4},{1,25},{... | collective-permute-start | bytes 98312 | tf_op jit(solution)/shard_map/ppermute | solution.py:26
  10.5 7.1 %collective-permute-start.8 = (bf16[64,256]{1,0:T(8,128)(2,1)S(1)}, bf16[64,256]{1,0:T(8,128)(2,1)S(1)}, u32[]{:S(2)}, u32[]{:S(2)}) collective-permute-start(bf16[64,256]{1,0:T(8,128)(2,1)S(1)} %get-tuple-element.14.refs_4_), channel_id=1, source_target_pairs={{0,20},{4,16},{8,28},{12,24},{16,4},{20,0},{24,12},{28,8},{1,21},{... | collective-permute-start | bytes 98312 | tf_op jit(solution)/shard_map/ppermute | solution.py:26
  11.2 6.3 %collective-permute-start.7 = (bf16[64,256]{1,0:T(8,128)(2,1)S(1)}, bf16[64,256]{1,0:T(8,128)(2,1)S(1)}, u32[]{:S(2)}, u32[]{:S(2)}) collective-permute-start(bf16[64,256]{1,0:T(8,128)(2,1)S(1)} %get-tuple-element.14.refs_4_), channel_id=1, source_target_pairs={{0,16},{4,20},{8,24},{12,28},{16,0},{20,4},{24,8},{28,12},{1,17},{... | collective-permute-start | bytes 98312 | tf_op jit(solution)/shard_map/ppermute | solution.py:26
  13.2 7.1 %collective-permute-start.6 = (bf16[64,256]{1,0:T(8,128)(2,1)S(1)}, bf16[64,256]{1,0:T(8,128)(2,1)S(1)}, u32[]{:S(2)}, u32[]{:S(2)}) collective-permute-start(bf16[64,256]{1,0:T(8,128)(2,1)S(1)} %get-tuple-element.14.refs_4_), channel_id=1, source_target_pairs={{0,12},{4,8},{8,4},{12,0},{16,28},{20,24},{24,20},{28,16},{1,13},{... | collective-permute-start | bytes 98312 | tf_op jit(solution)/shard_map/ppermute | solution.py:26
  15.5 13.0 %collective-permute-start.3 = (bf16[2,64,384]{2,1,0:T(8,128)(2,1)S(1)}, bf16[2,64,384]{2,1,0:T(8,128)(2,1)S(1)}, u32[]{:S(2)}, u32[]{:S(2)}) collective-permute-start(bf16[2,64,384]{2,1,0:T(8,128)(2,1)S(1)} %get-tuple-element.12.refs_0_.rows_own), channel_id=1, source_target_pairs={{0,3},{1,2},{2,1},{3,0},{4,7},{5,6},{6,5},{7,4},{8,11},{9,10},{10,... | collective-permute-start | bytes 294920 | tf_op jit(solution)/shard_map/ppermute | solution.py:26
  16.0 12.5 %collective-permute-start.2 = (bf16[2,64,384]{2,1,0:T(8,128)(2,1)S(1)}, bf16[2,64,384]{2,1,0:T(8,128)(2,1)S(1)}, u32[]{:S(2)}, u32[]{:S(2)}) collective-permute-start(bf16[2,64,384]{2,1,0:T(8,128)(2,1)S(1)} %get-tuple-element.12.refs_0_.rows_own), channel_id=1, source_target_pairs={{0,2},{1,3},{2,0},{3,1},{4,6},{5,7},{6,4},{7,5},{8,10},{9,11},{10,... | collective-permute-start | bytes 294920 | tf_op jit(solution)/shard_map/ppermute | solution.py:26
  17.5 11.0 %collective-permute-start.1 = (bf16[2,64,384]{2,1,0:T(8,128)(2,1)S(1)}, bf16[2,64,384]{2,1,0:T(8,128)(2,1)S(1)}, u32[]{:S(2)}, u32[]{:S(2)}) collective-permute-start(bf16[2,64,384]{2,1,0:T(8,128)(2,1)S(1)} %get-tuple-element.12.refs_0_.rows_own), channel_id=1, source_target_pairs={{0,1},{1,0},{2,3},{3,2},{4,5},{5,4},{6,7},{7,6},{8,9},{9,8},{10,11... | collective-permute-start | bytes 294920 | tf_op jit(solution)/shard_map/ppermute | solution.py:26
  17.5 27.6 %copy-start.1 = (f32[2,64,256]{2,1,0:T(8,128)S(1)}, f32[2,64,256]{2,1,0:T(8,128)}, u32[]{:S(2)}) copy-start(f32[2,64,256]{2,1,0:T(8,128)} %resid.3) | copy-start | bytes 393220
  17.5 27.6 %copy-start.10 = (s32[2]{0:T(128)S(1)}, s32[2]{0:T(128)}, u32[]{:S(2)}) copy-start(s32[2]{0:T(128)} %swap.1) | copy-start | bytes 28
  17.6 19.3 %collective-permute-start = (bf16[288,256]{1,0:T(8,128)(2,1)S(1)}, bf16[288,256]{1,0:T(8,128)(2,1)S(1)}, u32[]{:S(2)}, u32[]{:S(2)}) collective-permute-start(bf16[288,256]{1,0:T(8,128)(2,1)S(1)} %get-tuple-element.13.near), channel_id=1, source_target_pairs={{0,16},{4,20},{8,24},{12,28},{16,0},{20,4},{24,8},{28,12},{1,17},{... | collective-permute-start | bytes 442376 | tf_op jit(solution)/shard_map/ppermute | solution.py:26
  20.3 4.3 %collective-permute-start.5 = (bf16[64,256]{1,0:T(8,128)(2,1)S(1)}, bf16[64,256]{1,0:T(8,128)(2,1)S(1)}, u32[]{:S(2)}, u32[]{:S(2)}) collective-permute-start(bf16[64,256]{1,0:T(8,128)(2,1)S(1)} %get-tuple-element.14.refs_4_), channel_id=1, source_target_pairs={{0,8},{4,12},{8,0},{12,4},{16,24},{20,28},{24,16},{28,20},{1,9},{5... | collective-permute-start | bytes 98312 | tf_op jit(solution)/shard_map/ppermute | solution.py:26
  24.6 3.9 %collective-permute-start.4 = (bf16[64,256]{1,0:T(8,128)(2,1)S(1)}, bf16[64,256]{1,0:T(8,128)(2,1)S(1)}, u32[]{:S(2)}, u32[]{:S(2)}) collective-permute-start(bf16[64,256]{1,0:T(8,128)(2,1)S(1)} %get-tuple-element.14.refs_4_), channel_id=1, source_target_pairs={{0,4},{4,0},{8,12},{12,8},{16,20},{20,16},{24,28},{28,24},{1,5},{5... | collective-permute-start | bytes 98312 | tf_op jit(solution)/shard_map/ppermute | solution.py:26
  29.2 8.4 %collective-permute-start.17 = (bf16[128,256]{1,0:T(8,128)(2,1)S(1)}, bf16[128,256]{1,0:T(8,128)(2,1)S(1)}, u32[]{:S(2)}, u32[]{:S(2)}) collective-permute-start(bf16[128,256]{1,0:T(8,128)(2,1)S(1)} %intermediate.1.refs_0_), channel_id=1, source_target_pairs={{0,28},{4,24},{8,20},{12,16},{16,12},{20,8},{24,4},{28,0},{1,29},{... | collective-permute-start | bytes 196616 | tf_op jit(solution)/shard_map/ppermute | solution.py:26
  31.3 9.6 %collective-permute-start.16 = (bf16[128,256]{1,0:T(8,128)(2,1)S(1)}, bf16[128,256]{1,0:T(8,128)(2,1)S(1)}, u32[]{:S(2)}, u32[]{:S(2)}) collective-permute-start(bf16[128,256]{1,0:T(8,128)(2,1)S(1)} %intermediate.1.refs_0_), channel_id=1, source_target_pairs={{0,24},{4,28},{8,16},{12,20},{16,8},{20,12},{24,0},{28,4},{1,25},{... | collective-permute-start | bytes 196616 | tf_op jit(solution)/shard_map/ppermute | solution.py:26
  33.2 10.0 %collective-permute-start.15 = (bf16[128,256]{1,0:T(8,128)(2,1)S(1)}, bf16[128,256]{1,0:T(8,128)(2,1)S(1)}, u32[]{:S(2)}, u32[]{:S(2)}) collective-permute-start(bf16[128,256]{1,0:T(8,128)(2,1)S(1)} %intermediate.1.refs_0_), channel_id=1, source_target_pairs={{0,20},{4,16},{8,28},{12,24},{16,4},{20,0},{24,12},{28,8},{1,21},{... | collective-permute-start | bytes 196616 | tf_op jit(solution)/shard_map/ppermute | solution.py:26
  34.1 9.2 %collective-permute-start.14 = (bf16[128,256]{1,0:T(8,128)(2,1)S(1)}, bf16[128,256]{1,0:T(8,128)(2,1)S(1)}, u32[]{:S(2)}, u32[]{:S(2)}) collective-permute-start(bf16[128,256]{1,0:T(8,128)(2,1)S(1)} %intermediate.1.refs_0_), channel_id=1, source_target_pairs={{0,16},{4,20},{8,24},{12,28},{16,0},{20,4},{24,8},{28,12},{1,17},{... | collective-permute-start | bytes 196616 | tf_op jit(solution)/shard_map/ppermute | solution.py:26
  36.9 7.1 %collective-permute-start.13 = (bf16[128,256]{1,0:T(8,128)(2,1)S(1)}, bf16[128,256]{1,0:T(8,128)(2,1)S(1)}, u32[]{:S(2)}, u32[]{:S(2)}) collective-permute-start(bf16[128,256]{1,0:T(8,128)(2,1)S(1)} %intermediate.1.refs_0_), channel_id=1, source_target_pairs={{0,12},{4,8},{8,4},{12,0},{16,28},{20,24},{24,20},{28,16},{1,13},{... | collective-permute-start | bytes 196616 | tf_op jit(solution)/shard_map/ppermute | solution.py:26
  37.5 6.5 %collective-permute-start.12 = (bf16[128,256]{1,0:T(8,128)(2,1)S(1)}, bf16[128,256]{1,0:T(8,128)(2,1)S(1)}, u32[]{:S(2)}, u32[]{:S(2)}) collective-permute-start(bf16[128,256]{1,0:T(8,128)(2,1)S(1)} %intermediate.1.refs_0_), channel_id=1, source_target_pairs={{0,8},{4,12},{8,0},{12,4},{16,24},{20,28},{24,16},{28,20},{1,9},{5... | collective-permute-start | bytes 196616 | tf_op jit(solution)/shard_map/ppermute | solution.py:26
  40.9 4.3 %collective-permute-start.11 = (bf16[128,256]{1,0:T(8,128)(2,1)S(1)}, bf16[128,256]{1,0:T(8,128)(2,1)S(1)}, u32[]{:S(2)}, u32[]{:S(2)}) collective-permute-start(bf16[128,256]{1,0:T(8,128)(2,1)S(1)} %intermediate.1.refs_0_), channel_id=1, source_target_pairs={{0,4},{4,0},{8,12},{12,8},{16,20},{20,16},{24,28},{28,24},{1,5},{5... | collective-permute-start | bytes 196616 | tf_op jit(solution)/shard_map/ppermute | solution.py:26
  47.9 1.9 %collective-permute-start.18 = (bf16[2,64,256]{2,1,0:T(8,128)(2,1)S(1)}, bf16[2,64,256]{2,1,0:T(8,128)(2,1)S(1)}, u32[]{:S(2)}, u32[]{:S(2)}) collective-permute-start(bf16[2,64,256]{2,1,0:T(8,128)(2,1)S(1)} %get-tuple-element.16), channel_id=1, source_target_pairs={{0,1},{1,0},{2,3},{3,2},{4,5},{5,4},{6,7},{7,6},{8,9},{9,8},{10,11... | collective-permute-start | bytes 196616 | tf_op jit(solution)/shard_map/ppermute | solution.py:26
  48.0 4.8 %collective-permute-start.19 = (bf16[2,64,256]{2,1,0:T(8,128)(2,1)S(1)}, bf16[2,64,256]{2,1,0:T(8,128)(2,1)S(1)}, u32[]{:S(2)}, u32[]{:S(2)}) collective-permute-start(bf16[2,64,256]{2,1,0:T(8,128)(2,1)S(1)} %get-tuple-element.17), channel_id=1, source_target_pairs={{0,2},{1,3},{2,0},{3,1},{4,6},{5,7},{6,4},{7,5},{8,10},{9,11},{10,... | collective-permute-start | bytes 196616 | tf_op jit(solution)/shard_map/ppermute | solution.py:26
  49.2 4.3 %collective-permute-start.20 = (bf16[2,64,256]{2,1,0:T(8,128)(2,1)S(1)}, bf16[2,64,256]{2,1,0:T(8,128)(2,1)S(1)}, u32[]{:S(2)}, u32[]{:S(2)}) collective-permute-start(bf16[2,64,256]{2,1,0:T(8,128)(2,1)S(1)} %get-tuple-element.18), channel_id=1, source_target_pairs={{0,3},{1,2},{2,1},{3,0},{4,7},{5,6},{6,5},{7,4},{8,11},{9,10},{10,... | collective-permute-start | bytes 196616 | tf_op jit(solution)/shard_map/ppermute | solution.py:26

commit v2 on v1

v2 whole, which is shorter than its diff:
```python
import functools

import jax
import jax.numpy as jnp
from jax import lax
from jax.experimental import pallas as pl
from jax.experimental.pallas import tpu as pltpu
from jax.sharding import PartitionSpec as P

F32, BF16 = jnp.float32, jnp.bfloat16
DIRECT = 16
CORE = 1
NT = (((1,), (1,)), ((), ()))
TN = (((0,), (0,)), ((), ()))
TILE = 16


def dot(a, b, dims=(((1,), (0,)), ((), ()))):
    return lax.dot_general(a, b, dims, preferred_element_type=F32)


def iota(shape, dim):
    return lax.broadcasted_iota(jnp.int32, shape, dim)


def exchange(value, pair_offset, int_offset):
    n_pairs, n_ints = lax.axis_size("pairs"), lax.axis_size("ints")
    route = [
        (p * n_ints + q, (p ^ pair_offset) * n_ints + (q ^ int_offset)) for p in range(n_pairs) for q in range(n_ints)
    ]
    return lax.ppermute(value, ("pairs", "ints"), route)


def family_exchange(value, offset):
    n_pairs, n_ints = lax.axis_size("pairs"), lax.axis_size("ints")
    half = n_pairs // 2
    route = [
        (p * n_ints + q, (p ^ offset ^ (q % 2 * half)) * n_ints + q) for p in range(n_pairs) for q in range(n_ints)
    ]
    return lax.ppermute(value, ("pairs", "ints"), route)


def place():
    group, member, n_pairs = lax.axis_index("pairs"), lax.axis_index("ints"), lax.axis_size("pairs")
    core = member % 2
    return group, member, core, group ^ (core * (n_pairs // 2)), n_pairs // 2


def prepare(
    amps, block, resid, virt, pair, items, owners, wanted, share, lean_out, full_out, half_out, resid_out, *scratch
):
    hbm = (amps, block, resid, virt, pair, items, owners, wanted, share)
    held, sems = scratch[:-1], scratch[-1]
    copies = [pltpu.make_async_copy(src, dst, sems.at[i]) for i, (src, dst) in enumerate(zip(hbm, held))]
    for copy in copies:
        copy.start()
    amps, block, resid, virt, pair, items, owners, wanted, share = held
    pairs, height, domain = amps.shape
    rows = pairs * height
    member = lax.axis_index("ints")
    half_rows = half_out.shape[0]
    half_start = member // 2 * half_rows
    chosen = (iota((half_rows, domain), 1) == iota((half_rows, domain), 0) + half_start).astype(BF16)
    mine = (iota((height, domain), 1) == iota((height, domain), 0) + member * height).astype(BF16)

    for copy in copies[3:]:
        copy.wait()
    n_items, n_req = items.shape[1], owners.shape[1]
    named = jnp.concatenate(
        [jnp.broadcast_to(items[...].astype(F32), (TILE, n_items)), jnp.zeros((TILE, domain - n_items), F32)], axis=1
    ).astype(BF16)
    source = owners[...] * pairs + wanted[...]
    hits = (source == iota((domain, n_req), 0)).astype(BF16)
    row, col = iota((8, n_req), 0), iota((8, n_req), 1)
    into = ((col // (n_req // pairs) == row // pairs) & (share[...] == row % pairs)).astype(BF16)
    counts = dot(into, hits, NT)
    row = iota((8, domain), 0)
    energy = jnp.zeros((8, domain), F32)
    for p in range(pairs):
        energy = jnp.where(row == p, virt[p : p + 1, :], energy)
        energy = jnp.where(row == pairs + p, pair[p], energy)
    high = energy.astype(BF16).astype(F32)
    middle = (energy - high).astype(BF16).astype(F32)
    low = energy - high - middle
    full_out[rows + TILE + height :, :] = jnp.concatenate([counts, high, middle, low], axis=0).astype(BF16)
    lean_out[rows:, :] = named
    full_out[rows : rows + TILE, :] = named
    copies[0].wait()
    amp_half = amps[...].astype(BF16).reshape(rows, domain)
    lean_out[:rows, :] = amp_half
    full_out[:rows, :] = amp_half
    copies[1].wait()
    half_out[...] = dot(chosen, block[0], NT).astype(BF16)
    full_out[rows + TILE : rows + TILE + height, :] = dot(mine, block[0], NT).astype(BF16)
    copies[2].wait()
    resid_out[...] = resid[...].astype(BF16).reshape(rows, domain)


def ordered(core, own, other):
    return jnp.where(core == 0, own, other), jnp.where(core == 0, other, own)


def intermediate(n_shared, items, pairs, own, own_c, far, far_c, half_own, *refs):
    y_refs, rest, out = refs[: 4 * n_shared], refs[4 * n_shared : -1], refs[-1]
    half_rows, domain = half_own.shape
    height = half_rows // 2
    rows = pairs * height
    group, _, core, family, half = place()

    near = [own, own_c] + list(y_refs[: 2 * n_shared])
    away = [far, far_c] + list(y_refs[2 * n_shared :])
    lean = rows + TILE
    pieces = [jnp.where(core == 0, a[:lean, :], b[:lean, :]) for a, b in zip(near, away)]
    x = [jnp.concatenate([piece[p * height : (p + 1) * height] for piece in pieces], axis=0) for p in range(pairs)]
    x_all = jnp.concatenate(x, axis=0)
    spread = (iota((rows, domain), 0) * items // rows == iota((rows, domain), 1)).astype(BF16)
    named = [dot(spread, jnp.broadcast_to(piece[rows : rows + 1], (half_rows, domain)), NT) for piece in pieces]
    ids = jnp.concatenate(
        [name[p * height : (p + 1) * height] for p in range(pairs) for name in named], axis=0
    ).astype(jnp.int32)

    def chosen(block, index):
        return jnp.where(ids == index, dot(x_all, block, NT), 0.0)

    if len(rest) > 1:
        count = len(rest) // 2
        near_quarter = far[lean : lean + height, :]
        away_quarter = far_c[lean : lean + height, :]
        product = chosen(half_own[...], group)
        product += chosen(jnp.concatenate(ordered(core, near_quarter, away_quarter), axis=0), group ^ half)
        for j in range(count):
            product += chosen(rest[j][...], family ^ (j + 1))
            product += chosen(rest[count + j][...], family ^ half ^ (j + 1))
    else:
        product = lax.fori_loop(
            0,
            rest[0].shape[0],
            lambda k, sofar: sofar + chosen(rest[0][k], k),
            jnp.zeros((pairs * domain, half_rows), F32),
        )
    product = product.astype(BF16)
    for p in range(pairs):
        both = dot(product[p * domain : (p + 1) * domain], x[p], TN)
        out[p * half_rows : (p + 1) * half_rows, :] = both.astype(BF16)


def spread_counts(own, far, swaps, half_rows, lanes):
    start, pairs = own.shape[0] - 32, len(swaps)
    counts = jnp.concatenate([own[start : start + 8, :lanes], far[start : start + 8, :lanes]], axis=0)
    tall = 2 * pairs * pairs * half_rows
    term = iota((tall, 16), 0) // half_rows
    which = term
    for p, swap in enumerate(swaps):
        which = jnp.where(term // pairs == pairs + p, 8 + swap * pairs + term % pairs, which)
    return dot((which == iota((tall, 16), 1)).astype(BF16), counts).astype(BF16)


def weights(spread, source_group, pairs, half_rows):
    tall, lanes = spread.shape
    wide = pairs * half_rows
    same = iota((tall, wide), 0) % half_rows == iota((tall, wide), 1) % half_rows
    place_of = iota((lanes, wide), 0) == source_group * pairs + iota((lanes, wide), 1) // half_rows
    return jnp.where(same, dot(spread, place_of.astype(BF16)), 0.0).astype(BF16)


def lanes_of(pairs):
    return -(-lax.axis_size("pairs") * pairs // 128) * 128


def factors(n_units, resid, own, far, swap, weights_out, inverse_out, base_out, swap_out, *scratch):
    held, sems = scratch[:-1], scratch[-1]
    copies = [pltpu.make_async_copy(src, dst, sems.at[i]) for i, (src, dst) in enumerate(zip((resid, swap), held))]
    for copy in copies:
        copy.start()
    resid, swap = held
    pairs, height, domain = resid.shape
    half_rows = 2 * height
    wide = pairs * half_rows
    group, member, _, family, half = place()
    for copy in copies:
        copy.wait()
    swaps = [swap[p] - (group ^ half) * pairs for p in range(pairs)]
    spread = spread_counts(own, far, swaps, half_rows, lanes_of(pairs))
    for k in range(n_units):
        weights_out[:, k * wide : (k + 1) * wide] = weights(spread, family ^ k, pairs, half_rows)
    start = own.shape[0] - 24

    def energy_of(packed):
        parts = packed[start : start + 24, :].astype(F32)
        energy = parts[:8] + parts[8:16] + parts[16:24]
        return energy, energy.T

    def inverse(energy, tall_energy, p):
        divisor = tall_energy[:, p : p + 1] + energy[p : p + 1] - energy[pairs + p : pairs + p + 1]
        return 1.0 / divisor

    near, away = energy_of(own), energy_of(far)
    away = [inverse(*away, p) for p in range(pairs)]
    for p in range(pairs):
        inverse_out[p] = inverse(*near, p)
        inverse_out[pairs + p] = functools.reduce(
            lambda kept, k: jnp.where(swaps[p] == k, away[k], kept), range(1, pairs), away[0]
        )
        swap_out[p] = jnp.full(swap_out.shape[1:], swaps[p], jnp.int32)
    rows = pl.ds(pl.multiple_of(member * height, height), height)
    base_out[...] = resid[...] * inverse_out[:pairs, rows, :]


def cycle(n_sends, pairs, own, own_c, far, far_c, resid_far, mix, inverse, base, swap, *refs):
    units, (own_out, *sends), (here, there) = refs[: -n_sends - 3], refs[-n_sends - 3 : -2], refs[-2:]
    height, domain = resid_far.shape[0] // pairs, resid_far.shape[1]
    rows = pairs * height
    half_rows = 2 * height
    group, member, core, family, half = place()
    if len(units) > 1:
        mixed = dot(mix[...], jnp.concatenate([unit[...] for unit in units], axis=0))
    else:
        swaps = [swap[p, :1, :1] for p in range(pairs)]
        spread = spread_counts(own, far, swaps, half_rows, lanes_of(pairs))
        first = group - group % half
        mixed = lax.fori_loop(
            0,
            units[0].shape[0],
            lambda k, sofar: sofar
            + dot(weights(spread, (first + k) ^ (core * half), pairs, half_rows), units[0][k]),
            jnp.zeros((spread.shape[0], domain), F32),
        )
    mixed = mixed.astype(BF16)
    start = pl.ds(pl.multiple_of(member * height, height), height)

    def amps_of(mine, other):
        low, high = ordered(core, mine[:rows, :], other[:rows, :])
        return jnp.concatenate(
            [part[p * height : (p + 1) * height] for p in range(pairs) for part in (low, high)], axis=0
        )

    wide = pairs * half_rows
    near, away = amps_of(own, own_c), amps_of(far, far_c)
    for p in range(pairs):
        at = (pairs + p) * wide
        there[...] = dot(mixed[at : at + wide], away, TN)
        parts = [resid_far[k * height : (k + 1) * height, :].astype(F32) for k in range(pairs)]
        named = swap[p, :1, :1]
        there[start, :] += functools.reduce(
            lambda kept, k: jnp.where(named == k, parts[k], kept), range(1, pairs), parts[0]
        )
        mirror = (there[...] * inverse[pairs + p]).T
        at = p * wide
        here[p] = dot(mixed[at : at + wide], near, TN) * inverse[p] + mirror
    own_out[...] = here[:, start, :] + base[...]
    for offset, send in enumerate(sends, 1):
        to = pl.multiple_of((member ^ offset) * height, height)
        send[...] = here[:, pl.ds(to, height), :].astype(BF16)


VM = pl.BlockSpec(memory_space=pltpu.VMEM)
HB = pl.BlockSpec(memory_space=pltpu.HBM)


def stay(value):
    return pltpu.with_memory_space_constraint(value, pltpu.HBM)


def call(kernel, outs, in_specs, name, scratch=()):
    return pl.pallas_call(
        kernel,
        out_shape=outs,
        in_specs=in_specs,
        out_specs=jax.tree.map(lambda _: VM, outs),
        scratch_shapes=scratch,
        name=name,
        compiler_params=pltpu.CompilerParams(vmem_limit_bytes=48 * 1024 * 1024),
    )


def body(
    amps,
    resid_rest,
    int_blocks,
    virt_energy,
    pair_energy,
    item_block,
    share_owner,
    share_pair,
    share_amp,
    transpose_pair,
):
    n_pairs, n_ints = lax.axis_size("pairs"), lax.axis_size("ints")
    pairs, height, domain = amps.shape
    rows, half_rows, half = pairs * height, 2 * height, n_pairs // 2
    shape = jax.ShapeDtypeStruct
    operands = (
        amps,
        int_blocks,
        resid_rest,
        virt_energy,
        pair_energy,
        item_block.reshape(1, -1),
        share_owner.reshape(1, -1),
        share_pair.reshape(1, -1),
        share_amp.reshape(1, -1),
    )
    lean, own, half_own, resid_half = call(
        prepare,
        [
            shape((rows + TILE, domain), BF16),
            shape((rows + TILE + height + 32, domain), BF16),
            shape((half_rows, domain), BF16),
            shape((rows, domain), BF16),
        ],
        [HB] * len(operands),
        "prepare",
        [(pltpu.SMEM if o is pair_energy else pltpu.VMEM)(o.shape, o.dtype) for o in operands]
        + [pltpu.SemaphoreType.DMA((len(operands),))],
    )(*map(stay, operands))
    far = exchange(own, half, 0)
    y_own = [exchange(lean, 0, k) for k in range(2, n_ints, 2)]
    y_far = [exchange(lean, half, k) for k in range(2, n_ints, 2)]
    across = lambda value: exchange(value, 0, CORE)
    own_c, far_c = across(lean), across(far)
    if n_pairs <= DIRECT:
        blocks = [family_exchange(half_own, j) for j in range(1, half)]
        blocks += [across(block) for block in blocks]
    else:
        blocks = [lax.all_gather(half_own, "pairs", axis=0, tiled=False)]
    near_rows = [v for y in y_own for v in (y, across(y))]
    away_rows = [v for y in y_far for v in (y, across(y))]
    inter = call(
        functools.partial(intermediate, len(y_own), item_block.shape[0], pairs),
        shape((pairs * half_rows, domain), BF16),
        [VM] * (5 + len(near_rows) + len(away_rows) + len(blocks)),
        "intermediate",
    )(own, own_c, far, far_c, half_own, *near_rows, *away_rows, *blocks)
    if n_pairs <= DIRECT:
        units = [inter] + [exchange(inter, j, 0) for j in range(1, half)]
    else:
        every = lax.all_gather(inter, "pairs", axis=0, tiled=False)
        first = lax.axis_index("pairs") // half * half
        units = [lax.dynamic_slice_in_dim(every, first, half, 0)]
    resid_far = exchange(resid_half, half, 0)
    n_units = len(units)
    mix, inverse, base, swap = call(
        functools.partial(factors, n_units if n_units > 1 else 0),
        [
            shape((2 * pairs * pairs * half_rows, n_units * pairs * half_rows), BF16),
            shape((2 * pairs, domain, domain), F32),
            shape((pairs, height, domain), F32),
            shape((pairs, 8, 128), jnp.int32),
        ],
        [HB, VM, VM, HB],
        "factors",
        [
            pltpu.VMEM(resid_rest.shape, F32),
            pltpu.SMEM(transpose_pair.shape, jnp.int32),
            pltpu.SemaphoreType.DMA((2,)),
        ],
    )(stay(resid_rest), own, far, stay(transpose_pair))
    mine, *sends = call(
        functools.partial(cycle, n_ints - 1, pairs),
        [shape((pairs, height, domain), F32)] + [shape((pairs, height, domain), BF16)] * (n_ints - 1),
        [VM] * (9 + n_units),
        "cycle",
        [pltpu.VMEM((pairs, domain, domain), F32), pltpu.VMEM((domain, domain), F32)],
    )(own, own_c, far, far_c, resid_far, mix, inverse, base, swap, *units)
    for offset, send in enumerate(sends, 1):
        mine = mine + exchange(send, 0, offset).astype(F32)
    return -0.5 * mine


def solution(mesh):
    placed = (
        P("pairs", "ints", None),
        P("pairs", "ints", None),
        P("pairs", None, None),
        P("pairs", None),
        P("pairs"),
        P(("pairs", "ints"), None),
        P("pairs", None),
        P("pairs", None),
        P("pairs", None),
        P("pairs"),
    )
    return jax.shard_map(
        body, mesh=mesh, in_specs=placed, out_specs=P("pairs", "ints", None), check_vma=False
    )
```

time: 54.5 us -> 41 us (0.75)
  starting transfers between devices: 31.1 us -> 25 us
  waiting for transfers between devices: 14.8 us -> 9.37 us
  local copies, waits for them, and re-layouts: 3.44 us -> 0 us
  Pallas kernels: 4.11 us -> 5.71 us
    ppermute x21 -> x20, starting transfers between devices: 31.1 us -> 25 us  [the longest x17 21.5 us: exchange(): return lax.ppermute(value, ('pairs', 'ints'), route)]
    ppermute x21 -> x20, waiting for transfers between devices: 14.8 us -> 9.37 us  [the longest x17 7.04 us: exchange(): return lax.ppermute(value, ('pairs', 'ints'), route)]
    unnamed x22 -> x0, local copies, waits for them, and re-layouts: 3.44 us -> none
    pallas_call x3 -> x4, Pallas kernels: 4.11 us -> 5.71 us  [the longest x1 1.92 us: body(): call(functools.partial(factors, n_units if n_units > 1 else 0), [shape((2...]
  transfers between devices with their start and end apart: 21 -> 20, of which waited for: 9 -> 8; matrix products, arithmetic and copies ran while one was open for 0% -> 0% of each run, Pallas kernels for 1% -> 5%
where the time goes in v2:
time: 41 us; the launch traced here: 40.8 us
  starting transfers between devices  25 us (61%)
  waiting for transfers between devices  9.37 us (23%)
  Pallas kernels  5.71 us (14%)
  other arithmetic  0.69 us (2%)
    ppermute x17, starting transfers between devices, exchange(): return lax.ppermute(value, ('pairs', 'ints'), route)  21.5 us
    ppermute x17, waiting for transfers between devices, exchange(): return lax.ppermute(value, ('pairs', 'ints'), route)  7.04 us
    ppermute x3, starting transfers between devices, family_exchange(): return lax.ppermute(value, ('pairs', 'ints'), route)  3.49 us
    ppermute x3, waiting for transfers between devices, family_exchange(): return lax.ppermute(value, ('pairs', 'ints'), route)  2.33 us
    pallas_call x1, Pallas kernels, body(): call(functools.partial(factors, n_units if n_units > 1 else 0), [shape((2...  1.92 us
    pallas_call x1, Pallas kernels, body(): call(prepare, [shape((rows + TILE, domain), BF16), shape((rows + TILE + h...  1.39 us
    pallas_call x1, Pallas kernels, body(): call(functools.partial(cycle, n_ints - 1, pairs), [shape((pairs, height,...  1.38 us
    pallas_call x1, Pallas kernels, body(): call(functools.partial(intermediate, len(y_own), item_block.shape[0], pai...  1.02 us
  transfers between devices with their start and end apart: 20, of which 8 were waited for; matrix products, arithmetic and copies ran while one was open for 0% of the time, Pallas kernels for 5%

profile of v2, /device:TPU:0, one launch (start us, length us, event | category | flops | bytes accessed | tf_op | source)
XLA Modules:
  0.0 40.8 jit_solution(6687225809588315552)
XLA Ops:
  0.0 1.4 %prepare.1 = (bf16[144,256]{1,0:T(8,128)(2,1)S(1)}, bf16[240,256]{1,0:T(8,128)(2,1)S(1)}, bf16[128,256]{1,0:T(8,128)(2,1)S(1)}, bf16[128,256]{1,0:T(8,128)(2,1)S(1)}) custom-call(f32[2,64,256]{2,1,0:T(8,128)} %amps.1, bf16[1,256,256]{2,1,0:T(8,128)(2,1)} %block.1, f32[2,64,256]{2,1,0:T(8,128)} %resid.3, f32[2,256]{1,0:T(2,128)} %virt.1, f32[2]{0:T(128)} %pair.1, ...), custom_call_target="tpu_custom_call" | custom-call | tf_op jit(solution)/shard_map/prepare/pallas_call | solution.py:303
  1.4 4.1 %collective-permute-start.1 = (bf16[240,256]{1,0:T(8,128)(2,1)S(1)}, bf16[240,256]{1,0:T(8,128)(2,1)S(1)}, u32[]{:S(2)}, u32[]{:S(2)}) collective-permute-start(bf16[240,256]{1,0:T(8,128)(2,1)S(1)} %get-tuple-element.17.own), channel_id=1, source_target_pairs={{0,16},{1,17},{2,18},{3,19},{4,20},{5,21},{6,22},{7,23},{8,24},{9,... | collective-permute-start | bytes 368648 | tf_op jit(solution)/shard_map/ppermute | solution.py:31
  5.5 2.5 %collective-permute-start.10 = (bf16[128,256]{1,0:T(8,128)(2,1)S(1)}, bf16[128,256]{1,0:T(8,128)(2,1)S(1)}, u32[]{:S(2)}, u32[]{:S(2)}) collective-permute-start(bf16[128,256]{1,0:T(8,128)(2,1)S(1)} %get-tuple-element.24.half_own), channel_id=1, source_target_pairs={{0,12},{1,29},{2,14},{3,31},{4,8},{5,25},{6,10},{7,27},{8,4},{9,21... | collective-permute-start | bytes 196616 | tf_op jit(solution)/shard_map/ppermute | solution.py:40
  8.0 0.4 %collective-permute-start.9 = (bf16[128,256]{1,0:T(8,128)(2,1)S(1)}, bf16[128,256]{1,0:T(8,128)(2,1)S(1)}, u32[]{:S(2)}, u32[]{:S(2)}) collective-permute-start(bf16[128,256]{1,0:T(8,128)(2,1)S(1)} %get-tuple-element.24.half_own), channel_id=1, source_target_pairs={{0,8},{1,25},{2,10},{3,27},{4,12},{5,29},{6,14},{7,31},{8,0},{9,17... | collective-permute-start | bytes 196616 | tf_op jit(solution)/shard_map/ppermute | solution.py:40
  8.5 0.5 %collective-permute-start.8 = (bf16[128,256]{1,0:T(8,128)(2,1)S(1)}, bf16[128,256]{1,0:T(8,128)(2,1)S(1)}, u32[]{:S(2)}, u32[]{:S(2)}) collective-permute-start(bf16[128,256]{1,0:T(8,128)(2,1)S(1)} %get-tuple-element.24.half_own), channel_id=1, source_target_pairs={{0,4},{1,21},{2,6},{3,23},{4,0},{5,17},{6,2},{7,19},{8,12},{9,29},... | collective-permute-start | bytes 196616 | tf_op jit(solution)/shard_map/ppermute | solution.py:40
  9.0 1.3 %collective-permute-start.6 = (bf16[144,256]{1,0:T(8,128)(2,1)S(1)}, bf16[144,256]{1,0:T(8,128)(2,1)S(1)}, u32[]{:S(2)}, u32[]{:S(2)}) collective-permute-start(bf16[144,256]{1,0:T(8,128)(2,1)S(1)} %get-tuple-element.18), channel_id=1, source_target_pairs={{0,18},{1,19},{2,16},{3,17},{4,22},{5,23},{6,20},{7,21},{8,26},{9,... | collective-permute-start | bytes 221192 | tf_op jit(solution)/shard_map/ppermute | solution.py:31
  10.3 0.6 %collective-permute-done.10.refs_6_ = bf16[128,256]{1,0:T(8,128)(2,1)S(1)} collective-permute-done((bf16[128,256]{1,0:T(8,128)(2,1)S(1)}, bf16[128,256]{1,0:T(8,128)(2,1)S(1)}, u32[]{:S(2)}, u32[]{:S(2)}) %collective-permute-start.10) | collective-permute-done | bytes 65568 | tf_op jit(solution)/shard_map/ppermute | solution.py:40
  10.9 1.5 %collective-permute-start.4 = (bf16[144,256]{1,0:T(8,128)(2,1)S(1)}, bf16[144,256]{1,0:T(8,128)(2,1)S(1)}, u32[]{:S(2)}, u32[]{:S(2)}) collective-permute-start(bf16[144,256]{1,0:T(8,128)(2,1)S(1)} %get-tuple-element.18), channel_id=1, source_target_pairs={{0,2},{1,3},{2,0},{3,1},{4,6},{5,7},{6,4},{7,5},{8,10},{9,11},{10,... | collective-permute-start | bytes 221192 | tf_op jit(solution)/shard_map/ppermute | solution.py:31
  12.4 1.7 %collective-permute-done.9.refs_5_ = bf16[128,256]{1,0:T(8,128)(2,1)S(1)} collective-permute-done((bf16[128,256]{1,0:T(8,128)(2,1)S(1)}, bf16[128,256]{1,0:T(8,128)(2,1)S(1)}, u32[]{:S(2)}, u32[]{:S(2)}) %collective-permute-start.9) | collective-permute-done | bytes 65568 | tf_op jit(solution)/shard_map/ppermute | solution.py:40
  14.1 4.8 %collective-permute-start.13 = (bf16[128,256]{1,0:T(8,128)(2,1)S(1)}, bf16[128,256]{1,0:T(8,128)(2,1)S(1)}, u32[]{:S(2)}, u32[]{:S(2)}) collective-permute-start(bf16[128,256]{1,0:T(8,128)(2,1)S(1)} %collective-permute-done.10.refs_6_), channel_id=1, source_target_pairs={{0,1},{1,0},{2,3},{3,2},{4,5},{5,4},{6,7},{7,6},{8,9},{9,8},{10,11... | collective-permute-start | bytes 196616 | tf_op jit(solution)/shard_map/ppermute | solution.py:31
  19.0 0.0 collective-permute-start.2
  19.0 0.7 %collective-permute-start.7 = (bf16[144,256]{1,0:T(8,128)(2,1)S(1)}, bf16[144,256]{1,0:T(8,128)(2,1)S(1)}, u32[]{:S(2)}, u32[]{:S(2)}) collective-permute-start(bf16[144,256]{1,0:T(8,128)(2,1)S(1)} %collective-permute-done.6.refs_2_), channel_id=1, source_target_pairs={{0,1},{1,0},{2,3},{3,2},{4,5},{5,4},{6,7},{7,6},{8,9},{9,8},{10,11... | collective-permute-start | bytes 221192 | tf_op jit(solution)/shard_map/ppermute | solution.py:31
  19.7 0.0 collective-permute-start.5
  19.7 0.5 %collective-permute-start.12 = (bf16[128,256]{1,0:T(8,128)(2,1)S(1)}, bf16[128,256]{1,0:T(8,128)(2,1)S(1)}, u32[]{:S(2)}, u32[]{:S(2)}) collective-permute-start(bf16[128,256]{1,0:T(8,128)(2,1)S(1)} %collective-permute-done.9.refs_5_), channel_id=1, source_target_pairs={{0,1},{1,0},{2,3},{3,2},{4,5},{5,4},{6,7},{7,6},{8,9},{9,8},{10,11... | collective-permute-start | bytes 196616 | tf_op jit(solution)/shard_map/ppermute | solution.py:31
  20.2 0.1 collective-permute-start.11
  20.2 0.8 %collective-permute-done.12.refs_8_ = bf16[128,256]{1,0:T(8,128)(2,1)S(1)} collective-permute-done((bf16[128,256]{1,0:T(8,128)(2,1)S(1)}, bf16[128,256]{1,0:T(8,128)(2,1)S(1)}, u32[]{:S(2)}, u32[]{:S(2)}) %collective-permute-start.12) | collective-permute-done | bytes 65568 | tf_op jit(solution)/shard_map/ppermute | solution.py:31
  21.1 0.4 collective-permute-done.11.refs_7_
  21.4 1.0 %intermediate.1.refs_0_ = bf16[256,256]{1,0:T(8,128)(2,1)S(1)} custom-call(bf16[240,256]{1,0:T(8,128)(2,1)S(1)} %get-tuple-element.17.own, bf16[144,256]{1,0:T(8,128)(2,1)S(1)} %collective-permute-done.own_c, bf16[240,256]{1,0:T(8,128)(2,1)S(1)} %collective-permute-done.1.far, bf16[240,256]{1,0:T(8,128)(2,1)S(1)} %collective-permute-done.2.far_c, ...), custom_call_target="tpu_custom_call" | custom-call | tf_op jit(solution)/shard_map/intermediate/pallas_call | solution.py:328
  22.5 1.5 %collective-permute-start.16 = (bf16[256,256]{1,0:T(8,128)(2,1)S(1)}, bf16[256,256]{1,0:T(8,128)(2,1)S(1)}, u32[]{:S(2)}, u32[]{:S(2)}) collective-permute-start(bf16[256,256]{1,0:T(8,128)(2,1)S(1)} %intermediate.1.refs_0_), channel_id=1, source_target_pairs={{0,12},{1,13},{2,14},{3,15},{4,8},{5,9},{6,10},{7,11},{8,4},{9,5},... | collective-permute-start | bytes 393224 | tf_op jit(solution)/shard_map/ppermute | solution.py:31
  23.9 1.5 %collective-permute-start.15 = (bf16[256,256]{1,0:T(8,128)(2,1)S(1)}, bf16[256,256]{1,0:T(8,128)(2,1)S(1)}, u32[]{:S(2)}, u32[]{:S(2)}) collective-permute-start(bf16[256,256]{1,0:T(8,128)(2,1)S(1)} %intermediate.1.refs_0_), channel_id=1, source_target_pairs={{0,8},{1,9},{2,10},{3,11},{4,12},{5,13},{6,14},{7,15},{8,0},{9,1},... | collective-permute-start | bytes 393224 | tf_op jit(solution)/shard_map/ppermute | solution.py:31
  25.5 0.5 %collective-permute-start.14 = (bf16[256,256]{1,0:T(8,128)(2,1)S(1)}, bf16[256,256]{1,0:T(8,128)(2,1)S(1)}, u32[]{:S(2)}, u32[]{:S(2)}) collective-permute-start(bf16[256,256]{1,0:T(8,128)(2,1)S(1)} %intermediate.1.refs_0_), channel_id=1, source_target_pairs={{0,4},{1,5},{2,6},{3,7},{4,0},{5,1},{6,2},{7,3},{8,12},{9,13},{10,... | collective-permute-start | bytes 393224 | tf_op jit(solution)/shard_map/ppermute | solution.py:31
  26.0 3.0 %collective-permute-start.3 = (bf16[128,256]{1,0:T(8,128)(2,1)S(1)}, bf16[128,256]{1,0:T(8,128)(2,1)S(1)}, u32[]{:S(2)}, u32[]{:S(2)}) collective-permute-start(bf16[128,256]{1,0:T(8,128)(2,1)S(1)} %get-tuple-element.19), channel_id=1, source_target_pairs={{0,16},{1,17},{2,18},{3,19},{4,20},{5,21},{6,22},{7,23},{8,24},{9,... | collective-permute-start | bytes 196616 | tf_op jit(solution)/shard_map/ppermute | solution.py:31
  29.1 1.9 %factors.1 = (bf16[1024,1024]{1,0:T(8,128)(2,1)S(1)}, f32[4,256,256]{2,1,0:T(8,128)S(1)}, f32[2,64,256]{2,1,0:T(8,128)S(1)}, s32[2,8,128]{2,1,0:T(8,128)S(1)}) custom-call(f32[2,64,256]{2,1,0:T(8,128)} %resid.3, bf16[240,256]{1,0:T(8,128)(2,1)S(1)} %get-tuple-element.17.own, bf16[240,256]{1,0:T(8,128)(2,1)S(1)} %collective-permute-done.1.far, s32[2]{0:T(128)} %swap.1), custom_call_target="tpu_custom_call" | custom-call | tf_op jit(solution)/shard_map/factors/pallas_call | solution.py:342
  31.0 0.5 %collective-permute-done.3.resid_far = bf16[128,256]{1,0:T(8,128)(2,1)S(1)} collective-permute-done((bf16[128,256]{1,0:T(8,128)(2,1)S(1)}, bf16[128,256]{1,0:T(8,128)(2,1)S(1)}, u32[]{:S(2)}, u32[]{:S(2)}) %collective-permute-start.3) | collective-permute-done | bytes 65568 | tf_op jit(solution)/shard_map/ppermute | solution.py:31
  31.5 1.8 %collective-permute-done.15.refs_2_ = bf16[256,256]{1,0:T(8,128)(2,1)S(1)} collective-permute-done((bf16[256,256]{1,0:T(8,128)(2,1)S(1)}, bf16[256,256]{1,0:T(8,128)(2,1)S(1)}, u32[]{:S(2)}, u32[]{:S(2)}) %collective-permute-start.15) | collective-permute-done | bytes 131104 | tf_op jit(solution)/shard_map/ppermute | solution.py:31
  33.2 1.4 %cycle.1 = (f32[2,64,256]{2,1,0:T(8,128)S(1)}, bf16[2,64,256]{2,1,0:T(8,128)(2,1)S(1)}, bf16[2,64,256]{2,1,0:T(8,128)(2,1)S(1)}, bf16[2,64,256]{2,1,0:T(8,128)(2,1)S(1)}) custom-call(bf16[240,256]{1,0:T(8,128)(2,1)S(1)} %get-tuple-element.17.own, bf16[144,256]{1,0:T(8,128)(2,1)S(1)} %collective-permute-done.own_c, ...), custom_call_target="tpu_custom_call" | custom-call | tf_op jit(solution)/shard_map/cycle/pallas_call | solution.py:358
  34.6 0.1 collective-permute-start.17
  34.7 0.6 %collective-permute-start.18 = (bf16[2,64,256]{2,1,0:T(8,128)(2,1)S(1)}, bf16[2,64,256]{2,1,0:T(8,128)(2,1)S(1)}, u32[]{:S(2)}, u32[]{:S(2)}) collective-permute-start(bf16[2,64,256]{2,1,0:T(8,128)(2,1)S(1)} %get-tuple-element.27), channel_id=1, source_target_pairs={{0,2},{1,3},{2,0},{3,1},{4,6},{5,7},{6,4},{7,5},{8,10},{9,11},{10,... | collective-permute-start | bytes 196616 | tf_op jit(solution)/shard_map/ppermute | solution.py:31
  35.3 1.3 %collective-permute-start.19 = (bf16[2,64,256]{2,1,0:T(8,128)(2,1)S(1)}, bf16[2,64,256]{2,1,0:T(8,128)(2,1)S(1)}, u32[]{:S(2)}, u32[]{:S(2)}) collective-permute-start(bf16[2,64,256]{2,1,0:T(8,128)(2,1)S(1)} %get-tuple-element.28), channel_id=1, source_target_pairs={{0,3},{1,2},{2,1},{3,0},{4,7},{5,6},{6,5},{7,4},{8,11},{9,10},{10,... | collective-permute-start | bytes 196616 | tf_op jit(solution)/shard_map/ppermute | solution.py:31
  36.6 3.1 %collective-permute-done.18 = bf16[2,64,256]{2,1,0:T(8,128)(2,1)S(1)} collective-permute-done((bf16[2,64,256]{2,1,0:T(8,128)(2,1)S(1)}, bf16[2,64,256]{2,1,0:T(8,128)(2,1)S(1)}, u32[]{:S(2)}, u32[]{:S(2)}) %collective-permute-start.18) | collective-permute-done | bytes 65568 | tf_op jit(solution)/shard_map/ppermute | solution.py:31
  39.6 0.5 %collective-permute-done.19 = bf16[2,64,256]{2,1,0:T(8,128)(2,1)S(1)} collective-permute-done((bf16[2,64,256]{2,1,0:T(8,128)(2,1)S(1)}, bf16[2,64,256]{2,1,0:T(8,128)(2,1)S(1)}, u32[]{:S(2)}, u32[]{:S(2)}) %collective-permute-start.19) | collective-permute-done | bytes 65568 | tf_op jit(solution)/shard_map/ppermute | solution.py:31
  40.1 0.7 %add_multiply_fusion = f32[2,64,256]{2,1,0:T(8,128)} fusion(bf16[2,64,256]{2,1,0:T(8,128)(2,1)S(1)} %collective-permute-done.19, bf16[2,64,256]{2,1,0:T(8,128)(2,1)S(1)} %collective-permute-done.18, f32[2,64,256]{2,1,0:T(8,128)S(1)} %get-tuple-element.25, bf16[2,64,256]{2,1,0:T(8,128)(2,1)S(1)} %collective-permute-done.17), kind=kLoop, calls=%fused_computation | loop fusion | flops 229376 | bytes 458752 | tf_op jit(solution)/shard_map/mul | solution.py:367
  (13 shorter events, 0.0 us)
Async XLA Ops:
  1.4 17.6 %collective-permute-start.1 = (bf16[240,256]{1,0:T(8,128)(2,1)S(1)}, bf16[240,256]{1,0:T(8,128)(2,1)S(1)}, u32[]{:S(2)}, u32[]{:S(2)}) collective-permute-start(bf16[240,256]{1,0:T(8,128)(2,1)S(1)} %get-tuple-element.17.own), channel_id=1, source_target_pairs={{0,16},{1,17},{2,18},{3,19},{4,20},{5,21},{6,22},{7,23},{8,24},{9,... | collective-permute-start | bytes 368648 | tf_op jit(solution)/shard_map/ppermute | solution.py:31
  5.5 5.4 %collective-permute-start.10 = (bf16[128,256]{1,0:T(8,128)(2,1)S(1)}, bf16[128,256]{1,0:T(8,128)(2,1)S(1)}, u32[]{:S(2)}, u32[]{:S(2)}) collective-permute-start(bf16[128,256]{1,0:T(8,128)(2,1)S(1)} %get-tuple-element.24.half_own), channel_id=1, source_target_pairs={{0,12},{1,29},{2,14},{3,31},{4,8},{5,25},{6,10},{7,27},{8,4},{9,21... | collective-permute-start | bytes 196616 | tf_op jit(solution)/shard_map/ppermute | solution.py:40
  8.0 6.1 %collective-permute-start.9 = (bf16[128,256]{1,0:T(8,128)(2,1)S(1)}, bf16[128,256]{1,0:T(8,128)(2,1)S(1)}, u32[]{:S(2)}, u32[]{:S(2)}) collective-permute-start(bf16[128,256]{1,0:T(8,128)(2,1)S(1)} %get-tuple-element.24.half_own), channel_id=1, source_target_pairs={{0,8},{1,25},{2,10},{3,27},{4,12},{5,29},{6,14},{7,31},{8,0},{9,17... | collective-permute-start | bytes 196616 | tf_op jit(solution)/shard_map/ppermute | solution.py:40
  8.5 5.7 %collective-permute-start.8 = (bf16[128,256]{1,0:T(8,128)(2,1)S(1)}, bf16[128,256]{1,0:T(8,128)(2,1)S(1)}, u32[]{:S(2)}, u32[]{:S(2)}) collective-permute-start(bf16[128,256]{1,0:T(8,128)(2,1)S(1)} %get-tuple-element.24.half_own), channel_id=1, source_target_pairs={{0,4},{1,21},{2,6},{3,23},{4,0},{5,17},{6,2},{7,19},{8,12},{9,29},... | collective-permute-start | bytes 196616 | tf_op jit(solution)/shard_map/ppermute | solution.py:40
  9.0 10.0 %collective-permute-start.6 = (bf16[144,256]{1,0:T(8,128)(2,1)S(1)}, bf16[144,256]{1,0:T(8,128)(2,1)S(1)}, u32[]{:S(2)}, u32[]{:S(2)}) collective-permute-start(bf16[144,256]{1,0:T(8,128)(2,1)S(1)} %get-tuple-element.18), channel_id=1, source_target_pairs={{0,18},{1,19},{2,16},{3,17},{4,22},{5,23},{6,20},{7,21},{8,26},{9,... | collective-permute-start | bytes 221192 | tf_op jit(solution)/shard_map/ppermute | solution.py:31
  10.9 8.7 %collective-permute-start.4 = (bf16[144,256]{1,0:T(8,128)(2,1)S(1)}, bf16[144,256]{1,0:T(8,128)(2,1)S(1)}, u32[]{:S(2)}, u32[]{:S(2)}) collective-permute-start(bf16[144,256]{1,0:T(8,128)(2,1)S(1)} %get-tuple-element.18), channel_id=1, source_target_pairs={{0,2},{1,3},{2,0},{3,1},{4,6},{5,7},{6,4},{7,5},{8,10},{9,11},{10,... | collective-permute-start | bytes 221192 | tf_op jit(solution)/shard_map/ppermute | solution.py:31
  14.1 5.5 %collective-permute-start = (bf16[144,256]{1,0:T(8,128)(2,1)S(1)}, bf16[144,256]{1,0:T(8,128)(2,1)S(1)}, u32[]{:S(2)}, u32[]{:S(2)}) collective-permute-start(bf16[144,256]{1,0:T(8,128)(2,1)S(1)} %get-tuple-element.18), channel_id=1, source_target_pairs={{0,1},{1,0},{2,3},{3,2},{4,5},{5,4},{6,7},{7,6},{8,9},{9,8},{10,11... | collective-permute-start | bytes 221192 | tf_op jit(solution)/shard_map/ppermute | solution.py:31
  14.1 6.0 %collective-permute-start.13 = (bf16[128,256]{1,0:T(8,128)(2,1)S(1)}, bf16[128,256]{1,0:T(8,128)(2,1)S(1)}, u32[]{:S(2)}, u32[]{:S(2)}) collective-permute-start(bf16[128,256]{1,0:T(8,128)(2,1)S(1)} %collective-permute-done.10.refs_6_), channel_id=1, source_target_pairs={{0,1},{1,0},{2,3},{3,2},{4,5},{5,4},{6,7},{7,6},{8,9},{9,8},{10,11... | collective-permute-start | bytes 196616 | tf_op jit(solution)/shard_map/ppermute | solution.py:31
  19.0 2.5 %collective-permute-start.2 = (bf16[240,256]{1,0:T(8,128)(2,1)S(1)}, bf16[240,256]{1,0:T(8,128)(2,1)S(1)}, u32[]{:S(2)}, u32[]{:S(2)}) collective-permute-start(bf16[240,256]{1,0:T(8,128)(2,1)S(1)} %collective-permute-done.1.far), channel_id=1, source_target_pairs={{0,1},{1,0},{2,3},{3,2},{4,5},{5,4},{6,7},{7,6},{8,9},{9,8},{10,11... | collective-permute-start | bytes 368648 | tf_op jit(solution)/shard_map/ppermute | solution.py:31
  19.0 2.5 %collective-permute-start.7 = (bf16[144,256]{1,0:T(8,128)(2,1)S(1)}, bf16[144,256]{1,0:T(8,128)(2,1)S(1)}, u32[]{:S(2)}, u32[]{:S(2)}) collective-permute-start(bf16[144,256]{1,0:T(8,128)(2,1)S(1)} %collective-permute-done.6.refs_2_), channel_id=1, source_target_pairs={{0,1},{1,0},{2,3},{3,2},{4,5},{5,4},{6,7},{7,6},{8,9},{9,8},{10,11... | collective-permute-start | bytes 221192 | tf_op jit(solution)/shard_map/ppermute | solution.py:31
  19.7 1.8 %collective-permute-start.5 = (bf16[144,256]{1,0:T(8,128)(2,1)S(1)}, bf16[144,256]{1,0:T(8,128)(2,1)S(1)}, u32[]{:S(2)}, u32[]{:S(2)}) collective-permute-start(bf16[144,256]{1,0:T(8,128)(2,1)S(1)} %collective-permute-done.4.refs_0_), channel_id=1, source_target_pairs={{0,1},{1,0},{2,3},{3,2},{4,5},{5,4},{6,7},{7,6},{8,9},{9,8},{10,11... | collective-permute-start | bytes 221192 | tf_op jit(solution)/shard_map/ppermute | solution.py:31
  19.7 1.4 %collective-permute-start.12 = (bf16[128,256]{1,0:T(8,128)(2,1)S(1)}, bf16[128,256]{1,0:T(8,128)(2,1)S(1)}, u32[]{:S(2)}, u32[]{:S(2)}) collective-permute-start(bf16[128,256]{1,0:T(8,128)(2,1)S(1)} %collective-permute-done.9.refs_5_), channel_id=1, source_target_pairs={{0,1},{1,0},{2,3},{3,2},{4,5},{5,4},{6,7},{7,6},{8,9},{9,8},{10,11... | collective-permute-start | bytes 196616 | tf_op jit(solution)/shard_map/ppermute | solution.py:31
  20.2 1.3 %collective-permute-start.11 = (bf16[128,256]{1,0:T(8,128)(2,1)S(1)}, bf16[128,256]{1,0:T(8,128)(2,1)S(1)}, u32[]{:S(2)}, u32[]{:S(2)}) collective-permute-start(bf16[128,256]{1,0:T(8,128)(2,1)S(1)} %collective-permute-done.8.refs_4_), channel_id=1, source_target_pairs={{0,1},{1,0},{2,3},{3,2},{4,5},{5,4},{6,7},{7,6},{8,9},{9,8},{10,11... | collective-permute-start | bytes 196616 | tf_op jit(solution)/shard_map/ppermute | solution.py:31
  22.5 9.0 %collective-permute-start.16 = (bf16[256,256]{1,0:T(8,128)(2,1)S(1)}, bf16[256,256]{1,0:T(8,128)(2,1)S(1)}, u32[]{:S(2)}, u32[]{:S(2)}) collective-permute-start(bf16[256,256]{1,0:T(8,128)(2,1)S(1)} %intermediate.1.refs_0_), channel_id=1, source_target_pairs={{0,12},{1,13},{2,14},{3,15},{4,8},{5,9},{6,10},{7,11},{8,4},{9,5},... | collective-permute-start | bytes 393224 | tf_op jit(solution)/shard_map/ppermute | solution.py:31
  23.9 9.3 %collective-permute-start.15 = (bf16[256,256]{1,0:T(8,128)(2,1)S(1)}, bf16[256,256]{1,0:T(8,128)(2,1)S(1)}, u32[]{:S(2)}, u32[]{:S(2)}) collective-permute-start(bf16[256,256]{1,0:T(8,128)(2,1)S(1)} %intermediate.1.refs_0_), channel_id=1, source_target_pairs={{0,8},{1,9},{2,10},{3,11},{4,12},{5,13},{6,14},{7,15},{8,0},{9,1},... | collective-permute-start | bytes 393224 | tf_op jit(solution)/shard_map/ppermute | solution.py:31
  25.5 7.7 %collective-permute-start.14 = (bf16[256,256]{1,0:T(8,128)(2,1)S(1)}, bf16[256,256]{1,0:T(8,128)(2,1)S(1)}, u32[]{:S(2)}, u32[]{:S(2)}) collective-permute-start(bf16[256,256]{1,0:T(8,128)(2,1)S(1)} %intermediate.1.refs_0_), channel_id=1, source_target_pairs={{0,4},{1,5},{2,6},{3,7},{4,0},{5,1},{6,2},{7,3},{8,12},{9,13},{10,... | collective-permute-start | bytes 393224 | tf_op jit(solution)/shard_map/ppermute | solution.py:31
  26.0 5.4 %collective-permute-start.3 = (bf16[128,256]{1,0:T(8,128)(2,1)S(1)}, bf16[128,256]{1,0:T(8,128)(2,1)S(1)}, u32[]{:S(2)}, u32[]{:S(2)}) collective-permute-start(bf16[128,256]{1,0:T(8,128)(2,1)S(1)} %get-tuple-element.19), channel_id=1, source_target_pairs={{0,16},{1,17},{2,18},{3,19},{4,20},{5,21},{6,22},{7,23},{8,24},{9,... | collective-permute-start | bytes 196616 | tf_op jit(solution)/shard_map/ppermute | solution.py:31
  34.6 1.9 %collective-permute-start.17 = (bf16[2,64,256]{2,1,0:T(8,128)(2,1)S(1)}, bf16[2,64,256]{2,1,0:T(8,128)(2,1)S(1)}, u32[]{:S(2)}, u32[]{:S(2)}) collective-permute-start(bf16[2,64,256]{2,1,0:T(8,128)(2,1)S(1)} %get-tuple-element.26), channel_id=1, source_target_pairs={{0,1},{1,0},{2,3},{3,2},{4,5},{5,4},{6,7},{7,6},{8,9},{9,8},{10,11... | collective-permute-start | bytes 196616 | tf_op jit(solution)/shard_map/ppermute | solution.py:31
  34.7 5.0 %collective-permute-start.18 = (bf16[2,64,256]{2,1,0:T(8,128)(2,1)S(1)}, bf16[2,64,256]{2,1,0:T(8,128)(2,1)S(1)}, u32[]{:S(2)}, u32[]{:S(2)}) collective-permute-start(bf16[2,64,256]{2,1,0:T(8,128)(2,1)S(1)} %get-tuple-element.27), channel_id=1, source_target_pairs={{0,2},{1,3},{2,0},{3,1},{4,6},{5,7},{6,4},{7,5},{8,10},{9,11},{10,... | collective-permute-start | bytes 196616 | tf_op jit(solution)/shard_map/ppermute | solution.py:31
  35.3 4.9 %collective-permute-start.19 = (bf16[2,64,256]{2,1,0:T(8,128)(2,1)S(1)}, bf16[2,64,256]{2,1,0:T(8,128)(2,1)S(1)}, u32[]{:S(2)}, u32[]{:S(2)}) collective-permute-start(bf16[2,64,256]{2,1,0:T(8,128)(2,1)S(1)} %get-tuple-element.28), channel_id=1, source_target_pairs={{0,3},{1,2},{2,1},{3,0},{4,7},{5,6},{6,5},{7,4},{8,11},{9,10},{10,... | collective-permute-start | bytes 196616 | tf_op jit(solution)/shard_map/ppermute | solution.py:31

commit v3 on v2

--- a/solution.py
+++ b/solution.py
@@ -47,7 +47,7 @@
 
 
 def prepare(
-    amps, block, resid, virt, pair, items, owners, wanted, share, lean_out, full_out, half_out, resid_out, *scratch
+    amps, block, resid, virt, pair, items, owners, wanted, share, lean_out, half_out, tail_out, resid_out, *scratch
 ):
     hbm = (amps, block, resid, virt, pair, items, owners, wanted, share)
     held, sems = scratch[:-1], scratch[-1]
@@ -71,27 +71,29 @@
     ).astype(BF16)
     source = owners[...] * pairs + wanted[...]
     hits = (source == iota((domain, n_req), 0)).astype(BF16)
-    row, col = iota((8, n_req), 0), iota((8, n_req), 1)
+    row, col = iota((TILE, n_req), 0), iota((TILE, n_req), 1)
     into = ((col // (n_req // pairs) == row // pairs) & (share[...] == row % pairs)).astype(BF16)
-    counts = dot(into, hits, NT)
-    row = iota((8, domain), 0)
-    energy = jnp.zeros((8, domain), F32)
+    extras = dot(into, hits, NT)
+    terms, lines = pairs * pairs, 2 * pairs
+    row = iota((TILE, domain), 0)
+    line = (row - terms) % lines
+    energy = jnp.zeros((TILE, domain), F32)
     for p in range(pairs):
-        energy = jnp.where(row == p, virt[p : p + 1, :], energy)
-        energy = jnp.where(row == pairs + p, pair[p], energy)
+        energy = jnp.where(line == p, virt[p : p + 1, :], energy)
+        energy = jnp.where(line == pairs + p, pair[p], energy)
     high = energy.astype(BF16).astype(F32)
     middle = (energy - high).astype(BF16).astype(F32)
     low = energy - high - middle
-    full_out[rows + TILE + height :, :] = jnp.concatenate([counts, high, middle, low], axis=0).astype(BF16)
+    for k, part in enumerate((high, middle, low)):
+        extras = jnp.where((row - terms) // lines == k, jnp.where(row >= terms, part, extras), extras)
+    tail_out[:TILE, :] = extras.astype(BF16)
     lean_out[rows:, :] = named
-    full_out[rows : rows + TILE, :] = named
     copies[0].wait()
     amp_half = amps[...].astype(BF16).reshape(rows, domain)
     lean_out[:rows, :] = amp_half
-    full_out[:rows, :] = amp_half
     copies[1].wait()
     half_out[...] = dot(chosen, block[0], NT).astype(BF16)
-    full_out[rows + TILE : rows + TILE + height, :] = dot(mine, block[0], NT).astype(BF16)
+    tail_out[TILE:, :] = dot(mine, block[0], NT).astype(BF16)
     copies[2].wait()
     resid_out[...] = resid[...].astype(BF16).reshape(rows, domain)
 
@@ -100,7 +102,7 @@
     return jnp.where(core == 0, own, other), jnp.where(core == 0, other, own)
 
 
-def intermediate(n_shared, items, pairs, own, own_c, far, far_c, half_own, *refs):
+def intermediate(n_shared, items, pairs, own, own_c, far, far_c, far_tail, far_tail_c, half_own, *refs):
     y_refs, rest, out = refs[: 4 * n_shared], refs[4 * n_shared : -1], refs[-1]
     half_rows, domain = half_own.shape
     height = half_rows // 2
@@ -124,10 +126,8 @@
 
     if len(rest) > 1:
         count = len(rest) // 2
-        near_quarter = far[lean : lean + height, :]
-        away_quarter = far_c[lean : lean + height, :]
         product = chosen(half_own[...], group)
-        product += chosen(jnp.concatenate(ordered(core, near_quarter, away_quarter), axis=0), group ^ half)
+        product += chosen(jnp.concatenate(ordered(core, far_tail[TILE:, :], far_tail_c[TILE:, :]), axis=0), group ^ half)
         for j in range(count):
             product += chosen(rest[j][...], family ^ (j + 1))
             product += chosen(rest[count + j][...], family ^ half ^ (j + 1))
@@ -145,14 +145,14 @@
 
 
 def spread_counts(own, far, swaps, half_rows, lanes):
-    start, pairs = own.shape[0] - 32, len(swaps)
-    counts = jnp.concatenate([own[start : start + 8, :lanes], far[start : start + 8, :lanes]], axis=0)
+    pairs = len(swaps)
+    counts = jnp.concatenate([own[:TILE, :lanes], far[:TILE, :lanes]], axis=0)
     tall = 2 * pairs * pairs * half_rows
-    term = iota((tall, 16), 0) // half_rows
+    term = iota((tall, 2 * TILE), 0) // half_rows
     which = term
     for p, swap in enumerate(swaps):
-        which = jnp.where(term // pairs == pairs + p, 8 + swap * pairs + term % pairs, which)
-    return dot((which == iota((tall, 16), 1)).astype(BF16), counts).astype(BF16)
+        which = jnp.where(term // pairs == pairs + p, TILE + swap * pairs + term % pairs, which)
+    return dot((which == iota((tall, 2 * TILE), 1)).astype(BF16), counts).astype(BF16)
 
 
 def weights(spread, source_group, pairs, half_rows):
@@ -167,48 +167,54 @@
     return -(-lax.axis_size("pairs") * pairs // 128) * 128
 
 
-def factors(n_units, resid, own, far, swap, weights_out, inverse_out, base_out, swap_out, *scratch):
-    held, sems = scratch[:-1], scratch[-1]
-    copies = [pltpu.make_async_copy(src, dst, sems.at[i]) for i, (src, dst) in enumerate(zip((resid, swap), held))]
-    for copy in copies:
-        copy.start()
-    resid, swap = held
-    pairs, height, domain = resid.shape
-    half_rows = 2 * height
+def energies(packed, pairs):
+    parts, lines, start = packed[:TILE, :].astype(F32), 2 * pairs, pairs * pairs
+    energy = parts[start : start + lines]
+    for k in (1, 2):
+        energy += parts[start + k * lines : start + (k + 1) * lines]
+    energy = jnp.concatenate([energy, jnp.zeros((8 - lines, energy.shape[1]), F32)], axis=0)
+    return energy, energy.T
+
+
+def inverse_of(energy, tall_energy, p, pairs):
+    return 1.0 / (tall_energy[:, p : p + 1] + energy[p : p + 1] - energy[pairs + p : pairs + p + 1])
+
+
+def near_factors(resid, own, inverse_out, base_out, held, sem):
+    copy = pltpu.make_async_copy(resid, held, sem)
+    copy.start()
+    pairs, height, _ = resid.shape
+    near = energies(own, pairs)
+    for p in range(pairs):
+        inverse_out[p] = inverse_of(*near, p, pairs)
+    start = pl.multiple_of(lax.axis_index("ints") * height, height)
+    copy.wait()
+    base_out[...] = held[...] * inverse_out[:, pl.ds(start, height), :]
+
+
+def factors(n_units, pairs, own, far, swap, weights_out, inverse_out, swap_out, held, sem):
+    copy = pltpu.make_async_copy(swap, held, sem)
+    copy.start()
+    half_rows = weights_out.shape[0] // (2 * pairs * pairs)
     wide = pairs * half_rows
-    group, member, _, family, half = place()
-    for copy in copies:
-        copy.wait()
-    swaps = [swap[p] - (group ^ half) * pairs for p in range(pairs)]
+    group, _, _, family, half = place()
+    away = energies(far, pairs)
+    away = [inverse_of(*away, p, pairs) for p in range(pairs)]
+    copy.wait()
+    swaps = [held[p] - (group ^ half) * pairs for p in range(pairs)]
     spread = spread_counts(own, far, swaps, half_rows, lanes_of(pairs))
     for k in range(n_units):
         weights_out[:, k * wide : (k + 1) * wide] = weights(spread, family ^ k, pairs, half_rows)
-    start = own.shape[0] - 24
-
-    def energy_of(packed):
-        parts = packed[start : start + 24, :].astype(F32)
-        energy = parts[:8] + parts[8:16] + parts[16:24]
-        return energy, energy.T
-
-    def inverse(energy, tall_energy, p):
-        divisor = tall_energy[:, p : p + 1] + energy[p : p + 1] - energy[pairs + p : pairs + p + 1]
-        return 1.0 / divisor
-
-    near, away = energy_of(own), energy_of(far)
-    away = [inverse(*away, p) for p in range(pairs)]
     for p in range(pairs):
-        inverse_out[p] = inverse(*near, p)
-        inverse_out[pairs + p] = functools.reduce(
+        inverse_out[p] = functools.reduce(
             lambda kept, k: jnp.where(swaps[p] == k, away[k], kept), range(1, pairs), away[0]
         )
         swap_out[p] = jnp.full(swap_out.shape[1:], swaps[p], jnp.int32)
-    rows = pl.ds(pl.multiple_of(member * height, height), height)
-    base_out[...] = resid[...] * inverse_out[:pairs, rows, :]
-
-
-def cycle(n_sends, pairs, own, own_c, far, far_c, resid_far, mix, inverse, base, swap, *refs):
+
+
+def cycle(n_sends, pairs, own, own_c, far, far_c, tail, far_tail, resid_far, mix, inverse, inverse_far, base, swap, *refs):
     units, (own_out, *sends), (here, there) = refs[: -n_sends - 3], refs[-n_sends - 3 : -2], refs[-2:]
-    height, domain = resid_far.shape[0] // pairs, resid_far.shape[1]
+    height, domain = base.shape[1:]
     rows = pairs * height
     half_rows = 2 * height
     group, member, core, family, half = place()
@@ -216,7 +222,7 @@
         mixed = dot(mix[...], jnp.concatenate([unit[...] for unit in units], axis=0))
     else:
         swaps = [swap[p, :1, :1] for p in range(pairs)]
-        spread = spread_counts(own, far, swaps, half_rows, lanes_of(pairs))
+        spread = spread_counts(tail, far_tail, swaps, half_rows, lanes_of(pairs))
         first = group - group % half
         mixed = lax.fori_loop(
             0,
@@ -244,7 +250,7 @@
         there[start, :] += functools.reduce(
             lambda kept, k: jnp.where(named == k, parts[k], kept), range(1, pairs), parts[0]
         )
-        mirror = (there[...] * inverse[pairs + p]).T
+        mirror = (there[...] * inverse_far[p]).T
         at = p * wide
         here[p] = dot(mixed[at : at + wide], near, TN) * inverse[p] + mirror
     own_out[...] = here[:, start, :] + base[...]
@@ -257,11 +263,15 @@
 HB = pl.BlockSpec(memory_space=pltpu.HBM)
 
 
+def after(value, *others):
+    return lax.optimization_barrier((value, *others))[0] if others else value
+
+
 def stay(value):
     return pltpu.with_memory_space_constraint(value, pltpu.HBM)
 
 
-def call(kernel, outs, in_specs, name, scratch=()):
+def call(kernel, outs, in_specs, name, scratch=(), flops=0):
     return pl.pallas_call(
         kernel,
         out_shape=outs,
@@ -269,6 +279,7 @@
         out_specs=jax.tree.map(lambda _: VM, outs),
         scratch_shapes=scratch,
         name=name,
+        cost_estimate=pl.CostEstimate(flops=flops, bytes_accessed=0, transcendentals=0) if flops else None,
         compiler_params=pltpu.CompilerParams(vmem_limit_bytes=48 * 1024 * 1024),
     )
 
@@ -300,12 +311,12 @@
         share_pair.reshape(1, -1),
         share_amp.reshape(1, -1),
     )
-    lean, own, half_own, resid_half = call(
+    lean, half_own, tail, resid_half = call(
         prepare,
         [
             shape((rows + TILE, domain), BF16),
-            shape((rows + TILE + height + 32, domain), BF16),
             shape((half_rows, domain), BF16),
+            shape((TILE + height, domain), BF16),
             shape((rows, domain), BF16),
         ],
         [HB] * len(operands),
@@ -313,24 +324,37 @@
         [(pltpu.SMEM if o is pair_energy else pltpu.VMEM)(o.shape, o.dtype) for o in operands]
         + [pltpu.SemaphoreType.DMA((len(operands),))],
     )(*map(stay, operands))
-    far = exchange(own, half, 0)
+    inverse, base = call(
+        near_factors,
+        [shape((pairs, domain, domain), F32), shape((pairs, height, domain), F32)],
+        [HB, VM],
+        "near_factors",
+        [pltpu.VMEM(resid_rest.shape, F32), pltpu.SemaphoreType.DMA],
+        10**9,
+    )(stay(resid_rest), tail)
+
+    def across(value, *others):
+        return exchange(after(value, *others), 0, CORE)
+
+    far, far_tail = exchange(lean, half, 0), exchange(tail, half, 0)
     y_own = [exchange(lean, 0, k) for k in range(2, n_ints, 2)]
-    y_far = [exchange(lean, half, k) for k in range(2, n_ints, 2)]
-    across = lambda value: exchange(value, 0, CORE)
-    own_c, far_c = across(lean), across(far)
+    blocks = [family_exchange(half_own, j) for j in range(1, half)] if n_pairs <= DIRECT else []
+    y_far = [exchange(after(far, *y_own), 0, k) for k in range(2, n_ints, 2)]
+    lead = blocks[:1]
+    own_c, far_c = across(lean, *lead), across(far)
+    far_tail_c = across(far_tail)
     if n_pairs <= DIRECT:
-        blocks = [family_exchange(half_own, j) for j in range(1, half)]
         blocks += [across(block) for block in blocks]
     else:
         blocks = [lax.all_gather(half_own, "pairs", axis=0, tiled=False)]
-    near_rows = [v for y in y_own for v in (y, across(y))]
+    near_rows = [v for y in y_own for v in (y, across(y, *lead))]
     away_rows = [v for y in y_far for v in (y, across(y))]
     inter = call(
         functools.partial(intermediate, len(y_own), item_block.shape[0], pairs),
         shape((pairs * half_rows, domain), BF16),
-        [VM] * (5 + len(near_rows) + len(away_rows) + len(blocks)),
+        [VM] * (7 + len(near_rows) + len(away_rows) + len(blocks)),
         "intermediate",
-    )(own, own_c, far, far_c, half_own, *near_rows, *away_rows, *blocks)
+    )(lean, own_c, far, far_c, far_tail, far_tail_c, half_own, *near_rows, *away_rows, *blocks)
     if n_pairs <= DIRECT:
         units = [inter] + [exchange(inter, j, 0) for j in range(1, half)]
     else:
@@ -339,29 +363,24 @@
         units = [lax.dynamic_slice_in_dim(every, first, half, 0)]
     resid_far = exchange(resid_half, half, 0)
     n_units = len(units)
-    mix, inverse, base, swap = call(
-        functools.partial(factors, n_units if n_units > 1 else 0),
+    mix, inverse_far, swap = call(
+        functools.partial(factors, n_units if n_units > 1 else 0, pairs),
         [
             shape((2 * pairs * pairs * half_rows, n_units * pairs * half_rows), BF16),
-            shape((2 * pairs, domain, domain), F32),
-            shape((pairs, height, domain), F32),
+            shape((pairs, domain, domain), F32),
             shape((pairs, 8, 128), jnp.int32),
         ],
-        [HB, VM, VM, HB],
+        [VM, VM, HB],
         "factors",
-        [
-            pltpu.VMEM(resid_rest.shape, F32),
-            pltpu.SMEM(transpose_pair.shape, jnp.int32),
-            pltpu.SemaphoreType.DMA((2,)),
-        ],
-    )(stay(resid_rest), own, far, stay(transpose_pair))
+        [pltpu.SMEM(transpose_pair.shape, jnp.int32), pltpu.SemaphoreType.DMA],
+    )(tail, far_tail, stay(transpose_pair))
     mine, *sends = call(
         functools.partial(cycle, n_ints - 1, pairs),
         [shape((pairs, height, domain), F32)] + [shape((pairs, height, domain), BF16)] * (n_ints - 1),
-        [VM] * (9 + n_units),
+        [VM] * (12 + n_units),
         "cycle",
         [pltpu.VMEM((pairs, domain, domain), F32), pltpu.VMEM((domain, domain), F32)],
-    )(own, own_c, far, far_c, resid_far, mix, inverse, base, swap, *units)
+    )(lean, own_c, far, far_c, tail, far_tail, resid_far, mix, inverse, inverse_far, base, swap, *units)
     for offset, send in enumerate(sends, 1):
         mine = mine + exchange(send, 0, offset).astype(F32)
     return -0.5 * mine

time: 41 us -> 38.7 us (0.944)
  starting transfers between devices: 25 us -> 22.7 us
  waiting for transfers between devices: 9.37 us -> 8.77 us
  Pallas kernels: 5.71 us -> 6.21 us
    ppermute x17 -> x19, starting transfers between devices: 21.5 us -> 17.7 us  [exchange(): return lax.ppermute(value, ('pairs', 'ints'), route)]
    ppermute x3, starting transfers between devices: 3.49 us -> 5.08 us  [family_exchange(): return lax.ppermute(value, ('pairs', 'ints'), route)]
    ppermute x3, waiting for transfers between devices: 2.33 us -> 1.31 us  [family_exchange(): return lax.ppermute(value, ('pairs', 'ints'), route)]
    pallas_call x2 -> x3, Pallas kernels: 3.31 us -> 3.81 us  [the longest x1 1.5 us: body(): call(functools.partial(factors, n_units if n_units > 1 else 0, pairs), [s...]
    ppermute x17 -> x19, waiting for transfers between devices: 7.04 us -> 7.46 us  [exchange(): return lax.ppermute(value, ('pairs', 'ints'), route)]
  transfers between devices with their start and end apart: 20 -> 22, of which waited for: 8 -> 9; matrix products, arithmetic and copies ran while one was open for 0% -> 0% of each run, Pallas kernels for 5% -> 6%
where the time goes in v3:
time: 38.7 us; the launch traced here: 38.5 us
  starting transfers between devices  22.7 us (59%)
  waiting for transfers between devices  8.77 us (23%)
  Pallas kernels  6.21 us (16%)
  other arithmetic  0.69 us (2%)
    ppermute x19, starting transfers between devices, exchange(): return lax.ppermute(value, ('pairs', 'ints'), route)  17.7 us
    ppermute x19, waiting for transfers between devices, exchange(): return lax.ppermute(value, ('pairs', 'ints'), route)  7.46 us
    ppermute x3, starting transfers between devices, family_exchange(): return lax.ppermute(value, ('pairs', 'ints'), route)  5.08 us
    pallas_call x1, Pallas kernels, body(): call(functools.partial(factors, n_units if n_units > 1 else 0, pairs), [s...  1.5 us
    pallas_call x1, Pallas kernels, body(): call(prepare, [shape((rows + TILE, domain), BF16), shape((half_rows, doma...  1.39 us
    pallas_call x1, Pallas kernels, body(): call(functools.partial(cycle, n_ints - 1, pairs), [shape((pairs, height,...  1.38 us
    ppermute x3, waiting for transfers between devices, family_exchange(): return lax.ppermute(value, ('pairs', 'ints'), route)  1.31 us
    pallas_call x1, Pallas kernels, body(): call(functools.partial(intermediate, len(y_own), item_block.shape[0], pai...  1.01 us
  transfers between devices with their start and end apart: 22, of which 9 were waited for; matrix products, arithmetic and copies ran while one was open for 0% of the time, Pallas kernels for 6%

profile of v3, /device:TPU:0, one launch (start us, length us, event | category | flops | bytes accessed | tf_op | source)
XLA Modules:
  0.0 38.5 jit_solution(2710663974862231490)
XLA Ops:
  0.0 1.4 %prepare.1 = (bf16[144,256]{1,0:T(8,128)(2,1)S(1)}, bf16[128,256]{1,0:T(8,128)(2,1)S(1)}, bf16[80,256]{1,0:T(8,128)(2,1)S(1)}, bf16[128,256]{1,0:T(8,128)(2,1)S(1)}) custom-call(f32[2,64,256]{2,1,0:T(8,128)} %amps.1, bf16[1,256,256]{2,1,0:T(8,128)(2,1)} %block.1, f32[2,64,256]{2,1,0:T(8,128)} %resid.3, f32[2,256]{1,0:T(2,128)} %virt.1, f32[2]{0:T(128)} %pair.1, ...), custom_call_target="tpu_custom_call" | custom-call | tf_op jit(solution)/shard_map/prepare/pallas_call | solution.py:314
  1.4 3.0 %collective-permute-start.7 = (bf16[144,256]{1,0:T(8,128)(2,1)S(1)}, bf16[144,256]{1,0:T(8,128)(2,1)S(1)}, u32[]{:S(2)}, u32[]{:S(2)}) collective-permute-start(bf16[144,256]{1,0:T(8,128)(2,1)S(1)} %get-tuple-element.23.own), channel_id=1, source_target_pairs={{0,2},{1,3},{2,0},{3,1},{4,6},{5,7},{6,4},{7,5},{8,10},{9,11},{10,... | collective-permute-start | bytes 221192 | tf_op jit(solution)/shard_map/ppermute | solution.py:31
  4.4 2.6 %collective-permute-start.2 = (bf16[144,256]{1,0:T(8,128)(2,1)S(1)}, bf16[144,256]{1,0:T(8,128)(2,1)S(1)}, u32[]{:S(2)}, u32[]{:S(2)}) collective-permute-start(bf16[144,256]{1,0:T(8,128)(2,1)S(1)} %get-tuple-element.23.own), channel_id=1, source_target_pairs={{0,16},{1,17},{2,18},{3,19},{4,20},{5,21},{6,22},{7,23},{8,24},{9,... | collective-permute-start | bytes 221192 | tf_op jit(solution)/shard_map/ppermute | solution.py:31
  7.0 2.5 %collective-permute-start.12 = (bf16[128,256]{1,0:T(8,128)(2,1)S(1)}, bf16[128,256]{1,0:T(8,128)(2,1)S(1)}, u32[]{:S(2)}, u32[]{:S(2)}) collective-permute-start(bf16[128,256]{1,0:T(8,128)(2,1)S(1)} %get-tuple-element.22.half_own), channel_id=1, source_target_pairs={{0,12},{1,29},{2,14},{3,31},{4,8},{5,25},{6,10},{7,27},{8,4},{9,21... | collective-permute-start | bytes 196616 | tf_op jit(solution)/shard_map/ppermute | solution.py:40
  9.5 0.4 %collective-permute-start.11 = (bf16[128,256]{1,0:T(8,128)(2,1)S(1)}, bf16[128,256]{1,0:T(8,128)(2,1)S(1)}, u32[]{:S(2)}, u32[]{:S(2)}) collective-permute-start(bf16[128,256]{1,0:T(8,128)(2,1)S(1)} %get-tuple-element.22.half_own), channel_id=1, source_target_pairs={{0,8},{1,25},{2,10},{3,27},{4,12},{5,29},{6,14},{7,31},{8,0},{9,17... | collective-permute-start | bytes 196616 | tf_op jit(solution)/shard_map/ppermute | solution.py:40
  10.0 0.3 collective-permute-start.4
  10.3 0.5 %collective-permute-done.2.far = bf16[144,256]{1,0:T(8,128)(2,1)S(1)} collective-permute-done((bf16[144,256]{1,0:T(8,128)(2,1)S(1)}, bf16[144,256]{1,0:T(8,128)(2,1)S(1)}, u32[]{:S(2)}, u32[]{:S(2)}) %collective-permute-start.2) | collective-permute-done | bytes 73760 | tf_op jit(solution)/shard_map/ppermute | solution.py:31
  10.9 0.5 %collective-permute-start.9 = (bf16[144,256]{1,0:T(8,128)(2,1)S(1)}, bf16[144,256]{1,0:T(8,128)(2,1)S(1)}, u32[]{:S(2)}, u32[]{:S(2)}) collective-permute-start(bf16[144,256]{1,0:T(8,128)(2,1)S(1)} %collective-permute-done.2.far), channel_id=1, source_target_pairs={{0,2},{1,3},{2,0},{3,1},{4,6},{5,7},{6,4},{7,5},{8,10},{9,11},{10,... | collective-permute-start | bytes 221192 | tf_op jit(solution)/shard_map/ppermute | solution.py:31
  11.4 2.1 %collective-permute-start = (bf16[128,256]{1,0:T(8,128)(2,1)S(1)}, bf16[128,256]{1,0:T(8,128)(2,1)S(1)}, u32[]{:S(2)}, u32[]{:S(2)}) collective-permute-start(bf16[128,256]{1,0:T(8,128)(2,1)S(1)} %get-tuple-element.22.half_own), channel_id=1, source_target_pairs={{0,4},{1,21},{2,6},{3,23},{4,0},{5,17},{6,2},{7,19},{8,12},{9,29},... | collective-permute-start | bytes 196616 | tf_op jit(solution)/shard_map/ppermute | solution.py:40
  13.5 1.0 %collective-permute-done.11.refs_5_ = bf16[128,256]{1,0:T(8,128)(2,1)S(1)} collective-permute-done((bf16[128,256]{1,0:T(8,128)(2,1)S(1)}, bf16[128,256]{1,0:T(8,128)(2,1)S(1)}, u32[]{:S(2)}, u32[]{:S(2)}) %collective-permute-start.11) | collective-permute-done | bytes 65568 | tf_op jit(solution)/shard_map/ppermute | solution.py:40
  14.5 0.9 %collective-permute-done.4.far.far_tail = bf16[80,256]{1,0:T(8,128)(2,1)S(1)} collective-permute-done((bf16[80,256]{1,0:T(8,128)(2,1)S(1)}, bf16[80,256]{1,0:T(8,128)(2,1)S(1)}, u32[]{:S(2)}, u32[]{:S(2)}) %collective-permute-start.4) | collective-permute-done | bytes 40992 | tf_op jit(solution)/shard_map/ppermute | solution.py:31
  15.4 0.3 collective-permute-done.refs_4_
  15.7 1.1 %collective-permute-start.1 = (bf16[144,256]{1,0:T(8,128)(2,1)S(1)}, bf16[144,256]{1,0:T(8,128)(2,1)S(1)}, u32[]{:S(2)}, u32[]{:S(2)}) collective-permute-start(bf16[144,256]{1,0:T(8,128)(2,1)S(1)} %get-tuple-element.23.own), channel_id=1, source_target_pairs={{0,1},{1,0},{2,3},{3,2},{4,5},{5,4},{6,7},{7,6},{8,9},{9,8},{10,11... | collective-permute-start | bytes 221192 | tf_op jit(solution)/shard_map/ppermute | solution.py:31
  16.9 0.5 %collective-permute-start.3 = (bf16[144,256]{1,0:T(8,128)(2,1)S(1)}, bf16[144,256]{1,0:T(8,128)(2,1)S(1)}, u32[]{:S(2)}, u32[]{:S(2)}) collective-permute-start(bf16[144,256]{1,0:T(8,128)(2,1)S(1)} %collective-permute-done.2.far), channel_id=1, source_target_pairs={{0,1},{1,0},{2,3},{3,2},{4,5},{5,4},{6,7},{7,6},{8,9},{9,8},{10,11... | collective-permute-start | bytes 221192 | tf_op jit(solution)/shard_map/ppermute | solution.py:31
  17.5 0.4 %collective-permute-start.13 = (bf16[128,256]{1,0:T(8,128)(2,1)S(1)}, bf16[128,256]{1,0:T(8,128)(2,1)S(1)}, u32[]{:S(2)}, u32[]{:S(2)}) collective-permute-start(bf16[128,256]{1,0:T(8,128)(2,1)S(1)} %collective-permute-done.refs_4_), channel_id=1, source_target_pairs={{0,1},{1,0},{2,3},{3,2},{4,5},{5,4},{6,7},{7,6},{8,9},{9,8},{10,11... | collective-permute-start | bytes 196616 | tf_op jit(solution)/shard_map/ppermute | solution.py:31
  17.9 0.9 %collective-permute-done.13.refs_7_ = bf16[128,256]{1,0:T(8,128)(2,1)S(1)} collective-permute-done((bf16[128,256]{1,0:T(8,128)(2,1)S(1)}, bf16[128,256]{1,0:T(8,128)(2,1)S(1)}, u32[]{:S(2)}, u32[]{:S(2)}) %collective-permute-start.13) | collective-permute-done | bytes 65568 | tf_op jit(solution)/shard_map/ppermute | solution.py:31
  18.8 1.0 %intermediate.1.refs_0_ = bf16[256,256]{1,0:T(8,128)(2,1)S(1)} custom-call(bf16[144,256]{1,0:T(8,128)(2,1)S(1)} %get-tuple-element.23.own, bf16[144,256]{1,0:T(8,128)(2,1)S(1)} %collective-permute-done.1.own_c, bf16[144,256]{1,0:T(8,128)(2,1)S(1)} %collective-permute-done.2.far, bf16[144,256]{1,0:T(8,128)(2,1)S(1)} %collective-permute-done.3.far_c, ...), custom_call_target="tpu_custom_call" | custom-call | tf_op jit(solution)/shard_map/intermediate/pallas_call | solution.py:352
  19.9 2.4 %collective-permute-start.18 = (bf16[256,256]{1,0:T(8,128)(2,1)S(1)}, bf16[256,256]{1,0:T(8,128)(2,1)S(1)}, u32[]{:S(2)}, u32[]{:S(2)}) collective-permute-start(bf16[256,256]{1,0:T(8,128)(2,1)S(1)} %intermediate.1.refs_0_), channel_id=1, source_target_pairs={{0,12},{1,13},{2,14},{3,15},{4,8},{5,9},{6,10},{7,11},{8,4},{9,5},... | collective-permute-start | bytes 393224 | tf_op jit(solution)/shard_map/ppermute | solution.py:31
  22.3 0.6 %collective-permute-start.17 = (bf16[256,256]{1,0:T(8,128)(2,1)S(1)}, bf16[256,256]{1,0:T(8,128)(2,1)S(1)}, u32[]{:S(2)}, u32[]{:S(2)}) collective-permute-start(bf16[256,256]{1,0:T(8,128)(2,1)S(1)} %intermediate.1.refs_0_), channel_id=1, source_target_pairs={{0,8},{1,9},{2,10},{3,11},{4,12},{5,13},{6,14},{7,15},{8,0},{9,1},... | collective-permute-start | bytes 393224 | tf_op jit(solution)/shard_map/ppermute | solution.py:31
  22.9 0.5 %collective-permute-start.16 = (bf16[256,256]{1,0:T(8,128)(2,1)S(1)}, bf16[256,256]{1,0:T(8,128)(2,1)S(1)}, u32[]{:S(2)}, u32[]{:S(2)}) collective-permute-start(bf16[256,256]{1,0:T(8,128)(2,1)S(1)} %intermediate.1.refs_0_), channel_id=1, source_target_pairs={{0,4},{1,5},{2,6},{3,7},{4,0},{5,1},{6,2},{7,3},{8,12},{9,13},{10,... | collective-permute-start | bytes 393224 | tf_op jit(solution)/shard_map/ppermute | solution.py:31
  23.4 3.5 %collective-permute-start.5 = (bf16[128,256]{1,0:T(8,128)(2,1)S(1)}, bf16[128,256]{1,0:T(8,128)(2,1)S(1)}, u32[]{:S(2)}, u32[]{:S(2)}) collective-permute-start(bf16[128,256]{1,0:T(8,128)(2,1)S(1)} %get-tuple-element.25), channel_id=1, source_target_pairs={{0,16},{1,17},{2,18},{3,19},{4,20},{5,21},{6,22},{7,23},{8,24},{9,... | collective-permute-start | bytes 196616 | tf_op jit(solution)/shard_map/ppermute | solution.py:31
  27.0 0.9 %near_factors.1 = (f32[2,256,256]{2,1,0:T(8,128)S(1)}, f32[2,64,256]{2,1,0:T(8,128)S(1)}) custom-call(f32[2,64,256]{2,1,0:T(8,128)} %resid.3, bf16[80,256]{1,0:T(8,128)(2,1)S(1)} %get-tuple-element.24.own.tail), custom_call_target="tpu_custom_call" | custom-call | flops 1000000000 | tf_op jit(solution)/shard_map/near_factors/pallas_call | solution.py:327
  27.9 1.5 %factors.1 = (bf16[1024,1024]{1,0:T(8,128)(2,1)S(1)}, f32[2,256,256]{2,1,0:T(8,128)S(1)}, s32[2,8,128]{2,1,0:T(8,128)S(1)}) custom-call(bf16[80,256]{1,0:T(8,128)(2,1)S(1)} %get-tuple-element.24.own.tail, bf16[80,256]{1,0:T(8,128)(2,1)S(1)} %collective-permute-done.4.far.far_tail, s32[2]{0:T(128)} %swap.1), custom_call_target="tpu_custom_call" | custom-call | tf_op jit(solution)/shard_map/factors/pallas_call | solution.py:366
  29.4 0.2 collective-permute-done.5.resid_far
  29.5 1.3 %collective-permute-done.17.refs_2_ = bf16[256,256]{1,0:T(8,128)(2,1)S(1)} collective-permute-done((bf16[256,256]{1,0:T(8,128)(2,1)S(1)}, bf16[256,256]{1,0:T(8,128)(2,1)S(1)}, u32[]{:S(2)}, u32[]{:S(2)}) %collective-permute-start.17) | collective-permute-done | bytes 131104 | tf_op jit(solution)/shard_map/ppermute | solution.py:31
  30.9 1.4 %cycle.1 = (f32[2,64,256]{2,1,0:T(8,128)S(1)}, bf16[2,64,256]{2,1,0:T(8,128)(2,1)S(1)}, bf16[2,64,256]{2,1,0:T(8,128)(2,1)S(1)}, bf16[2,64,256]{2,1,0:T(8,128)(2,1)S(1)}) custom-call(bf16[144,256]{1,0:T(8,128)(2,1)S(1)} %get-tuple-element.23.own, bf16[144,256]{1,0:T(8,128)(2,1)S(1)} %collective-permute-done.1.own_c, ...), custom_call_target="tpu_custom_call" | custom-call | tf_op jit(solution)/shard_map/cycle/pallas_call | solution.py:377
  32.2 0.1 collective-permute-start.19
  32.3 1.1 %collective-permute-start.20 = (bf16[2,64,256]{2,1,0:T(8,128)(2,1)S(1)}, bf16[2,64,256]{2,1,0:T(8,128)(2,1)S(1)}, u32[]{:S(2)}, u32[]{:S(2)}) collective-permute-start(bf16[2,64,256]{2,1,0:T(8,128)(2,1)S(1)} %get-tuple-element.35), channel_id=1, source_target_pairs={{0,2},{1,3},{2,0},{3,1},{4,6},{5,7},{6,4},{7,5},{8,10},{9,11},{10,... | collective-permute-start | bytes 196616 | tf_op jit(solution)/shard_map/ppermute | solution.py:31
  33.4 0.8 %collective-permute-start.21 = (bf16[2,64,256]{2,1,0:T(8,128)(2,1)S(1)}, bf16[2,64,256]{2,1,0:T(8,128)(2,1)S(1)}, u32[]{:S(2)}, u32[]{:S(2)}) collective-permute-start(bf16[2,64,256]{2,1,0:T(8,128)(2,1)S(1)} %get-tuple-element.36), channel_id=1, source_target_pairs={{0,3},{1,2},{2,1},{3,0},{4,7},{5,6},{6,5},{7,4},{8,11},{9,10},{10,... | collective-permute-start | bytes 196616 | tf_op jit(solution)/shard_map/ppermute | solution.py:31
  34.2 3.1 %collective-permute-done.20 = bf16[2,64,256]{2,1,0:T(8,128)(2,1)S(1)} collective-permute-done((bf16[2,64,256]{2,1,0:T(8,128)(2,1)S(1)}, bf16[2,64,256]{2,1,0:T(8,128)(2,1)S(1)}, u32[]{:S(2)}, u32[]{:S(2)}) %collective-permute-start.20) | collective-permute-done | bytes 65568 | tf_op jit(solution)/shard_map/ppermute | solution.py:31
  37.3 0.5 %collective-permute-done.21 = bf16[2,64,256]{2,1,0:T(8,128)(2,1)S(1)} collective-permute-done((bf16[2,64,256]{2,1,0:T(8,128)(2,1)S(1)}, bf16[2,64,256]{2,1,0:T(8,128)(2,1)S(1)}, u32[]{:S(2)}, u32[]{:S(2)}) %collective-permute-start.21) | collective-permute-done | bytes 65568 | tf_op jit(solution)/shard_map/ppermute | solution.py:31
  37.8 0.7 %add_multiply_fusion = f32[2,64,256]{2,1,0:T(8,128)} fusion(bf16[2,64,256]{2,1,0:T(8,128)(2,1)S(1)} %collective-permute-done.21, bf16[2,64,256]{2,1,0:T(8,128)(2,1)S(1)} %collective-permute-done.20, f32[2,64,256]{2,1,0:T(8,128)S(1)} %get-tuple-element.33, bf16[2,64,256]{2,1,0:T(8,128)(2,1)S(1)} %collective-permute-done.19), kind=kLoop, calls=%fused_computation | loop fusion | flops 229376 | bytes 458752 | tf_op jit(solution)/shard_map/mul | solution.py:386
  (18 shorter events, 0.1 us)
Async XLA Ops:
  1.4 8.9 %collective-permute-start.7 = (bf16[144,256]{1,0:T(8,128)(2,1)S(1)}, bf16[144,256]{1,0:T(8,128)(2,1)S(1)}, u32[]{:S(2)}, u32[]{:S(2)}) collective-permute-start(bf16[144,256]{1,0:T(8,128)(2,1)S(1)} %get-tuple-element.23.own), channel_id=1, source_target_pairs={{0,2},{1,3},{2,0},{3,1},{4,6},{5,7},{6,4},{7,5},{8,10},{9,11},{10,... | collective-permute-start | bytes 221192 | tf_op jit(solution)/shard_map/ppermute | solution.py:31
  4.4 6.4 %collective-permute-start.2 = (bf16[144,256]{1,0:T(8,128)(2,1)S(1)}, bf16[144,256]{1,0:T(8,128)(2,1)S(1)}, u32[]{:S(2)}, u32[]{:S(2)}) collective-permute-start(bf16[144,256]{1,0:T(8,128)(2,1)S(1)} %get-tuple-element.23.own), channel_id=1, source_target_pairs={{0,16},{1,17},{2,18},{3,19},{4,20},{5,21},{6,22},{7,23},{8,24},{9,... | collective-permute-start | bytes 221192 | tf_op jit(solution)/shard_map/ppermute | solution.py:31
  7.0 6.5 %collective-permute-start.12 = (bf16[128,256]{1,0:T(8,128)(2,1)S(1)}, bf16[128,256]{1,0:T(8,128)(2,1)S(1)}, u32[]{:S(2)}, u32[]{:S(2)}) collective-permute-start(bf16[128,256]{1,0:T(8,128)(2,1)S(1)} %get-tuple-element.22.half_own), channel_id=1, source_target_pairs={{0,12},{1,29},{2,14},{3,31},{4,8},{5,25},{6,10},{7,27},{8,4},{9,21... | collective-permute-start | bytes 196616 | tf_op jit(solution)/shard_map/ppermute | solution.py:40
  9.5 5.0 %collective-permute-start.11 = (bf16[128,256]{1,0:T(8,128)(2,1)S(1)}, bf16[128,256]{1,0:T(8,128)(2,1)S(1)}, u32[]{:S(2)}, u32[]{:S(2)}) collective-permute-start(bf16[128,256]{1,0:T(8,128)(2,1)S(1)} %get-tuple-element.22.half_own), channel_id=1, source_target_pairs={{0,8},{1,25},{2,10},{3,27},{4,12},{5,29},{6,14},{7,31},{8,0},{9,17... | collective-permute-start | bytes 196616 | tf_op jit(solution)/shard_map/ppermute | solution.py:40
  10.0 5.4 %collective-permute-start.4 = (bf16[80,256]{1,0:T(8,128)(2,1)S(1)}, bf16[80,256]{1,0:T(8,128)(2,1)S(1)}, u32[]{:S(2)}, u32[]{:S(2)}) collective-permute-start(bf16[80,256]{1,0:T(8,128)(2,1)S(1)} %get-tuple-element.24.own.tail), channel_id=1, source_target_pairs={{0,16},{1,17},{2,18},{3,19},{4,20},{5,21},{6,22},{7,23},{8,24},{9,... | collective-permute-start | bytes 122888 | tf_op jit(solution)/shard_map/ppermute | solution.py:31
  10.9 6.5 %collective-permute-start.9 = (bf16[144,256]{1,0:T(8,128)(2,1)S(1)}, bf16[144,256]{1,0:T(8,128)(2,1)S(1)}, u32[]{:S(2)}, u32[]{:S(2)}) collective-permute-start(bf16[144,256]{1,0:T(8,128)(2,1)S(1)} %collective-permute-done.2.far), channel_id=1, source_target_pairs={{0,2},{1,3},{2,0},{3,1},{4,6},{5,7},{6,4},{7,5},{8,10},{9,11},{10,... | collective-permute-start | bytes 221192 | tf_op jit(solution)/shard_map/ppermute | solution.py:31
  11.4 4.4 %collective-permute-start = (bf16[128,256]{1,0:T(8,128)(2,1)S(1)}, bf16[128,256]{1,0:T(8,128)(2,1)S(1)}, u32[]{:S(2)}, u32[]{:S(2)}) collective-permute-start(bf16[128,256]{1,0:T(8,128)(2,1)S(1)} %get-tuple-element.22.half_own), channel_id=1, source_target_pairs={{0,4},{1,21},{2,6},{3,23},{4,0},{5,17},{6,2},{7,19},{8,12},{9,29},... | collective-permute-start | bytes 196616 | tf_op jit(solution)/shard_map/ppermute | solution.py:40
  13.5 3.4 %collective-permute-start.15 = (bf16[128,256]{1,0:T(8,128)(2,1)S(1)}, bf16[128,256]{1,0:T(8,128)(2,1)S(1)}, u32[]{:S(2)}, u32[]{:S(2)}) collective-permute-start(bf16[128,256]{1,0:T(8,128)(2,1)S(1)} %collective-permute-done.12.refs_6_), channel_id=1, source_target_pairs={{0,1},{1,0},{2,3},{3,2},{4,5},{5,4},{6,7},{7,6},{8,9},{9,8},{10,11... | collective-permute-start | bytes 196616 | tf_op jit(solution)/shard_map/ppermute | solution.py:31
  14.5 3.0 %collective-permute-start.14 = (bf16[128,256]{1,0:T(8,128)(2,1)S(1)}, bf16[128,256]{1,0:T(8,128)(2,1)S(1)}, u32[]{:S(2)}, u32[]{:S(2)}) collective-permute-start(bf16[128,256]{1,0:T(8,128)(2,1)S(1)} %collective-permute-done.11.refs_5_), channel_id=1, source_target_pairs={{0,1},{1,0},{2,3},{3,2},{4,5},{5,4},{6,7},{7,6},{8,9},{9,8},{10,11... | collective-permute-start | bytes 196616 | tf_op jit(solution)/shard_map/ppermute | solution.py:31
  15.4 1.5 %collective-permute-start.6 = (bf16[80,256]{1,0:T(8,128)(2,1)S(1)}, bf16[80,256]{1,0:T(8,128)(2,1)S(1)}, u32[]{:S(2)}, u32[]{:S(2)}) collective-permute-start(bf16[80,256]{1,0:T(8,128)(2,1)S(1)} %collective-permute-done.4.far.far_tail), channel_id=1, source_target_pairs={{0,1},{1,0},{2,3},{3,2},{4,5},{5,4},{6,7},{7,6},{8,9},{9,8},{10,11... | collective-permute-start | bytes 122888 | tf_op jit(solution)/shard_map/ppermute | solution.py:31
  15.7 3.1 %collective-permute-start.1 = (bf16[144,256]{1,0:T(8,128)(2,1)S(1)}, bf16[144,256]{1,0:T(8,128)(2,1)S(1)}, u32[]{:S(2)}, u32[]{:S(2)}) collective-permute-start(bf16[144,256]{1,0:T(8,128)(2,1)S(1)} %get-tuple-element.23.own), channel_id=1, source_target_pairs={{0,1},{1,0},{2,3},{3,2},{4,5},{5,4},{6,7},{7,6},{8,9},{9,8},{10,11... | collective-permute-start | bytes 221192 | tf_op jit(solution)/shard_map/ppermute | solution.py:31
  16.9 1.9 %collective-permute-start.8 = (bf16[144,256]{1,0:T(8,128)(2,1)S(1)}, bf16[144,256]{1,0:T(8,128)(2,1)S(1)}, u32[]{:S(2)}, u32[]{:S(2)}) collective-permute-start(bf16[144,256]{1,0:T(8,128)(2,1)S(1)} %collective-permute-done.7.refs_0_), channel_id=1, source_target_pairs={{0,1},{1,0},{2,3},{3,2},{4,5},{5,4},{6,7},{7,6},{8,9},{9,8},{10,11... | collective-permute-start | bytes 221192 | tf_op jit(solution)/shard_map/ppermute | solution.py:31
  16.9 1.9 %collective-permute-start.3 = (bf16[144,256]{1,0:T(8,128)(2,1)S(1)}, bf16[144,256]{1,0:T(8,128)(2,1)S(1)}, u32[]{:S(2)}, u32[]{:S(2)}) collective-permute-start(bf16[144,256]{1,0:T(8,128)(2,1)S(1)} %collective-permute-done.2.far), channel_id=1, source_target_pairs={{0,1},{1,0},{2,3},{3,2},{4,5},{5,4},{6,7},{7,6},{8,9},{9,8},{10,11... | collective-permute-start | bytes 221192 | tf_op jit(solution)/shard_map/ppermute | solution.py:31
  17.4 1.4 %collective-permute-start.10 = (bf16[144,256]{1,0:T(8,128)(2,1)S(1)}, bf16[144,256]{1,0:T(8,128)(2,1)S(1)}, u32[]{:S(2)}, u32[]{:S(2)}) collective-permute-start(bf16[144,256]{1,0:T(8,128)(2,1)S(1)} %collective-permute-done.9.refs_2_), channel_id=1, source_target_pairs={{0,1},{1,0},{2,3},{3,2},{4,5},{5,4},{6,7},{7,6},{8,9},{9,8},{10,11... | collective-permute-start | bytes 221192 | tf_op jit(solution)/shard_map/ppermute | solution.py:31
  17.5 1.3 %collective-permute-start.13 = (bf16[128,256]{1,0:T(8,128)(2,1)S(1)}, bf16[128,256]{1,0:T(8,128)(2,1)S(1)}, u32[]{:S(2)}, u32[]{:S(2)}) collective-permute-start(bf16[128,256]{1,0:T(8,128)(2,1)S(1)} %collective-permute-done.refs_4_), channel_id=1, source_target_pairs={{0,1},{1,0},{2,3},{3,2},{4,5},{5,4},{6,7},{7,6},{8,9},{9,8},{10,11... | collective-permute-start | bytes 196616 | tf_op jit(solution)/shard_map/ppermute | solution.py:31
  19.9 9.7 %collective-permute-start.18 = (bf16[256,256]{1,0:T(8,128)(2,1)S(1)}, bf16[256,256]{1,0:T(8,128)(2,1)S(1)}, u32[]{:S(2)}, u32[]{:S(2)}) collective-permute-start(bf16[256,256]{1,0:T(8,128)(2,1)S(1)} %intermediate.1.refs_0_), channel_id=1, source_target_pairs={{0,12},{1,13},{2,14},{3,15},{4,8},{5,9},{6,10},{7,11},{8,4},{9,5},... | collective-permute-start | bytes 393224 | tf_op jit(solution)/shard_map/ppermute | solution.py:31
  22.3 8.6 %collective-permute-start.17 = (bf16[256,256]{1,0:T(8,128)(2,1)S(1)}, bf16[256,256]{1,0:T(8,128)(2,1)S(1)}, u32[]{:S(2)}, u32[]{:S(2)}) collective-permute-start(bf16[256,256]{1,0:T(8,128)(2,1)S(1)} %intermediate.1.refs_0_), channel_id=1, source_target_pairs={{0,8},{1,9},{2,10},{3,11},{4,12},{5,13},{6,14},{7,15},{8,0},{9,1},... | collective-permute-start | bytes 393224 | tf_op jit(solution)/shard_map/ppermute | solution.py:31
  22.9 8.0 %collective-permute-start.16 = (bf16[256,256]{1,0:T(8,128)(2,1)S(1)}, bf16[256,256]{1,0:T(8,128)(2,1)S(1)}, u32[]{:S(2)}, u32[]{:S(2)}) collective-permute-start(bf16[256,256]{1,0:T(8,128)(2,1)S(1)} %intermediate.1.refs_0_), channel_id=1, source_target_pairs={{0,4},{1,5},{2,6},{3,7},{4,0},{5,1},{6,2},{7,3},{8,12},{9,13},{10,... | collective-permute-start | bytes 393224 | tf_op jit(solution)/shard_map/ppermute | solution.py:31
  23.4 6.1 %collective-permute-start.5 = (bf16[128,256]{1,0:T(8,128)(2,1)S(1)}, bf16[128,256]{1,0:T(8,128)(2,1)S(1)}, u32[]{:S(2)}, u32[]{:S(2)}) collective-permute-start(bf16[128,256]{1,0:T(8,128)(2,1)S(1)} %get-tuple-element.25), channel_id=1, source_target_pairs={{0,16},{1,17},{2,18},{3,19},{4,20},{5,21},{6,22},{7,23},{8,24},{9,... | collective-permute-start | bytes 196616 | tf_op jit(solution)/shard_map/ppermute | solution.py:31
  32.2 1.9 %collective-permute-start.19 = (bf16[2,64,256]{2,1,0:T(8,128)(2,1)S(1)}, bf16[2,64,256]{2,1,0:T(8,128)(2,1)S(1)}, u32[]{:S(2)}, u32[]{:S(2)}) collective-permute-start(bf16[2,64,256]{2,1,0:T(8,128)(2,1)S(1)} %get-tuple-element.34), channel_id=1, source_target_pairs={{0,1},{1,0},{2,3},{3,2},{4,5},{5,4},{6,7},{7,6},{8,9},{9,8},{10,11... | collective-permute-start | bytes 196616 | tf_op jit(solution)/shard_map/ppermute | solution.py:31
  32.3 4.9 %collective-permute-start.20 = (bf16[2,64,256]{2,1,0:T(8,128)(2,1)S(1)}, bf16[2,64,256]{2,1,0:T(8,128)(2,1)S(1)}, u32[]{:S(2)}, u32[]{:S(2)}) collective-permute-start(bf16[2,64,256]{2,1,0:T(8,128)(2,1)S(1)} %get-tuple-element.35), channel_id=1, source_target_pairs={{0,2},{1,3},{2,0},{3,1},{4,6},{5,7},{6,4},{7,5},{8,10},{9,11},{10,... | collective-permute-start | bytes 196616 | tf_op jit(solution)/shard_map/ppermute | solution.py:31
  33.4 4.4 %collective-permute-start.21 = (bf16[2,64,256]{2,1,0:T(8,128)(2,1)S(1)}, bf16[2,64,256]{2,1,0:T(8,128)(2,1)S(1)}, u32[]{:S(2)}, u32[]{:S(2)}) collective-permute-start(bf16[2,64,256]{2,1,0:T(8,128)(2,1)S(1)} %get-tuple-element.36), channel_id=1, source_target_pairs={{0,3},{1,2},{2,1},{3,0},{4,7},{5,6},{6,5},{7,4},{8,11},{9,10},{10,... | collective-permute-start | bytes 196616 | tf_op jit(solution)/shard_map/ppermute | solution.py:31

commit v4 on v3

--- a/solution.py
+++ b/solution.py
@@ -102,46 +102,64 @@
     return jnp.where(core == 0, own, other), jnp.where(core == 0, other, own)
 
 
-def intermediate(n_shared, items, pairs, own, own_c, far, far_c, far_tail, far_tail_c, half_own, *refs):
-    y_refs, rest, out = refs[: 4 * n_shared], refs[4 * n_shared : -1], refs[-1]
+def partials(n_shared, items, pairs, own, far, far_tail, far_tail_c, half_own, *refs):
+    y_refs, rest, (keep_out, give_out) = refs[: 2 * n_shared], refs[2 * n_shared : -2], refs[-2:]
     half_rows, domain = half_own.shape
     height = half_rows // 2
     rows = pairs * height
     group, _, core, family, half = place()
-
-    near = [own, own_c] + list(y_refs[: 2 * n_shared])
-    away = [far, far_c] + list(y_refs[2 * n_shared :])
-    lean = rows + TILE
-    pieces = [jnp.where(core == 0, a[:lean, :], b[:lean, :]) for a, b in zip(near, away)]
-    x = [jnp.concatenate([piece[p * height : (p + 1) * height] for piece in pieces], axis=0) for p in range(pairs)]
+    near = [own] + list(y_refs[:n_shared])
+    away = [far] + list(y_refs[n_shared:])
+    x = [
+        jnp.concatenate([piece[p * height : (p + 1) * height, :] for piece in side], axis=0)
+        for side in (near, away)
+        for p in range(pairs)
+    ]
     x_all = jnp.concatenate(x, axis=0)
+    deep = len(near) * height
     spread = (iota((rows, domain), 0) * items // rows == iota((rows, domain), 1)).astype(BF16)
-    named = [dot(spread, jnp.broadcast_to(piece[rows : rows + 1], (half_rows, domain)), NT) for piece in pieces]
+
+    def names(piece):
+        return dot(spread, jnp.broadcast_to(piece[rows : rows + TILE, :][:1], (half_rows, domain)), NT)
+
+    named = [[names(piece) for piece in side] for side in (near, away)]
     ids = jnp.concatenate(
-        [name[p * height : (p + 1) * height] for p in range(pairs) for name in named], axis=0
+        [name[p * height : (p + 1) * height] for side in named for p in range(pairs) for name in side], axis=0
     ).astype(jnp.int32)
 
     def chosen(block, index):
         return jnp.where(ids == index, dot(x_all, block, NT), 0.0)
 
+    def chosen_two(sofar, one, two, index, other):
+        both = dot(x_all, jnp.concatenate([one, two], axis=0), NT)
+        sofar = jnp.where(ids == index, both[:, :half_rows], sofar)
+        return jnp.where(ids == other, both[:, half_rows:], sofar)
+
     if len(rest) > 1:
         count = len(rest) // 2
-        product = chosen(half_own[...], group)
-        product += chosen(jnp.concatenate(ordered(core, far_tail[TILE:, :], far_tail_c[TILE:, :]), axis=0), group ^ half)
+        mirror = jnp.concatenate(ordered(core, far_tail[TILE:, :], far_tail_c[TILE:, :]), axis=0)
+        product = chosen_two(jnp.zeros(ids.shape, F32), half_own[...], mirror, group, group ^ half)
         for j in range(count):
-            product += chosen(rest[j][...], family ^ (j + 1))
-            product += chosen(rest[count + j][...], family ^ half ^ (j + 1))
+            product = chosen_two(product, rest[j][...], rest[count + j][...], family ^ (j + 1), family ^ half ^ (j + 1))
     else:
         product = lax.fori_loop(
             0,
             rest[0].shape[0],
             lambda k, sofar: sofar + chosen(rest[0][k], k),
-            jnp.zeros((pairs * domain, half_rows), F32),
+            jnp.zeros(ids.shape, F32),
         )
     product = product.astype(BF16)
     for p in range(pairs):
-        both = dot(product[p * domain : (p + 1) * domain], x[p], TN)
-        out[p * half_rows : (p + 1) * half_rows, :] = both.astype(BF16)
+        both = [
+            dot(product[k * deep : (k + 1) * deep], x[k], TN).astype(BF16) for k in (p, pairs + p)
+        ]
+        keep_out[p * half_rows : (p + 1) * half_rows, :], give_out[p * half_rows : (p + 1) * half_rows, :] = ordered(
+            core, *both
+        )
+
+
+def joined(keep, given, out):
+    out[...] = (keep[...].astype(F32) + given[...].astype(F32)).astype(BF16)
 
 
 def spread_counts(own, far, swaps, half_rows, lanes):
@@ -192,12 +210,14 @@
     base_out[...] = held[...] * inverse_out[:, pl.ds(start, height), :]
 
 
-def factors(n_units, pairs, own, far, swap, weights_out, inverse_out, swap_out, held, sem):
+def factors(n_units, pairs, own, far, resid_far, swap, weights_out, inverse_out, bias_out, swap_out, held, sem):
     copy = pltpu.make_async_copy(swap, held, sem)
     copy.start()
     half_rows = weights_out.shape[0] // (2 * pairs * pairs)
     wide = pairs * half_rows
     group, _, _, family, half = place()
+    height, domain = resid_far.shape[0] // pairs, resid_far.shape[1]
+    spot = (iota((height, domain), 1) == iota((height, domain), 0) + lax.axis_index("ints") * height).astype(BF16)
     away = energies(far, pairs)
     away = [inverse_of(*away, p, pairs) for p in range(pairs)]
     copy.wait()
@@ -209,11 +229,16 @@
         inverse_out[p] = functools.reduce(
             lambda kept, k: jnp.where(swaps[p] == k, away[k], kept), range(1, pairs), away[0]
         )
+        parts = [resid_far[k * height : (k + 1) * height, :] for k in range(pairs)]
+        part = functools.reduce(
+            lambda kept, k: jnp.where(swaps[p] == k, parts[k], kept), range(1, pairs), parts[0]
+        )
+        bias_out[p] = dot(part, spot, TN) * inverse_out[p]
         swap_out[p] = jnp.full(swap_out.shape[1:], swaps[p], jnp.int32)
 
 
-def cycle(n_sends, pairs, own, own_c, far, far_c, tail, far_tail, resid_far, mix, inverse, inverse_far, base, swap, *refs):
-    units, (own_out, *sends), (here, there) = refs[: -n_sends - 3], refs[-n_sends - 3 : -2], refs[-2:]
+def cycle(n_sends, pairs, own, own_c, far, far_c, tail, far_tail, mix, inverse, inverse_far, bias, base, swap, *refs):
+    units, (own_out, *sends), here = refs[: -n_sends - 2], refs[-n_sends - 2 : -1], refs[-1]
     height, domain = base.shape[1:]
     rows = pairs * height
     half_rows = 2 * height
@@ -244,13 +269,7 @@
     near, away = amps_of(own, own_c), amps_of(far, far_c)
     for p in range(pairs):
         at = (pairs + p) * wide
-        there[...] = dot(mixed[at : at + wide], away, TN)
-        parts = [resid_far[k * height : (k + 1) * height, :].astype(F32) for k in range(pairs)]
-        named = swap[p, :1, :1]
-        there[start, :] += functools.reduce(
-            lambda kept, k: jnp.where(named == k, parts[k], kept), range(1, pairs), parts[0]
-        )
-        mirror = (there[...] * inverse_far[p]).T
+        mirror = dot(away, mixed[at : at + wide], TN) * inverse_far[p] + bias[p]
         at = p * wide
         here[p] = dot(mixed[at : at + wide], near, TN) * inverse[p] + mirror
     own_out[...] = here[:, start, :] + base[...]
@@ -340,21 +359,19 @@
     y_own = [exchange(lean, 0, k) for k in range(2, n_ints, 2)]
     blocks = [family_exchange(half_own, j) for j in range(1, half)] if n_pairs <= DIRECT else []
     y_far = [exchange(after(far, *y_own), 0, k) for k in range(2, n_ints, 2)]
-    lead = blocks[:1]
-    own_c, far_c = across(lean, *lead), across(far)
     far_tail_c = across(far_tail)
     if n_pairs <= DIRECT:
         blocks += [across(block) for block in blocks]
     else:
         blocks = [lax.all_gather(half_own, "pairs", axis=0, tiled=False)]
-    near_rows = [v for y in y_own for v in (y, across(y, *lead))]
-    away_rows = [v for y in y_far for v in (y, across(y))]
-    inter = call(
-        functools.partial(intermediate, len(y_own), item_block.shape[0], pairs),
-        shape((pairs * half_rows, domain), BF16),
-        [VM] * (7 + len(near_rows) + len(away_rows) + len(blocks)),
-        "intermediate",
-    )(lean, own_c, far, far_c, far_tail, far_tail_c, half_own, *near_rows, *away_rows, *blocks)
+    keep, give = call(
+        functools.partial(partials, len(y_own), item_block.shape[0], pairs),
+        [shape((pairs * half_rows, domain), BF16)] * 2,
+        [VM] * (5 + len(y_own) + len(y_far) + len(blocks)),
+        "partials",
+    )(lean, far, far_tail, far_tail_c, half_own, *y_own, *y_far, *blocks)
+    inter = call(joined, shape((pairs * half_rows, domain), BF16), [VM] * 2, "joined")(keep, across(give))
+    own_c, far_c = across(lean), across(far)
     if n_pairs <= DIRECT:
         units = [inter] + [exchange(inter, j, 0) for j in range(1, half)]
     else:
@@ -363,26 +380,27 @@
         units = [lax.dynamic_slice_in_dim(every, first, half, 0)]
     resid_far = exchange(resid_half, half, 0)
     n_units = len(units)
-    mix, inverse_far, swap = call(
+    mix, inverse_far, bias, swap = call(
         functools.partial(factors, n_units if n_units > 1 else 0, pairs),
         [
             shape((2 * pairs * pairs * half_rows, n_units * pairs * half_rows), BF16),
             shape((pairs, domain, domain), F32),
+            shape((pairs, domain, domain), F32),
             shape((pairs, 8, 128), jnp.int32),
         ],
-        [VM, VM, HB],
+        [VM, VM, VM, HB],
         "factors",
         [pltpu.SMEM(transpose_pair.shape, jnp.int32), pltpu.SemaphoreType.DMA],
-    )(tail, far_tail, stay(transpose_pair))
+    )(tail, far_tail, resid_far, stay(transpose_pair))
     mine, *sends = call(
         functools.partial(cycle, n_ints - 1, pairs),
         [shape((pairs, height, domain), F32)] + [shape((pairs, height, domain), BF16)] * (n_ints - 1),
         [VM] * (12 + n_units),
         "cycle",
-        [pltpu.VMEM((pairs, domain, domain), F32), pltpu.VMEM((domain, domain), F32)],
-    )(lean, own_c, far, far_c, tail, far_tail, resid_far, mix, inverse, inverse_far, base, swap, *units)
-    for offset, send in enumerate(sends, 1):
-        mine = mine + exchange(send, 0, offset).astype(F32)
+        [pltpu.VMEM((pairs, domain, domain), F32)],
+    )(lean, own_c, far, far_c, tail, far_tail, mix, inverse, inverse_far, bias, base, swap, *units)
+    for offset in [*range(2, n_ints), 1]:
+        mine = mine + exchange(sends[offset - 1], 0, offset).astype(F32)
     return -0.5 * mine
 
 

time: 38.7 us -> 37.3 us (0.964)
  starting transfers between devices: 22.7 us -> 19.7 us
  waiting for transfers between devices: 8.77 us -> 10.7 us
    ppermute x3, waiting for transfers between devices: 1.31 us -> 3.12 us  [family_exchange(): return lax.ppermute(value, ('pairs', 'ints'), route)]
    ppermute x3, starting transfers between devices: 5.08 us -> 3.49 us  [family_exchange(): return lax.ppermute(value, ('pairs', 'ints'), route)]
    ppermute x19 -> x18, starting transfers between devices: 17.7 us -> 16.2 us  [exchange(): return lax.ppermute(value, ('pairs', 'ints'), route)]
    pallas_call x1 -> x2, Pallas kernels: 1.01 us -> 0.8 us  [the longest x1 0.76 us: body(): call(functools.partial(partials, len(y_own), item_block.shape[0], pairs),...]
    ppermute x19 -> x18, waiting for transfers between devices: 7.46 us -> 7.53 us  [exchange(): return lax.ppermute(value, ('pairs', 'ints'), route)]
  transfers between devices with their start and end apart: 22 -> 21, of which waited for: 9 -> 9; matrix products, arithmetic and copies ran while one was open for 0% -> 0% of each run, Pallas kernels for 6% -> 7%
where the time goes in v4:
time: 37.3 us; the launch traced here: 37.1 us
  starting transfers between devices  19.7 us (53%)
  waiting for transfers between devices  10.7 us (29%)
  Pallas kernels  5.93 us (16%)
  other arithmetic  0.69 us (2%)
    ppermute x18, starting transfers between devices, exchange(): return lax.ppermute(value, ('pairs', 'ints'), route)  16.2 us
    ppermute x18, waiting for transfers between devices, exchange(): return lax.ppermute(value, ('pairs', 'ints'), route)  7.53 us
    ppermute x3, starting transfers between devices, family_exchange(): return lax.ppermute(value, ('pairs', 'ints'), route)  3.49 us
    ppermute x3, waiting for transfers between devices, family_exchange(): return lax.ppermute(value, ('pairs', 'ints'), route)  3.12 us
    pallas_call x1, Pallas kernels, body(): call(functools.partial(factors, n_units if n_units > 1 else 0, pairs), [s...  1.61 us
    pallas_call x1, Pallas kernels, body(): call(prepare, [shape((rows + TILE, domain), BF16), shape((half_rows, doma...  1.39 us
    pallas_call x1, Pallas kernels, body(): call(functools.partial(cycle, n_ints - 1, pairs), [shape((pairs, height,...  1.21 us
    pallas_call x1, Pallas kernels, body(): call(near_factors, [shape((pairs, domain, domain), F32), shape((pairs, he...  0.93 us
  transfers between devices with their start and end apart: 21, of which 9 were waited for; matrix products, arithmetic and copies ran while one was open for 0% of the time, Pallas kernels for 7%

profile of v4, /device:TPU:0, one launch (start us, length us, event | category | flops | bytes accessed | tf_op | source)
XLA Modules:
  0.0 37.1 jit_solution(18409305118910214702)
XLA Ops:
  0.0 1.4 %prepare.1 = (bf16[144,256]{1,0:T(8,128)(2,1)S(1)}, bf16[128,256]{1,0:T(8,128)(2,1)S(1)}, bf16[80,256]{1,0:T(8,128)(2,1)S(1)}, bf16[128,256]{1,0:T(8,128)(2,1)S(1)}) custom-call(f32[2,64,256]{2,1,0:T(8,128)} %amps.1, bf16[1,256,256]{2,1,0:T(8,128)(2,1)} %block.1, f32[2,64,256]{2,1,0:T(8,128)} %resid.3, f32[2,256]{1,0:T(2,128)} %virt.1, f32[2]{0:T(128)} %pair.1, ...), custom_call_target="tpu_custom_call" | custom-call | tf_op jit(solution)/shard_map/prepare/pallas_call | solution.py:333
  1.4 3.0 %collective-permute-start.6 = (bf16[144,256]{1,0:T(8,128)(2,1)S(1)}, bf16[144,256]{1,0:T(8,128)(2,1)S(1)}, u32[]{:S(2)}, u32[]{:S(2)}) collective-permute-start(bf16[144,256]{1,0:T(8,128)(2,1)S(1)} %get-tuple-element.22.own), channel_id=1, source_target_pairs={{0,2},{1,3},{2,0},{3,1},{4,6},{5,7},{6,4},{7,5},{8,10},{9,11},{10,... | collective-permute-start | bytes 221192 | tf_op jit(solution)/shard_map/ppermute | solution.py:31
  4.4 2.6 %collective-permute-start.1 = (bf16[144,256]{1,0:T(8,128)(2,1)S(1)}, bf16[144,256]{1,0:T(8,128)(2,1)S(1)}, u32[]{:S(2)}, u32[]{:S(2)}) collective-permute-start(bf16[144,256]{1,0:T(8,128)(2,1)S(1)} %get-tuple-element.22.own), channel_id=1, source_target_pairs={{0,16},{1,17},{2,18},{3,19},{4,20},{5,21},{6,22},{7,23},{8,24},{9,... | collective-permute-start | bytes 221192 | tf_op jit(solution)/shard_map/ppermute | solution.py:31
  7.0 2.5 %collective-permute-start.10 = (bf16[128,256]{1,0:T(8,128)(2,1)S(1)}, bf16[128,256]{1,0:T(8,128)(2,1)S(1)}, u32[]{:S(2)}, u32[]{:S(2)}) collective-permute-start(bf16[128,256]{1,0:T(8,128)(2,1)S(1)} %get-tuple-element.31.half_own), channel_id=1, source_target_pairs={{0,12},{1,29},{2,14},{3,31},{4,8},{5,25},{6,10},{7,27},{8,4},{9,21... | collective-permute-start | bytes 196616 | tf_op jit(solution)/shard_map/ppermute | solution.py:40
  9.5 0.4 %collective-permute-start.9 = (bf16[128,256]{1,0:T(8,128)(2,1)S(1)}, bf16[128,256]{1,0:T(8,128)(2,1)S(1)}, u32[]{:S(2)}, u32[]{:S(2)}) collective-permute-start(bf16[128,256]{1,0:T(8,128)(2,1)S(1)} %get-tuple-element.31.half_own), channel_id=1, source_target_pairs={{0,8},{1,25},{2,10},{3,27},{4,12},{5,29},{6,14},{7,31},{8,0},{9,17... | collective-permute-start | bytes 196616 | tf_op jit(solution)/shard_map/ppermute | solution.py:40
  10.0 0.5 %collective-permute-start.8 = (bf16[128,256]{1,0:T(8,128)(2,1)S(1)}, bf16[128,256]{1,0:T(8,128)(2,1)S(1)}, u32[]{:S(2)}, u32[]{:S(2)}) collective-permute-start(bf16[128,256]{1,0:T(8,128)(2,1)S(1)} %get-tuple-element.31.half_own), channel_id=1, source_target_pairs={{0,4},{1,21},{2,6},{3,23},{4,0},{5,17},{6,2},{7,19},{8,12},{9,29},... | collective-permute-start | bytes 196616 | tf_op jit(solution)/shard_map/ppermute | solution.py:40
  10.5 0.3 collective-permute-start.3
  10.8 0.0 collective-permute-done.1.far
  10.9 0.5 %collective-permute-start.7 = (bf16[144,256]{1,0:T(8,128)(2,1)S(1)}, bf16[144,256]{1,0:T(8,128)(2,1)S(1)}, u32[]{:S(2)}, u32[]{:S(2)}) collective-permute-start(bf16[144,256]{1,0:T(8,128)(2,1)S(1)} %collective-permute-done.1.far), channel_id=1, source_target_pairs={{0,2},{1,3},{2,0},{3,1},{4,6},{5,7},{6,4},{7,5},{8,10},{9,11},{10,... | collective-permute-start | bytes 221192 | tf_op jit(solution)/shard_map/ppermute | solution.py:31
  11.4 1.7 %collective-permute-done.10.refs_4_ = bf16[128,256]{1,0:T(8,128)(2,1)S(1)} collective-permute-done((bf16[128,256]{1,0:T(8,128)(2,1)S(1)}, bf16[128,256]{1,0:T(8,128)(2,1)S(1)}, u32[]{:S(2)}, u32[]{:S(2)}) %collective-permute-start.10) | collective-permute-done | bytes 65568 | tf_op jit(solution)/shard_map/ppermute | solution.py:40
  13.1 1.4 %collective-permute-done.9.refs_3_ = bf16[128,256]{1,0:T(8,128)(2,1)S(1)} collective-permute-done((bf16[128,256]{1,0:T(8,128)(2,1)S(1)}, bf16[128,256]{1,0:T(8,128)(2,1)S(1)}, u32[]{:S(2)}, u32[]{:S(2)}) %collective-permute-start.9) | collective-permute-done | bytes 65568 | tf_op jit(solution)/shard_map/ppermute | solution.py:40
  14.5 1.4 %collective-permute-start.11 = (bf16[128,256]{1,0:T(8,128)(2,1)S(1)}, bf16[128,256]{1,0:T(8,128)(2,1)S(1)}, u32[]{:S(2)}, u32[]{:S(2)}) collective-permute-start(bf16[128,256]{1,0:T(8,128)(2,1)S(1)} %collective-permute-done.8.refs_2_), channel_id=1, source_target_pairs={{0,1},{1,0},{2,3},{3,2},{4,5},{5,4},{6,7},{7,6},{8,9},{9,8},{10,11... | collective-permute-start | bytes 196616 | tf_op jit(solution)/shard_map/ppermute | solution.py:31
  15.9 0.9 %collective-permute-done.3.far.far_tail = bf16[80,256]{1,0:T(8,128)(2,1)S(1)} collective-permute-done((bf16[80,256]{1,0:T(8,128)(2,1)S(1)}, bf16[80,256]{1,0:T(8,128)(2,1)S(1)}, u32[]{:S(2)}, u32[]{:S(2)}) %collective-permute-start.3) | collective-permute-done | bytes 40992 | tf_op jit(solution)/shard_map/ppermute | solution.py:31
  16.7 0.2 collective-permute-start.5
  16.9 1.0 %collective-permute-done.5.far_tail_c = bf16[80,256]{1,0:T(8,128)(2,1)S(1)} collective-permute-done((bf16[80,256]{1,0:T(8,128)(2,1)S(1)}, bf16[80,256]{1,0:T(8,128)(2,1)S(1)}, u32[]{:S(2)}, u32[]{:S(2)}) %collective-permute-start.5) | collective-permute-done | bytes 40992 | tf_op jit(solution)/shard_map/ppermute | solution.py:31
  18.0 0.8 %partials.1 = (bf16[256,256]{1,0:T(8,128)(2,1)S(1)}, bf16[256,256]{1,0:T(8,128)(2,1)S(1)}) custom-call(bf16[144,256]{1,0:T(8,128)(2,1)S(1)} %get-tuple-element.22.own, bf16[144,256]{1,0:T(8,128)(2,1)S(1)} %collective-permute-done.1.far, bf16[80,256]{1,0:T(8,128)(2,1)S(1)} %collective-permute-done.3.far.far_tail, ...), custom_call_target="tpu_custom_call" | custom-call | tf_op jit(solution)/shard_map/partials/pallas_call | solution.py:367
  18.7 0.2 collective-permute-start.14
  19.0 1.6 %collective-permute-start.4 = (bf16[128,256]{1,0:T(8,128)(2,1)S(1)}, bf16[128,256]{1,0:T(8,128)(2,1)S(1)}, u32[]{:S(2)}, u32[]{:S(2)}) collective-permute-start(bf16[128,256]{1,0:T(8,128)(2,1)S(1)} %get-tuple-element.24), channel_id=1, source_target_pairs={{0,16},{1,17},{2,18},{3,19},{4,20},{5,21},{6,22},{7,23},{8,24},{9,... | collective-permute-start | bytes 196616 | tf_op jit(solution)/shard_map/ppermute | solution.py:31
  20.7 2.9 %collective-permute-start.17 = (bf16[256,256]{1,0:T(8,128)(2,1)S(1)}, bf16[256,256]{1,0:T(8,128)(2,1)S(1)}, u32[]{:S(2)}, u32[]{:S(2)}) collective-permute-start(bf16[256,256]{1,0:T(8,128)(2,1)S(1)} %joined.1.refs_0_), channel_id=1, source_target_pairs={{0,12},{1,13},{2,14},{3,15},{4,8},{5,9},{6,10},{7,11},{8,4},{9,5},... | collective-permute-start | bytes 393224 | tf_op jit(solution)/shard_map/ppermute | solution.py:31
  23.6 1.2 %collective-permute-start.15 = (bf16[256,256]{1,0:T(8,128)(2,1)S(1)}, bf16[256,256]{1,0:T(8,128)(2,1)S(1)}, u32[]{:S(2)}, u32[]{:S(2)}) collective-permute-start(bf16[256,256]{1,0:T(8,128)(2,1)S(1)} %joined.1.refs_0_), channel_id=1, source_target_pairs={{0,4},{1,5},{2,6},{3,7},{4,0},{5,1},{6,2},{7,3},{8,12},{9,13},{10,... | collective-permute-start | bytes 393224 | tf_op jit(solution)/shard_map/ppermute | solution.py:31
  24.8 0.9 %collective-permute-done.4.resid_far = bf16[128,256]{1,0:T(8,128)(2,1)S(1)} collective-permute-done((bf16[128,256]{1,0:T(8,128)(2,1)S(1)}, bf16[128,256]{1,0:T(8,128)(2,1)S(1)}, u32[]{:S(2)}, u32[]{:S(2)}) %collective-permute-start.4) | collective-permute-done | bytes 65568 | tf_op jit(solution)/shard_map/ppermute | solution.py:31
  25.7 0.9 %near_factors.1 = (f32[2,256,256]{2,1,0:T(8,128)S(1)}, f32[2,64,256]{2,1,0:T(8,128)S(1)}) custom-call(f32[2,64,256]{2,1,0:T(8,128)} %resid.3, bf16[80,256]{1,0:T(8,128)(2,1)S(1)} %get-tuple-element.23.own.tail), custom_call_target="tpu_custom_call" | custom-call | flops 1000000000 | tf_op jit(solution)/shard_map/near_factors/pallas_call | solution.py:346
  26.7 1.6 %factors.1 = (bf16[1024,1024]{1,0:T(8,128)(2,1)S(1)}, f32[2,256,256]{2,1,0:T(8,128)S(1)}, f32[2,256,256]{2,1,0:T(8,128)S(1)}, s32[2,8,128]{2,1,0:T(8,128)S(1)}) custom-call(bf16[80,256]{1,0:T(8,128)(2,1)S(1)} %get-tuple-element.23.own.tail, bf16[80,256]{1,0:T(8,128)(2,1)S(1)} %collective-permute-done.3.far.far_tail, ...), custom_call_target="tpu_custom_call" | custom-call | tf_op jit(solution)/shard_map/factors/pallas_call | solution.py:383
  28.3 0.9 %collective-permute-done.17.refs_3_ = bf16[256,256]{1,0:T(8,128)(2,1)S(1)} collective-permute-done((bf16[256,256]{1,0:T(8,128)(2,1)S(1)}, bf16[256,256]{1,0:T(8,128)(2,1)S(1)}, u32[]{:S(2)}, u32[]{:S(2)}) %collective-permute-start.17) | collective-permute-done | bytes 131104 | tf_op jit(solution)/shard_map/ppermute | solution.py:31
  29.2 1.0 %collective-permute-done.16.refs_2_ = bf16[256,256]{1,0:T(8,128)(2,1)S(1)} collective-permute-done((bf16[256,256]{1,0:T(8,128)(2,1)S(1)}, bf16[256,256]{1,0:T(8,128)(2,1)S(1)}, u32[]{:S(2)}, u32[]{:S(2)}) %collective-permute-start.16) | collective-permute-done | bytes 131104 | tf_op jit(solution)/shard_map/ppermute | solution.py:31
  30.1 0.1 collective-permute-done.15.refs_1_
  30.2 1.2 %cycle.1 = (f32[2,64,256]{2,1,0:T(8,128)S(1)}, bf16[2,64,256]{2,1,0:T(8,128)(2,1)S(1)}, bf16[2,64,256]{2,1,0:T(8,128)(2,1)S(1)}, bf16[2,64,256]{2,1,0:T(8,128)(2,1)S(1)}) custom-call(bf16[144,256]{1,0:T(8,128)(2,1)S(1)} %get-tuple-element.22.own, bf16[144,256]{1,0:T(8,128)(2,1)S(1)} %collective-permute-done.own_c, ...), custom_call_target="tpu_custom_call" | custom-call | tf_op jit(solution)/shard_map/cycle/pallas_call | solution.py:395
  31.4 0.6 %collective-permute-start.18 = (bf16[2,64,256]{2,1,0:T(8,128)(2,1)S(1)}, bf16[2,64,256]{2,1,0:T(8,128)(2,1)S(1)}, u32[]{:S(2)}, u32[]{:S(2)}) collective-permute-start(bf16[2,64,256]{2,1,0:T(8,128)(2,1)S(1)} %get-tuple-element.36), channel_id=1, source_target_pairs={{0,2},{1,3},{2,0},{3,1},{4,6},{5,7},{6,4},{7,5},{8,10},{9,11},{10,... | collective-permute-start | bytes 196616 | tf_op jit(solution)/shard_map/ppermute | solution.py:31
  32.0 0.0 collective-permute-start.19
  32.0 1.6 %collective-permute-start.20 = (bf16[2,64,256]{2,1,0:T(8,128)(2,1)S(1)}, bf16[2,64,256]{2,1,0:T(8,128)(2,1)S(1)}, u32[]{:S(2)}, u32[]{:S(2)}) collective-permute-start(bf16[2,64,256]{2,1,0:T(8,128)(2,1)S(1)} %get-tuple-element.38), channel_id=1, source_target_pairs={{0,1},{1,0},{2,3},{3,2},{4,5},{5,4},{6,7},{7,6},{8,9},{9,8},{10,11... | collective-permute-start | bytes 196616 | tf_op jit(solution)/shard_map/ppermute | solution.py:31
  33.6 2.8 %collective-permute-done.18 = bf16[2,64,256]{2,1,0:T(8,128)(2,1)S(1)} collective-permute-done((bf16[2,64,256]{2,1,0:T(8,128)(2,1)S(1)}, bf16[2,64,256]{2,1,0:T(8,128)(2,1)S(1)}, u32[]{:S(2)}, u32[]{:S(2)}) %collective-permute-start.18) | collective-permute-done | bytes 65568 | tf_op jit(solution)/shard_map/ppermute | solution.py:31
  36.4 0.7 %add_multiply_fusion = f32[2,64,256]{2,1,0:T(8,128)} fusion(bf16[2,64,256]{2,1,0:T(8,128)(2,1)S(1)} %collective-permute-done.20, bf16[2,64,256]{2,1,0:T(8,128)(2,1)S(1)} %collective-permute-done.19, f32[2,64,256]{2,1,0:T(8,128)S(1)} %get-tuple-element.35, bf16[2,64,256]{2,1,0:T(8,128)(2,1)S(1)} %collective-permute-done.18), kind=kLoop, calls=%fused_computation | loop fusion | flops 229376 | bytes 458752 | tf_op jit(solution)/shard_map/mul | solution.py:404
  (17 shorter events, 0.1 us)
Async XLA Ops:
  1.4 9.1 %collective-permute-start.6 = (bf16[144,256]{1,0:T(8,128)(2,1)S(1)}, bf16[144,256]{1,0:T(8,128)(2,1)S(1)}, u32[]{:S(2)}, u32[]{:S(2)}) collective-permute-start(bf16[144,256]{1,0:T(8,128)(2,1)S(1)} %get-tuple-element.22.own), channel_id=1, source_target_pairs={{0,2},{1,3},{2,0},{3,1},{4,6},{5,7},{6,4},{7,5},{8,10},{9,11},{10,... | collective-permute-start | bytes 221192 | tf_op jit(solution)/shard_map/ppermute | solution.py:31
  4.4 6.4 %collective-permute-start.1 = (bf16[144,256]{1,0:T(8,128)(2,1)S(1)}, bf16[144,256]{1,0:T(8,128)(2,1)S(1)}, u32[]{:S(2)}, u32[]{:S(2)}) collective-permute-start(bf16[144,256]{1,0:T(8,128)(2,1)S(1)} %get-tuple-element.22.own), channel_id=1, source_target_pairs={{0,16},{1,17},{2,18},{3,19},{4,20},{5,21},{6,22},{7,23},{8,24},{9,... | collective-permute-start | bytes 221192 | tf_op jit(solution)/shard_map/ppermute | solution.py:31
  7.0 6.1 %collective-permute-start.10 = (bf16[128,256]{1,0:T(8,128)(2,1)S(1)}, bf16[128,256]{1,0:T(8,128)(2,1)S(1)}, u32[]{:S(2)}, u32[]{:S(2)}) collective-permute-start(bf16[128,256]{1,0:T(8,128)(2,1)S(1)} %get-tuple-element.31.half_own), channel_id=1, source_target_pairs={{0,12},{1,29},{2,14},{3,31},{4,8},{5,25},{6,10},{7,27},{8,4},{9,21... | collective-permute-start | bytes 196616 | tf_op jit(solution)/shard_map/ppermute | solution.py:40
  9.5 5.0 %collective-permute-start.9 = (bf16[128,256]{1,0:T(8,128)(2,1)S(1)}, bf16[128,256]{1,0:T(8,128)(2,1)S(1)}, u32[]{:S(2)}, u32[]{:S(2)}) collective-permute-start(bf16[128,256]{1,0:T(8,128)(2,1)S(1)} %get-tuple-element.31.half_own), channel_id=1, source_target_pairs={{0,8},{1,25},{2,10},{3,27},{4,12},{5,29},{6,14},{7,31},{8,0},{9,17... | collective-permute-start | bytes 196616 | tf_op jit(solution)/shard_map/ppermute | solution.py:40
  10.0 4.5 %collective-permute-start.8 = (bf16[128,256]{1,0:T(8,128)(2,1)S(1)}, bf16[128,256]{1,0:T(8,128)(2,1)S(1)}, u32[]{:S(2)}, u32[]{:S(2)}) collective-permute-start(bf16[128,256]{1,0:T(8,128)(2,1)S(1)} %get-tuple-element.31.half_own), channel_id=1, source_target_pairs={{0,4},{1,21},{2,6},{3,23},{4,0},{5,17},{6,2},{7,19},{8,12},{9,29},... | collective-permute-start | bytes 196616 | tf_op jit(solution)/shard_map/ppermute | solution.py:40
  10.5 6.2 %collective-permute-start.3 = (bf16[80,256]{1,0:T(8,128)(2,1)S(1)}, bf16[80,256]{1,0:T(8,128)(2,1)S(1)}, u32[]{:S(2)}, u32[]{:S(2)}) collective-permute-start(bf16[80,256]{1,0:T(8,128)(2,1)S(1)} %get-tuple-element.23.own.tail), channel_id=1, source_target_pairs={{0,16},{1,17},{2,18},{3,19},{4,20},{5,21},{6,22},{7,23},{8,24},{9,... | collective-permute-start | bytes 122888 | tf_op jit(solution)/shard_map/ppermute | solution.py:31
  10.9 7.1 %collective-permute-start.7 = (bf16[144,256]{1,0:T(8,128)(2,1)S(1)}, bf16[144,256]{1,0:T(8,128)(2,1)S(1)}, u32[]{:S(2)}, u32[]{:S(2)}) collective-permute-start(bf16[144,256]{1,0:T(8,128)(2,1)S(1)} %collective-permute-done.1.far), channel_id=1, source_target_pairs={{0,2},{1,3},{2,0},{3,1},{4,6},{5,7},{6,4},{7,5},{8,10},{9,11},{10,... | collective-permute-start | bytes 221192 | tf_op jit(solution)/shard_map/ppermute | solution.py:31
  13.1 4.9 %collective-permute-start.13 = (bf16[128,256]{1,0:T(8,128)(2,1)S(1)}, bf16[128,256]{1,0:T(8,128)(2,1)S(1)}, u32[]{:S(2)}, u32[]{:S(2)}) collective-permute-start(bf16[128,256]{1,0:T(8,128)(2,1)S(1)} %collective-permute-done.10.refs_4_), channel_id=1, source_target_pairs={{0,1},{1,0},{2,3},{3,2},{4,5},{5,4},{6,7},{7,6},{8,9},{9,8},{10,11... | collective-permute-start | bytes 196616 | tf_op jit(solution)/shard_map/ppermute | solution.py:31
  14.5 3.5 %collective-permute-start.12 = (bf16[128,256]{1,0:T(8,128)(2,1)S(1)}, bf16[128,256]{1,0:T(8,128)(2,1)S(1)}, u32[]{:S(2)}, u32[]{:S(2)}) collective-permute-start(bf16[128,256]{1,0:T(8,128)(2,1)S(1)} %collective-permute-done.9.refs_3_), channel_id=1, source_target_pairs={{0,1},{1,0},{2,3},{3,2},{4,5},{5,4},{6,7},{7,6},{8,9},{9,8},{10,11... | collective-permute-start | bytes 196616 | tf_op jit(solution)/shard_map/ppermute | solution.py:31
  14.5 3.5 %collective-permute-start.11 = (bf16[128,256]{1,0:T(8,128)(2,1)S(1)}, bf16[128,256]{1,0:T(8,128)(2,1)S(1)}, u32[]{:S(2)}, u32[]{:S(2)}) collective-permute-start(bf16[128,256]{1,0:T(8,128)(2,1)S(1)} %collective-permute-done.8.refs_2_), channel_id=1, source_target_pairs={{0,1},{1,0},{2,3},{3,2},{4,5},{5,4},{6,7},{7,6},{8,9},{9,8},{10,11... | collective-permute-start | bytes 196616 | tf_op jit(solution)/shard_map/ppermute | solution.py:31
  16.7 1.2 %collective-permute-start.5 = (bf16[80,256]{1,0:T(8,128)(2,1)S(1)}, bf16[80,256]{1,0:T(8,128)(2,1)S(1)}, u32[]{:S(2)}, u32[]{:S(2)}) collective-permute-start(bf16[80,256]{1,0:T(8,128)(2,1)S(1)} %collective-permute-done.3.far.far_tail), channel_id=1, source_target_pairs={{0,1},{1,0},{2,3},{3,2},{4,5},{5,4},{6,7},{7,6},{8,9},{9,8},{10,11... | collective-permute-start | bytes 122888 | tf_op jit(solution)/shard_map/ppermute | solution.py:31
  18.7 1.9 %collective-permute-start.14 = (bf16[256,256]{1,0:T(8,128)(2,1)S(1)}, bf16[256,256]{1,0:T(8,128)(2,1)S(1)}, u32[]{:S(2)}, u32[]{:S(2)}) collective-permute-start(bf16[256,256]{1,0:T(8,128)(2,1)S(1)} %get-tuple-element.34), channel_id=1, source_target_pairs={{0,1},{1,0},{2,3},{3,2},{4,5},{5,4},{6,7},{7,6},{8,9},{9,8},{10,11... | collective-permute-start | bytes 393224 | tf_op jit(solution)/shard_map/ppermute | solution.py:31
  19.0 6.7 %collective-permute-start.4 = (bf16[128,256]{1,0:T(8,128)(2,1)S(1)}, bf16[128,256]{1,0:T(8,128)(2,1)S(1)}, u32[]{:S(2)}, u32[]{:S(2)}) collective-permute-start(bf16[128,256]{1,0:T(8,128)(2,1)S(1)} %get-tuple-element.24), channel_id=1, source_target_pairs={{0,16},{1,17},{2,18},{3,19},{4,20},{5,21},{6,22},{7,23},{8,24},{9,... | collective-permute-start | bytes 196616 | tf_op jit(solution)/shard_map/ppermute | solution.py:31
  20.7 8.5 %collective-permute-start.17 = (bf16[256,256]{1,0:T(8,128)(2,1)S(1)}, bf16[256,256]{1,0:T(8,128)(2,1)S(1)}, u32[]{:S(2)}, u32[]{:S(2)}) collective-permute-start(bf16[256,256]{1,0:T(8,128)(2,1)S(1)} %joined.1.refs_0_), channel_id=1, source_target_pairs={{0,12},{1,13},{2,14},{3,15},{4,8},{5,9},{6,10},{7,11},{8,4},{9,5},... | collective-permute-start | bytes 393224 | tf_op jit(solution)/shard_map/ppermute | solution.py:31
  23.6 6.5 %collective-permute-start.16 = (bf16[256,256]{1,0:T(8,128)(2,1)S(1)}, bf16[256,256]{1,0:T(8,128)(2,1)S(1)}, u32[]{:S(2)}, u32[]{:S(2)}) collective-permute-start(bf16[256,256]{1,0:T(8,128)(2,1)S(1)} %joined.1.refs_0_), channel_id=1, source_target_pairs={{0,8},{1,9},{2,10},{3,11},{4,12},{5,13},{6,14},{7,15},{8,0},{9,1},... | collective-permute-start | bytes 393224 | tf_op jit(solution)/shard_map/ppermute | solution.py:31
  23.6 6.6 %collective-permute-start.15 = (bf16[256,256]{1,0:T(8,128)(2,1)S(1)}, bf16[256,256]{1,0:T(8,128)(2,1)S(1)}, u32[]{:S(2)}, u32[]{:S(2)}) collective-permute-start(bf16[256,256]{1,0:T(8,128)(2,1)S(1)} %joined.1.refs_0_), channel_id=1, source_target_pairs={{0,4},{1,5},{2,6},{3,7},{4,0},{5,1},{6,2},{7,3},{8,12},{9,13},{10,... | collective-permute-start | bytes 393224 | tf_op jit(solution)/shard_map/ppermute | solution.py:31
  24.8 3.5 %collective-permute-start = (bf16[144,256]{1,0:T(8,128)(2,1)S(1)}, bf16[144,256]{1,0:T(8,128)(2,1)S(1)}, u32[]{:S(2)}, u32[]{:S(2)}) collective-permute-start(bf16[144,256]{1,0:T(8,128)(2,1)S(1)} %get-tuple-element.22.own), channel_id=1, source_target_pairs={{0,1},{1,0},{2,3},{3,2},{4,5},{5,4},{6,7},{7,6},{8,9},{9,8},{10,11... | collective-permute-start | bytes 221192 | tf_op jit(solution)/shard_map/ppermute | solution.py:31
  25.7 2.6 %collective-permute-start.2 = (bf16[144,256]{1,0:T(8,128)(2,1)S(1)}, bf16[144,256]{1,0:T(8,128)(2,1)S(1)}, u32[]{:S(2)}, u32[]{:S(2)}) collective-permute-start(bf16[144,256]{1,0:T(8,128)(2,1)S(1)} %collective-permute-done.1.far), channel_id=1, source_target_pairs={{0,1},{1,0},{2,3},{3,2},{4,5},{5,4},{6,7},{7,6},{8,9},{9,8},{10,11... | collective-permute-start | bytes 221192 | tf_op jit(solution)/shard_map/ppermute | solution.py:31
  31.4 5.0 %collective-permute-start.18 = (bf16[2,64,256]{2,1,0:T(8,128)(2,1)S(1)}, bf16[2,64,256]{2,1,0:T(8,128)(2,1)S(1)}, u32[]{:S(2)}, u32[]{:S(2)}) collective-permute-start(bf16[2,64,256]{2,1,0:T(8,128)(2,1)S(1)} %get-tuple-element.36), channel_id=1, source_target_pairs={{0,2},{1,3},{2,0},{3,1},{4,6},{5,7},{6,4},{7,5},{8,10},{9,11},{10,... | collective-permute-start | bytes 196616 | tf_op jit(solution)/shard_map/ppermute | solution.py:31
  32.0 4.4 %collective-permute-start.19 = (bf16[2,64,256]{2,1,0:T(8,128)(2,1)S(1)}, bf16[2,64,256]{2,1,0:T(8,128)(2,1)S(1)}, u32[]{:S(2)}, u32[]{:S(2)}) collective-permute-start(bf16[2,64,256]{2,1,0:T(8,128)(2,1)S(1)} %get-tuple-element.37), channel_id=1, source_target_pairs={{0,3},{1,2},{2,1},{3,0},{4,7},{5,6},{6,5},{7,4},{8,11},{9,10},{10,... | collective-permute-start | bytes 196616 | tf_op jit(solution)/shard_map/ppermute | solution.py:31
  32.0 4.4 %collective-permute-start.20 = (bf16[2,64,256]{2,1,0:T(8,128)(2,1)S(1)}, bf16[2,64,256]{2,1,0:T(8,128)(2,1)S(1)}, u32[]{:S(2)}, u32[]{:S(2)}) collective-permute-start(bf16[2,64,256]{2,1,0:T(8,128)(2,1)S(1)} %get-tuple-element.38), channel_id=1, source_target_pairs={{0,1},{1,0},{2,3},{3,2},{4,5},{5,4},{6,7},{7,6},{8,9},{9,8},{10,11... | collective-permute-start | bytes 196616 | tf_op jit(solution)/shard_map/ppermute | solution.py:31

commit v5 on v4

--- a/solution.py
+++ b/solution.py
@@ -173,12 +173,27 @@
     return dot((which == iota((tall, 2 * TILE), 1)).astype(BF16), counts).astype(BF16)
 
 
-def weights(spread, source_group, pairs, half_rows):
-    tall, lanes = spread.shape
-    wide = pairs * half_rows
-    same = iota((tall, wide), 0) % half_rows == iota((tall, wide), 1) % half_rows
-    place_of = iota((lanes, wide), 0) == source_group * pairs + iota((lanes, wide), 1) // half_rows
-    return jnp.where(same, dot(spread, place_of.astype(BF16)), 0.0).astype(BF16)
+def shares(spread, source_group, at, pairs, half_rows, flipped):
+    wide, lanes = pairs * half_rows, spread.shape[1]
+    picked = (iota((wide, lanes), 1) == source_group * pairs + iota((wide, lanes), 0) // half_rows).astype(BF16)
+    part = spread[at * wide : (at + 1) * wide]
+    same = iota((wide, wide), 0) % half_rows == iota((wide, wide), 1) % half_rows
+    return jnp.where(same, dot(part, picked, NT) if flipped else dot(picked, part, NT), 0.0).astype(BF16)
+
+
+def rows_of(core, mine, other, pairs):
+    rows = mine.shape[0] - TILE
+    height = rows // pairs
+    low, high = ordered(core, mine[:rows, :], other[:rows, :])
+    return jnp.concatenate(
+        [part[p * height : (p + 1) * height] for p in range(pairs) for part in (low, high)], axis=0
+    )
+
+
+def mixed_rows(spread, source_group, near, away, pairs, half_rows):
+    z = [dot(shares(spread, source_group, p, pairs, half_rows, False), near) for p in range(pairs)]
+    zt = [dot(away, shares(spread, source_group, pairs + p, pairs, half_rows, True), TN) for p in range(pairs)]
+    return jnp.concatenate(z, axis=1).astype(BF16), jnp.concatenate(zt, axis=0).astype(BF16)
 
 
 def lanes_of(pairs):
@@ -210,21 +225,27 @@
     base_out[...] = held[...] * inverse_out[:, pl.ds(start, height), :]
 
 
-def factors(n_units, pairs, own, far, resid_far, swap, weights_out, inverse_out, bias_out, swap_out, held, sem):
+def factors(
+    n_units, pairs, own, own_c, far, far_c, tail, far_tail, resid_far, swap, z_out, zt_out, inverse_out, bias_out, swap_out, held, sem
+):
     copy = pltpu.make_async_copy(swap, held, sem)
     copy.start()
-    half_rows = weights_out.shape[0] // (2 * pairs * pairs)
+    group, _, core, family, half = place()
+    height, domain = resid_far.shape[0] // pairs, resid_far.shape[1]
+    half_rows = 2 * height
     wide = pairs * half_rows
-    group, _, _, family, half = place()
-    height, domain = resid_far.shape[0] // pairs, resid_far.shape[1]
     spot = (iota((height, domain), 1) == iota((height, domain), 0) + lax.axis_index("ints") * height).astype(BF16)
-    away = energies(far, pairs)
+    away = energies(far_tail, pairs)
     away = [inverse_of(*away, p, pairs) for p in range(pairs)]
     copy.wait()
     swaps = [held[p] - (group ^ half) * pairs for p in range(pairs)]
-    spread = spread_counts(own, far, swaps, half_rows, lanes_of(pairs))
+    if n_units:
+        spread = spread_counts(tail, far_tail, swaps, half_rows, lanes_of(pairs))
+        near_rows, away_rows = rows_of(core, own, own_c, pairs), rows_of(core, far, far_c, pairs)
     for k in range(n_units):
-        weights_out[:, k * wide : (k + 1) * wide] = weights(spread, family ^ k, pairs, half_rows)
+        z, zt = mixed_rows(spread, family ^ k, near_rows, away_rows, pairs, half_rows)
+        z_out[k * wide : (k + 1) * wide, :] = z
+        zt_out[:, k * wide : (k + 1) * wide] = zt
     for p in range(pairs):
         inverse_out[p] = functools.reduce(
             lambda kept, k: jnp.where(swaps[p] == k, away[k], kept), range(1, pairs), away[0]
@@ -237,41 +258,47 @@
         swap_out[p] = jnp.full(swap_out.shape[1:], swaps[p], jnp.int32)
 
 
-def cycle(n_sends, pairs, own, own_c, far, far_c, tail, far_tail, mix, inverse, inverse_far, bias, base, swap, *refs):
+def summed(units, starts, z, zt):
+    both = jnp.concatenate([unit[...] for unit in units], axis=0)
+    wide = units[0].shape[0]
+    z_part = jnp.concatenate([z[k * wide : (k + 1) * wide, :] for k in starts], axis=0)
+    zt_part = jnp.concatenate([zt[:, k * wide : (k + 1) * wide] for k in starts], axis=1)
+    return dot(both, z_part, TN), dot(zt_part, both)
+
+
+def cycle_first(starts, pairs, own, own_c, far, far_c, tail, far_tail, z, zt, swap, *refs):
+    units, near_out, away_out = refs[:-2], refs[-2], refs[-1]
+    if starts:
+        near_out[...], away_out[...] = summed(units, starts, z, zt)
+        return
+    half_rows = units[0].shape[1] // pairs
+    group, _, core, _, half = place()
+    spread = spread_counts(tail, far_tail, [swap[p, :1, :1] for p in range(pairs)], half_rows, lanes_of(pairs))
+    near_rows, away_rows = rows_of(core, own, own_c, pairs), rows_of(core, far, far_c, pairs)
+    first = group - group % half
+    near_out[...], away_out[...] = jnp.zeros(near_out.shape, F32), jnp.zeros(away_out.shape, F32)
+
+    def step(k, none):
+        part, part_t = mixed_rows(spread, (first + k) ^ (core * half), near_rows, away_rows, pairs, half_rows)
+        near_out[...] += dot(units[0][k], part, TN)
+        away_out[...] += dot(part_t, units[0][k])
+        return none
+
+    lax.fori_loop(0, units[0].shape[0], step, 0)
+
+
+def cycle_last(n_sends, starts, z, zt, near, away, inverse, inverse_far, bias, base, *refs):
     units, (own_out, *sends), here = refs[: -n_sends - 2], refs[-n_sends - 2 : -1], refs[-1]
-    height, domain = base.shape[1:]
-    rows = pairs * height
-    half_rows = 2 * height
-    group, member, core, family, half = place()
-    if len(units) > 1:
-        mixed = dot(mix[...], jnp.concatenate([unit[...] for unit in units], axis=0))
-    else:
-        swaps = [swap[p, :1, :1] for p in range(pairs)]
-        spread = spread_counts(tail, far_tail, swaps, half_rows, lanes_of(pairs))
-        first = group - group % half
-        mixed = lax.fori_loop(
-            0,
-            units[0].shape[0],
-            lambda k, sofar: sofar
-            + dot(weights(spread, (first + k) ^ (core * half), pairs, half_rows), units[0][k]),
-            jnp.zeros((spread.shape[0], domain), F32),
-        )
-    mixed = mixed.astype(BF16)
+    pairs, height, domain = base.shape
+    member = lax.axis_index("ints")
+    near, away = near[...], away[...]
+    if units:
+        more, more_away = summed(units, starts, z, zt)
+        near, away = near + more, away + more_away
+    for p in range(pairs):
+        part = slice(p * domain, (p + 1) * domain)
+        here[p] = near[:, part] * inverse[p] + (away[part] * inverse_far[p] + bias[p])
     start = pl.ds(pl.multiple_of(member * height, height), height)
-
-    def amps_of(mine, other):
-        low, high = ordered(core, mine[:rows, :], other[:rows, :])
-        return jnp.concatenate(
-            [part[p * height : (p + 1) * height] for p in range(pairs) for part in (low, high)], axis=0
-        )
-
-    wide = pairs * half_rows
-    near, away = amps_of(own, own_c), amps_of(far, far_c)
-    for p in range(pairs):
-        at = (pairs + p) * wide
-        mirror = dot(away, mixed[at : at + wide], TN) * inverse_far[p] + bias[p]
-        at = p * wide
-        here[p] = dot(mixed[at : at + wide], near, TN) * inverse[p] + mirror
     own_out[...] = here[:, start, :] + base[...]
     for offset, send in enumerate(sends, 1):
         to = pl.multiple_of((member ^ offset) * height, height)
@@ -380,25 +407,36 @@
         units = [lax.dynamic_slice_in_dim(every, first, half, 0)]
     resid_far = exchange(resid_half, half, 0)
     n_units = len(units)
-    mix, inverse_far, bias, swap = call(
-        functools.partial(factors, n_units if n_units > 1 else 0, pairs),
+    wide, planned = pairs * half_rows, n_units if n_units > 1 else 0
+    z, zt, inverse_far, bias, swap = call(
+        functools.partial(factors, planned, pairs),
         [
-            shape((2 * pairs * pairs * half_rows, n_units * pairs * half_rows), BF16),
+            shape((n_units * wide, pairs * domain), BF16),
+            shape((pairs * domain, n_units * wide), BF16),
             shape((pairs, domain, domain), F32),
             shape((pairs, domain, domain), F32),
             shape((pairs, 8, 128), jnp.int32),
         ],
-        [VM, VM, VM, HB],
+        [VM] * 7 + [HB],
         "factors",
         [pltpu.SMEM(transpose_pair.shape, jnp.int32), pltpu.SemaphoreType.DMA],
-    )(tail, far_tail, resid_far, stay(transpose_pair))
+    )(lean, own_c, far, far_c, tail, far_tail, resid_far, stay(transpose_pair))
+    early = [0, planned - 1] if planned else []
+    late = [k for k in range(planned) if k not in early]
+    first_units = [units[k] for k in early] or units
+    near, away = call(
+        functools.partial(cycle_first, early, pairs),
+        [shape((domain, pairs * domain), F32), shape((pairs * domain, domain), F32)],
+        [VM] * (9 + len(first_units)),
+        "cycle_first",
+    )(lean, own_c, far, far_c, tail, far_tail, z, zt, swap, *first_units)
     mine, *sends = call(
-        functools.partial(cycle, n_ints - 1, pairs),
+        functools.partial(cycle_last, n_ints - 1, late),
         [shape((pairs, height, domain), F32)] + [shape((pairs, height, domain), BF16)] * (n_ints - 1),
-        [VM] * (12 + n_units),
-        "cycle",
+        [VM] * (8 + len(late)),
+        "cycle_last",
         [pltpu.VMEM((pairs, domain, domain), F32)],
-    )(lean, own_c, far, far_c, tail, far_tail, mix, inverse, inverse_far, bias, base, swap, *units)
+    )(z, zt, near, away, inverse, inverse_far, bias, base, *[units[k] for k in late])
     for offset in [*range(2, n_ints), 1]:
         mine = mine + exchange(sends[offset - 1], 0, offset).astype(F32)
     return -0.5 * mine

time: 37.3 us -> 37.1 us (level)
  waiting for transfers between devices: 10.7 us -> 9.09 us
  starting transfers between devices: 19.7 us -> 20.6 us
  Pallas kernels: 5.93 us -> 6.41 us
    ppermute x3, waiting for transfers between devices: 3.12 us -> 1.67 us  [family_exchange(): return lax.ppermute(value, ('pairs', 'ints'), route)]
    ppermute x18, starting transfers between devices: 16.2 us -> 17.1 us  [exchange(): return lax.ppermute(value, ('pairs', 'ints'), route)]
    pallas_call x2 -> x3, Pallas kernels: 2.82 us -> 3.3 us  [the longest x1 2.3 us: body(): call(functools.partial(factors, planned, pairs), [shape((n_units * wide,...]
  transfers between devices with their start and end apart: 21 -> 21, of which waited for: 9 -> 7; matrix products, arithmetic and copies ran while one was open for 0% -> 0% of each run, Pallas kernels for 7% -> 10%
where the time goes in v5:
time: 37.1 us; the launch traced here: 36.9 us
  starting transfers between devices  20.6 us (56%)
  waiting for transfers between devices  9.09 us (25%)
  Pallas kernels  6.41 us (17%)
  other arithmetic  0.7 us (2%)
    ppermute x18, starting transfers between devices, exchange(): return lax.ppermute(value, ('pairs', 'ints'), route)  17.1 us
    ppermute x18, waiting for transfers between devices, exchange(): return lax.ppermute(value, ('pairs', 'ints'), route)  7.42 us
    ppermute x3, starting transfers between devices, family_exchange(): return lax.ppermute(value, ('pairs', 'ints'), route)  3.49 us
    pallas_call x1, Pallas kernels, body(): call(functools.partial(factors, planned, pairs), [shape((n_units * wide,...  2.3 us
    ppermute x3, waiting for transfers between devices, family_exchange(): return lax.ppermute(value, ('pairs', 'ints'), route)  1.67 us
    pallas_call x1, Pallas kernels, body(): call(prepare, [shape((rows + TILE, domain), BF16), shape((half_rows, doma...  1.39 us
    pallas_call x1, Pallas kernels, body(): call(near_factors, [shape((pairs, domain, domain), F32), shape((pairs, he...  0.93 us
    pallas_call x1, Pallas kernels, body(): call(functools.partial(partials, len(y_own), item_block.shape[0], pairs),...  0.76 us
  transfers between devices with their start and end apart: 21, of which 7 were waited for; matrix products, arithmetic and copies ran while one was open for 0% of the time, Pallas kernels for 10%

profile of v5, /device:TPU:0, one launch (start us, length us, event | category | flops | bytes accessed | tf_op | source)
XLA Modules:
  0.0 36.9 jit_solution(967866450492954101)
XLA Ops:
  0.0 1.4 %prepare.1 = (bf16[144,256]{1,0:T(8,128)(2,1)S(1)}, bf16[128,256]{1,0:T(8,128)(2,1)S(1)}, bf16[80,256]{1,0:T(8,128)(2,1)S(1)}, bf16[128,256]{1,0:T(8,128)(2,1)S(1)}) custom-call(f32[2,64,256]{2,1,0:T(8,128)} %amps.1, bf16[1,256,256]{2,1,0:T(8,128)(2,1)} %block.1, f32[2,64,256]{2,1,0:T(8,128)} %resid.3, f32[2,256]{1,0:T(2,128)} %virt.1, f32[2]{0:T(128)} %pair.1, ...), custom_call_target="tpu_custom_call" | custom-call | tf_op jit(solution)/shard_map/prepare/pallas_call | solution.py:360
  1.4 4.1 %collective-permute-start.1 = (bf16[144,256]{1,0:T(8,128)(2,1)S(1)}, bf16[144,256]{1,0:T(8,128)(2,1)S(1)}, u32[]{:S(2)}, u32[]{:S(2)}) collective-permute-start(bf16[144,256]{1,0:T(8,128)(2,1)S(1)} %get-tuple-element.25.own), channel_id=1, source_target_pairs={{0,16},{1,17},{2,18},{3,19},{4,20},{5,21},{6,22},{7,23},{8,24},{9,... | collective-permute-start | bytes 221192 | tf_op jit(solution)/shard_map/ppermute | solution.py:31
  5.5 1.5 %collective-permute-start.6 = (bf16[144,256]{1,0:T(8,128)(2,1)S(1)}, bf16[144,256]{1,0:T(8,128)(2,1)S(1)}, u32[]{:S(2)}, u32[]{:S(2)}) collective-permute-start(bf16[144,256]{1,0:T(8,128)(2,1)S(1)} %get-tuple-element.25.own), channel_id=1, source_target_pairs={{0,2},{1,3},{2,0},{3,1},{4,6},{5,7},{6,4},{7,5},{8,10},{9,11},{10,... | collective-permute-start | bytes 221192 | tf_op jit(solution)/shard_map/ppermute | solution.py:31
  7.0 1.5 %collective-permute-start.8 = (bf16[128,256]{1,0:T(8,128)(2,1)S(1)}, bf16[128,256]{1,0:T(8,128)(2,1)S(1)}, u32[]{:S(2)}, u32[]{:S(2)}) collective-permute-start(bf16[128,256]{1,0:T(8,128)(2,1)S(1)} %get-tuple-element.31.half_own), channel_id=1, source_target_pairs={{0,4},{1,21},{2,6},{3,23},{4,0},{5,17},{6,2},{7,19},{8,12},{9,29},... | collective-permute-start | bytes 196616 | tf_op jit(solution)/shard_map/ppermute | solution.py:40
  8.5 1.6 %collective-permute-start.9 = (bf16[128,256]{1,0:T(8,128)(2,1)S(1)}, bf16[128,256]{1,0:T(8,128)(2,1)S(1)}, u32[]{:S(2)}, u32[]{:S(2)}) collective-permute-start(bf16[128,256]{1,0:T(8,128)(2,1)S(1)} %get-tuple-element.31.half_own), channel_id=1, source_target_pairs={{0,8},{1,25},{2,10},{3,27},{4,12},{5,29},{6,14},{7,31},{8,0},{9,17... | collective-permute-start | bytes 196616 | tf_op jit(solution)/shard_map/ppermute | solution.py:40
  10.1 0.4 %collective-permute-start.10 = (bf16[128,256]{1,0:T(8,128)(2,1)S(1)}, bf16[128,256]{1,0:T(8,128)(2,1)S(1)}, u32[]{:S(2)}, u32[]{:S(2)}) collective-permute-start(bf16[128,256]{1,0:T(8,128)(2,1)S(1)} %get-tuple-element.31.half_own), channel_id=1, source_target_pairs={{0,12},{1,29},{2,14},{3,31},{4,8},{5,25},{6,10},{7,27},{8,4},{9,21... | collective-permute-start | bytes 196616 | tf_op jit(solution)/shard_map/ppermute | solution.py:40
  10.5 0.3 collective-permute-start.3
  10.8 2.1 %collective-permute-start.7 = (bf16[144,256]{1,0:T(8,128)(2,1)S(1)}, bf16[144,256]{1,0:T(8,128)(2,1)S(1)}, u32[]{:S(2)}, u32[]{:S(2)}) collective-permute-start(bf16[144,256]{1,0:T(8,128)(2,1)S(1)} %collective-permute-done.1.far), channel_id=1, source_target_pairs={{0,2},{1,3},{2,0},{3,1},{4,6},{5,7},{6,4},{7,5},{8,10},{9,11},{10,... | collective-permute-start | bytes 221192 | tf_op jit(solution)/shard_map/ppermute | solution.py:31
  13.0 1.0 %collective-permute-start.12 = (bf16[128,256]{1,0:T(8,128)(2,1)S(1)}, bf16[128,256]{1,0:T(8,128)(2,1)S(1)}, u32[]{:S(2)}, u32[]{:S(2)}) collective-permute-start(bf16[128,256]{1,0:T(8,128)(2,1)S(1)} %collective-permute-done.9.refs_3_), channel_id=1, source_target_pairs={{0,1},{1,0},{2,3},{3,2},{4,5},{5,4},{6,7},{7,6},{8,9},{9,8},{10,11... | collective-permute-start | bytes 196616 | tf_op jit(solution)/shard_map/ppermute | solution.py:31
  14.0 1.7 %collective-permute-done.10.refs_4_ = bf16[128,256]{1,0:T(8,128)(2,1)S(1)} collective-permute-done((bf16[128,256]{1,0:T(8,128)(2,1)S(1)}, bf16[128,256]{1,0:T(8,128)(2,1)S(1)}, u32[]{:S(2)}, u32[]{:S(2)}) %collective-permute-start.10) | collective-permute-done | bytes 65568 | tf_op jit(solution)/shard_map/ppermute | solution.py:40
  15.7 0.8 %collective-permute-start.13 = (bf16[128,256]{1,0:T(8,128)(2,1)S(1)}, bf16[128,256]{1,0:T(8,128)(2,1)S(1)}, u32[]{:S(2)}, u32[]{:S(2)}) collective-permute-start(bf16[128,256]{1,0:T(8,128)(2,1)S(1)} %collective-permute-done.10.refs_4_), channel_id=1, source_target_pairs={{0,1},{1,0},{2,3},{3,2},{4,5},{5,4},{6,7},{7,6},{8,9},{9,8},{10,11... | collective-permute-start | bytes 196616 | tf_op jit(solution)/shard_map/ppermute | solution.py:31
  16.5 0.5 %collective-permute-done.3.far_tail = bf16[80,256]{1,0:T(8,128)(2,1)S(1)} collective-permute-done((bf16[80,256]{1,0:T(8,128)(2,1)S(1)}, bf16[80,256]{1,0:T(8,128)(2,1)S(1)}, u32[]{:S(2)}, u32[]{:S(2)}) %collective-permute-start.3) | collective-permute-done | bytes 40992 | tf_op jit(solution)/shard_map/ppermute | solution.py:31
  17.0 1.2 %collective-permute-done.5.far_tail_c = bf16[80,256]{1,0:T(8,128)(2,1)S(1)} collective-permute-done((bf16[80,256]{1,0:T(8,128)(2,1)S(1)}, bf16[80,256]{1,0:T(8,128)(2,1)S(1)}, u32[]{:S(2)}, u32[]{:S(2)}) %collective-permute-start.5) | collective-permute-done | bytes 40992 | tf_op jit(solution)/shard_map/ppermute | solution.py:31
  18.2 0.8 %partials.1 = (bf16[256,256]{1,0:T(8,128)(2,1)S(1)}, bf16[256,256]{1,0:T(8,128)(2,1)S(1)}) custom-call(bf16[144,256]{1,0:T(8,128)(2,1)S(1)} %get-tuple-element.25.own, bf16[144,256]{1,0:T(8,128)(2,1)S(1)} %collective-permute-done.1.far, bf16[80,256]{1,0:T(8,128)(2,1)S(1)} %collective-permute-done.3.far_tail, ...), custom_call_target="tpu_custom_call" | custom-call | tf_op jit(solution)/shard_map/partials/pallas_call | solution.py:394
  19.0 0.2 collective-permute-start.14
  19.2 1.2 %collective-permute-start.4 = (bf16[128,256]{1,0:T(8,128)(2,1)S(1)}, bf16[128,256]{1,0:T(8,128)(2,1)S(1)}, u32[]{:S(2)}, u32[]{:S(2)}) collective-permute-start(bf16[128,256]{1,0:T(8,128)(2,1)S(1)} %get-tuple-element.27), channel_id=1, source_target_pairs={{0,16},{1,17},{2,18},{3,19},{4,20},{5,21},{6,22},{7,23},{8,24},{9,... | collective-permute-start | bytes 196616 | tf_op jit(solution)/shard_map/ppermute | solution.py:31
  20.4 0.0 collective-permute-done.14.given
  20.4 2.3 %collective-permute-start.15 = (bf16[256,256]{1,0:T(8,128)(2,1)S(1)}, bf16[256,256]{1,0:T(8,128)(2,1)S(1)}, u32[]{:S(2)}, u32[]{:S(2)}) collective-permute-start(bf16[256,256]{1,0:T(8,128)(2,1)S(1)} %joined.1.refs_0_), channel_id=1, source_target_pairs={{0,12},{1,13},{2,14},{3,15},{4,8},{5,9},{6,10},{7,11},{8,4},{9,5},... | collective-permute-start | bytes 393224 | tf_op jit(solution)/shard_map/ppermute | solution.py:31
  22.8 1.1 %collective-permute-start.16 = (bf16[256,256]{1,0:T(8,128)(2,1)S(1)}, bf16[256,256]{1,0:T(8,128)(2,1)S(1)}, u32[]{:S(2)}, u32[]{:S(2)}) collective-permute-start(bf16[256,256]{1,0:T(8,128)(2,1)S(1)} %joined.1.refs_0_), channel_id=1, source_target_pairs={{0,4},{1,5},{2,6},{3,7},{4,0},{5,1},{6,2},{7,3},{8,12},{9,13},{10,... | collective-permute-start | bytes 393224 | tf_op jit(solution)/shard_map/ppermute | solution.py:31
  23.9 0.1 collective-permute-start.17
  24.0 2.0 %collective-permute-done.4.resid_far = bf16[128,256]{1,0:T(8,128)(2,1)S(1)} collective-permute-done((bf16[128,256]{1,0:T(8,128)(2,1)S(1)}, bf16[128,256]{1,0:T(8,128)(2,1)S(1)}, u32[]{:S(2)}, u32[]{:S(2)}) %collective-permute-start.4) | collective-permute-done | bytes 65568 | tf_op jit(solution)/shard_map/ppermute | solution.py:31
  26.0 0.9 %near_factors.1 = (f32[2,256,256]{2,1,0:T(8,128)S(1)}, f32[2,64,256]{2,1,0:T(8,128)S(1)}) custom-call(f32[2,64,256]{2,1,0:T(8,128)} %resid.3, bf16[80,256]{1,0:T(8,128)(2,1)S(1)} %get-tuple-element.26.tail.own), custom_call_target="tpu_custom_call" | custom-call | flops 1000000000 | tf_op jit(solution)/shard_map/near_factors/pallas_call | solution.py:373
  26.9 0.3 collective-permute-done.2.far_c
  27.2 2.3 %factors.1 = (bf16[1024,512]{1,0:T(8,128)(2,1)S(1)}, bf16[512,1024]{1,0:T(8,128)(2,1)S(1)}, f32[2,256,256]{2,1,0:T(8,128)S(1)}, f32[2,256,256]{2,1,0:T(8,128)S(1)}, s32[2,8,128]{2,1,0:T(8,128)S(1)}) custom-call(bf16[144,256]{1,0:T(8,128)(2,1)S(1)} %get-tuple-element.25.own, bf16[144,256]{1,0:T(8,128)(2,1)S(1)} %collective-permute-done.own_c, ...), custom_call_target="tpu_custom_call" | custom-call | tf_op jit(solution)/shard_map/factors/pallas_call | solution.py:411
  29.6 0.5 %cycle_first.1 = (f32[256,512]{1,0:T(8,128)S(1)}, f32[512,256]{1,0:T(8,128)S(1)}) custom-call(bf16[144,256]{1,0:T(8,128)(2,1)S(1)} %get-tuple-element.25.own, bf16[144,256]{1,0:T(8,128)(2,1)S(1)} %collective-permute-done.own_c, bf16[144,256]{1,0:T(8,128)(2,1)S(1)} %collective-permute-done.1.far, bf16[144,256]{1,0:T(8,128)(2,1)S(1)} %collective-permute-done.2.far_c, ...), custom_call_target="tpu_custom_call" | custom-call | tf_op jit(solution)/shard_map/cycle_first/pallas_call | solution.py:427
  30.0 1.0 %collective-permute-done.17.refs_1_ = bf16[256,256]{1,0:T(8,128)(2,1)S(1)} collective-permute-done((bf16[256,256]{1,0:T(8,128)(2,1)S(1)}, bf16[256,256]{1,0:T(8,128)(2,1)S(1)}, u32[]{:S(2)}, u32[]{:S(2)}) %collective-permute-start.17) | collective-permute-done | bytes 131104 | tf_op jit(solution)/shard_map/ppermute | solution.py:31
  31.0 0.5 %cycle_last.1 = (f32[2,64,256]{2,1,0:T(8,128)S(1)}, bf16[2,64,256]{2,1,0:T(8,128)(2,1)S(1)}, bf16[2,64,256]{2,1,0:T(8,128)(2,1)S(1)}, bf16[2,64,256]{2,1,0:T(8,128)(2,1)S(1)}) custom-call(bf16[1024,512]{1,0:T(8,128)(2,1)S(1)} %get-tuple-element.28.z, bf16[512,1024]{1,0:T(8,128)(2,1)S(1)} %get-tuple-element.29.zt, f32[256,512]{1,0:T(8,128)S(1)} %get-tuple-element.35.near, ...), custom_call_target="tpu_custom_call" | custom-call | tf_op jit(solution)/shard_map/cycle_last/pallas_call | solution.py:433
  31.6 0.2 collective-permute-start.18
  31.8 0.8 %collective-permute-start.19 = (bf16[2,64,256]{2,1,0:T(8,128)(2,1)S(1)}, bf16[2,64,256]{2,1,0:T(8,128)(2,1)S(1)}, u32[]{:S(2)}, u32[]{:S(2)}) collective-permute-start(bf16[2,64,256]{2,1,0:T(8,128)(2,1)S(1)} %get-tuple-element.43), channel_id=1, source_target_pairs={{0,3},{1,2},{2,1},{3,0},{4,7},{5,6},{6,5},{7,4},{8,11},{9,10},{10,... | collective-permute-start | bytes 196616 | tf_op jit(solution)/shard_map/ppermute | solution.py:31
  32.6 1.2 %collective-permute-start.20 = (bf16[2,64,256]{2,1,0:T(8,128)(2,1)S(1)}, bf16[2,64,256]{2,1,0:T(8,128)(2,1)S(1)}, u32[]{:S(2)}, u32[]{:S(2)}) collective-permute-start(bf16[2,64,256]{2,1,0:T(8,128)(2,1)S(1)} %get-tuple-element.44), channel_id=1, source_target_pairs={{0,1},{1,0},{2,3},{3,2},{4,5},{5,4},{6,7},{7,6},{8,9},{9,8},{10,11... | collective-permute-start | bytes 196616 | tf_op jit(solution)/shard_map/ppermute | solution.py:31
  33.8 2.4 %collective-permute-done.18 = bf16[2,64,256]{2,1,0:T(8,128)(2,1)S(1)} collective-permute-done((bf16[2,64,256]{2,1,0:T(8,128)(2,1)S(1)}, bf16[2,64,256]{2,1,0:T(8,128)(2,1)S(1)}, u32[]{:S(2)}, u32[]{:S(2)}) %collective-permute-start.18) | collective-permute-done | bytes 65568 | tf_op jit(solution)/shard_map/ppermute | solution.py:31
  36.2 0.7 %add_multiply_fusion = f32[2,64,256]{2,1,0:T(8,128)} fusion(bf16[2,64,256]{2,1,0:T(8,128)(2,1)S(1)} %collective-permute-done.20, bf16[2,64,256]{2,1,0:T(8,128)(2,1)S(1)} %collective-permute-done.19, f32[2,64,256]{2,1,0:T(8,128)S(1)} %get-tuple-element.41, bf16[2,64,256]{2,1,0:T(8,128)(2,1)S(1)} %collective-permute-done.18), kind=kLoop, calls=%fused_computation | loop fusion | flops 229376 | bytes 458752 | tf_op jit(solution)/shard_map/mul | solution.py:442
  (18 shorter events, 0.1 us)
Async XLA Ops:
  1.4 9.1 %collective-permute-start.1 = (bf16[144,256]{1,0:T(8,128)(2,1)S(1)}, bf16[144,256]{1,0:T(8,128)(2,1)S(1)}, u32[]{:S(2)}, u32[]{:S(2)}) collective-permute-start(bf16[144,256]{1,0:T(8,128)(2,1)S(1)} %get-tuple-element.25.own), channel_id=1, source_target_pairs={{0,16},{1,17},{2,18},{3,19},{4,20},{5,21},{6,22},{7,23},{8,24},{9,... | collective-permute-start | bytes 221192 | tf_op jit(solution)/shard_map/ppermute | solution.py:31
  5.5 5.4 %collective-permute-start.6 = (bf16[144,256]{1,0:T(8,128)(2,1)S(1)}, bf16[144,256]{1,0:T(8,128)(2,1)S(1)}, u32[]{:S(2)}, u32[]{:S(2)}) collective-permute-start(bf16[144,256]{1,0:T(8,128)(2,1)S(1)} %get-tuple-element.25.own), channel_id=1, source_target_pairs={{0,2},{1,3},{2,0},{3,1},{4,6},{5,7},{6,4},{7,5},{8,10},{9,11},{10,... | collective-permute-start | bytes 221192 | tf_op jit(solution)/shard_map/ppermute | solution.py:31
  7.0 6.0 %collective-permute-start.8 = (bf16[128,256]{1,0:T(8,128)(2,1)S(1)}, bf16[128,256]{1,0:T(8,128)(2,1)S(1)}, u32[]{:S(2)}, u32[]{:S(2)}) collective-permute-start(bf16[128,256]{1,0:T(8,128)(2,1)S(1)} %get-tuple-element.31.half_own), channel_id=1, source_target_pairs={{0,4},{1,21},{2,6},{3,23},{4,0},{5,17},{6,2},{7,19},{8,12},{9,29},... | collective-permute-start | bytes 196616 | tf_op jit(solution)/shard_map/ppermute | solution.py:40
  8.5 4.5 %collective-permute-start.9 = (bf16[128,256]{1,0:T(8,128)(2,1)S(1)}, bf16[128,256]{1,0:T(8,128)(2,1)S(1)}, u32[]{:S(2)}, u32[]{:S(2)}) collective-permute-start(bf16[128,256]{1,0:T(8,128)(2,1)S(1)} %get-tuple-element.31.half_own), channel_id=1, source_target_pairs={{0,8},{1,25},{2,10},{3,27},{4,12},{5,29},{6,14},{7,31},{8,0},{9,17... | collective-permute-start | bytes 196616 | tf_op jit(solution)/shard_map/ppermute | solution.py:40
  10.1 5.6 %collective-permute-start.10 = (bf16[128,256]{1,0:T(8,128)(2,1)S(1)}, bf16[128,256]{1,0:T(8,128)(2,1)S(1)}, u32[]{:S(2)}, u32[]{:S(2)}) collective-permute-start(bf16[128,256]{1,0:T(8,128)(2,1)S(1)} %get-tuple-element.31.half_own), channel_id=1, source_target_pairs={{0,12},{1,29},{2,14},{3,31},{4,8},{5,25},{6,10},{7,27},{8,4},{9,21... | collective-permute-start | bytes 196616 | tf_op jit(solution)/shard_map/ppermute | solution.py:40
  10.5 6.5 %collective-permute-start.3 = (bf16[80,256]{1,0:T(8,128)(2,1)S(1)}, bf16[80,256]{1,0:T(8,128)(2,1)S(1)}, u32[]{:S(2)}, u32[]{:S(2)}) collective-permute-start(bf16[80,256]{1,0:T(8,128)(2,1)S(1)} %get-tuple-element.26.tail.own), channel_id=1, source_target_pairs={{0,16},{1,17},{2,18},{3,19},{4,20},{5,21},{6,22},{7,23},{8,24},{9,... | collective-permute-start | bytes 122888 | tf_op jit(solution)/shard_map/ppermute | solution.py:31
  10.8 7.4 %collective-permute-start.7 = (bf16[144,256]{1,0:T(8,128)(2,1)S(1)}, bf16[144,256]{1,0:T(8,128)(2,1)S(1)}, u32[]{:S(2)}, u32[]{:S(2)}) collective-permute-start(bf16[144,256]{1,0:T(8,128)(2,1)S(1)} %collective-permute-done.1.far), channel_id=1, source_target_pairs={{0,2},{1,3},{2,0},{3,1},{4,6},{5,7},{6,4},{7,5},{8,10},{9,11},{10,... | collective-permute-start | bytes 221192 | tf_op jit(solution)/shard_map/ppermute | solution.py:31
  13.0 5.2 %collective-permute-start.11 = (bf16[128,256]{1,0:T(8,128)(2,1)S(1)}, bf16[128,256]{1,0:T(8,128)(2,1)S(1)}, u32[]{:S(2)}, u32[]{:S(2)}) collective-permute-start(bf16[128,256]{1,0:T(8,128)(2,1)S(1)} %collective-permute-done.8.refs_2_), channel_id=1, source_target_pairs={{0,1},{1,0},{2,3},{3,2},{4,5},{5,4},{6,7},{7,6},{8,9},{9,8},{10,11... | collective-permute-start | bytes 196616 | tf_op jit(solution)/shard_map/ppermute | solution.py:31
  13.0 5.2 %collective-permute-start.12 = (bf16[128,256]{1,0:T(8,128)(2,1)S(1)}, bf16[128,256]{1,0:T(8,128)(2,1)S(1)}, u32[]{:S(2)}, u32[]{:S(2)}) collective-permute-start(bf16[128,256]{1,0:T(8,128)(2,1)S(1)} %collective-permute-done.9.refs_3_), channel_id=1, source_target_pairs={{0,1},{1,0},{2,3},{3,2},{4,5},{5,4},{6,7},{7,6},{8,9},{9,8},{10,11... | collective-permute-start | bytes 196616 | tf_op jit(solution)/shard_map/ppermute | solution.py:31
  15.7 2.5 %collective-permute-start.13 = (bf16[128,256]{1,0:T(8,128)(2,1)S(1)}, bf16[128,256]{1,0:T(8,128)(2,1)S(1)}, u32[]{:S(2)}, u32[]{:S(2)}) collective-permute-start(bf16[128,256]{1,0:T(8,128)(2,1)S(1)} %collective-permute-done.10.refs_4_), channel_id=1, source_target_pairs={{0,1},{1,0},{2,3},{3,2},{4,5},{5,4},{6,7},{7,6},{8,9},{9,8},{10,11... | collective-permute-start | bytes 196616 | tf_op jit(solution)/shard_map/ppermute | solution.py:31
  17.0 1.2 %collective-permute-start.5 = (bf16[80,256]{1,0:T(8,128)(2,1)S(1)}, bf16[80,256]{1,0:T(8,128)(2,1)S(1)}, u32[]{:S(2)}, u32[]{:S(2)}) collective-permute-start(bf16[80,256]{1,0:T(8,128)(2,1)S(1)} %collective-permute-done.3.far_tail), channel_id=1, source_target_pairs={{0,1},{1,0},{2,3},{3,2},{4,5},{5,4},{6,7},{7,6},{8,9},{9,8},{10,11... | collective-permute-start | bytes 122888 | tf_op jit(solution)/shard_map/ppermute | solution.py:31
  19.0 1.4 %collective-permute-start.14 = (bf16[256,256]{1,0:T(8,128)(2,1)S(1)}, bf16[256,256]{1,0:T(8,128)(2,1)S(1)}, u32[]{:S(2)}, u32[]{:S(2)}) collective-permute-start(bf16[256,256]{1,0:T(8,128)(2,1)S(1)} %get-tuple-element.34), channel_id=1, source_target_pairs={{0,1},{1,0},{2,3},{3,2},{4,5},{5,4},{6,7},{7,6},{8,9},{9,8},{10,11... | collective-permute-start | bytes 393224 | tf_op jit(solution)/shard_map/ppermute | solution.py:31
  19.2 6.8 %collective-permute-start.4 = (bf16[128,256]{1,0:T(8,128)(2,1)S(1)}, bf16[128,256]{1,0:T(8,128)(2,1)S(1)}, u32[]{:S(2)}, u32[]{:S(2)}) collective-permute-start(bf16[128,256]{1,0:T(8,128)(2,1)S(1)} %get-tuple-element.27), channel_id=1, source_target_pairs={{0,16},{1,17},{2,18},{3,19},{4,20},{5,21},{6,22},{7,23},{8,24},{9,... | collective-permute-start | bytes 196616 | tf_op jit(solution)/shard_map/ppermute | solution.py:31
  20.4 9.1 %collective-permute-start.15 = (bf16[256,256]{1,0:T(8,128)(2,1)S(1)}, bf16[256,256]{1,0:T(8,128)(2,1)S(1)}, u32[]{:S(2)}, u32[]{:S(2)}) collective-permute-start(bf16[256,256]{1,0:T(8,128)(2,1)S(1)} %joined.1.refs_0_), channel_id=1, source_target_pairs={{0,12},{1,13},{2,14},{3,15},{4,8},{5,9},{6,10},{7,11},{8,4},{9,5},... | collective-permute-start | bytes 393224 | tf_op jit(solution)/shard_map/ppermute | solution.py:31
  22.8 7.3 %collective-permute-start.16 = (bf16[256,256]{1,0:T(8,128)(2,1)S(1)}, bf16[256,256]{1,0:T(8,128)(2,1)S(1)}, u32[]{:S(2)}, u32[]{:S(2)}) collective-permute-start(bf16[256,256]{1,0:T(8,128)(2,1)S(1)} %joined.1.refs_0_), channel_id=1, source_target_pairs={{0,4},{1,5},{2,6},{3,7},{4,0},{5,1},{6,2},{7,3},{8,12},{9,13},{10,... | collective-permute-start | bytes 393224 | tf_op jit(solution)/shard_map/ppermute | solution.py:31
  23.9 7.2 %collective-permute-start.17 = (bf16[256,256]{1,0:T(8,128)(2,1)S(1)}, bf16[256,256]{1,0:T(8,128)(2,1)S(1)}, u32[]{:S(2)}, u32[]{:S(2)}) collective-permute-start(bf16[256,256]{1,0:T(8,128)(2,1)S(1)} %joined.1.refs_0_), channel_id=1, source_target_pairs={{0,8},{1,9},{2,10},{3,11},{4,12},{5,13},{6,14},{7,15},{8,0},{9,1},... | collective-permute-start | bytes 393224 | tf_op jit(solution)/shard_map/ppermute | solution.py:31
  24.0 2.9 %collective-permute-start = (bf16[144,256]{1,0:T(8,128)(2,1)S(1)}, bf16[144,256]{1,0:T(8,128)(2,1)S(1)}, u32[]{:S(2)}, u32[]{:S(2)}) collective-permute-start(bf16[144,256]{1,0:T(8,128)(2,1)S(1)} %get-tuple-element.25.own), channel_id=1, source_target_pairs={{0,1},{1,0},{2,3},{3,2},{4,5},{5,4},{6,7},{7,6},{8,9},{9,8},{10,11... | collective-permute-start | bytes 221192 | tf_op jit(solution)/shard_map/ppermute | solution.py:31
  26.0 1.3 %collective-permute-start.2 = (bf16[144,256]{1,0:T(8,128)(2,1)S(1)}, bf16[144,256]{1,0:T(8,128)(2,1)S(1)}, u32[]{:S(2)}, u32[]{:S(2)}) collective-permute-start(bf16[144,256]{1,0:T(8,128)(2,1)S(1)} %collective-permute-done.1.far), channel_id=1, source_target_pairs={{0,1},{1,0},{2,3},{3,2},{4,5},{5,4},{6,7},{7,6},{8,9},{9,8},{10,11... | collective-permute-start | bytes 221192 | tf_op jit(solution)/shard_map/ppermute | solution.py:31
  31.6 4.6 %collective-permute-start.18 = (bf16[2,64,256]{2,1,0:T(8,128)(2,1)S(1)}, bf16[2,64,256]{2,1,0:T(8,128)(2,1)S(1)}, u32[]{:S(2)}, u32[]{:S(2)}) collective-permute-start(bf16[2,64,256]{2,1,0:T(8,128)(2,1)S(1)} %get-tuple-element.42), channel_id=1, source_target_pairs={{0,2},{1,3},{2,0},{3,1},{4,6},{5,7},{6,4},{7,5},{8,10},{9,11},{10,... | collective-permute-start | bytes 196616 | tf_op jit(solution)/shard_map/ppermute | solution.py:31
  31.8 4.4 %collective-permute-start.19 = (bf16[2,64,256]{2,1,0:T(8,128)(2,1)S(1)}, bf16[2,64,256]{2,1,0:T(8,128)(2,1)S(1)}, u32[]{:S(2)}, u32[]{:S(2)}) collective-permute-start(bf16[2,64,256]{2,1,0:T(8,128)(2,1)S(1)} %get-tuple-element.43), channel_id=1, source_target_pairs={{0,3},{1,2},{2,1},{3,0},{4,7},{5,6},{6,5},{7,4},{8,11},{9,10},{10,... | collective-permute-start | bytes 196616 | tf_op jit(solution)/shard_map/ppermute | solution.py:31
  32.6 3.6 %collective-permute-start.20 = (bf16[2,64,256]{2,1,0:T(8,128)(2,1)S(1)}, bf16[2,64,256]{2,1,0:T(8,128)(2,1)S(1)}, u32[]{:S(2)}, u32[]{:S(2)}) collective-permute-start(bf16[2,64,256]{2,1,0:T(8,128)(2,1)S(1)} %get-tuple-element.44), channel_id=1, source_target_pairs={{0,1},{1,0},{2,3},{3,2},{4,5},{5,4},{6,7},{7,6},{8,9},{9,8},{10,11... | collective-permute-start | bytes 196616 | tf_op jit(solution)/shard_map/ppermute | solution.py:31

commit v6 on v5

--- a/solution.py
+++ b/solution.py
@@ -102,8 +102,8 @@
     return jnp.where(core == 0, own, other), jnp.where(core == 0, other, own)
 
 
-def partials(n_shared, items, pairs, own, far, far_tail, far_tail_c, half_own, *refs):
-    y_refs, rest, (keep_out, give_out) = refs[: 2 * n_shared], refs[2 * n_shared : -2], refs[-2:]
+def products(n_shared, items, pairs, own, far, half_own, *refs):
+    y_refs, rest, (product_out, ids_out) = refs[: 2 * n_shared], refs[2 * n_shared : -2], refs[-2:]
     half_rows, domain = half_own.shape
     height = half_rows // 2
     rows = pairs * height
@@ -137,8 +137,7 @@
 
     if len(rest) > 1:
         count = len(rest) // 2
-        mirror = jnp.concatenate(ordered(core, far_tail[TILE:, :], far_tail_c[TILE:, :]), axis=0)
-        product = chosen_two(jnp.zeros(ids.shape, F32), half_own[...], mirror, group, group ^ half)
+        product = chosen(half_own[...], group)
         for j in range(count):
             product = chosen_two(product, rest[j][...], rest[count + j][...], family ^ (j + 1), family ^ half ^ (j + 1))
     else:
@@ -148,6 +147,28 @@
             lambda k, sofar: sofar + chosen(rest[0][k], k),
             jnp.zeros(ids.shape, F32),
         )
+    product_out[...] = product
+    ids_out[...] = ids
+
+
+def partials(n_shared, pairs, direct, own, far, far_tail, far_tail_c, product, ids, *refs):
+    y_refs, (keep_out, give_out) = refs[: 2 * n_shared], refs[2 * n_shared :]
+    half_rows, domain = ids.shape[1], own.shape[1]
+    height = half_rows // 2
+    group, _, core, family, half = place()
+    near = [own] + list(y_refs[:n_shared])
+    away = [far] + list(y_refs[n_shared:])
+    x = [
+        jnp.concatenate([piece[p * height : (p + 1) * height, :] for piece in side], axis=0)
+        for side in (near, away)
+        for p in range(pairs)
+    ]
+    x_all = jnp.concatenate(x, axis=0)
+    deep = len(near) * height
+    product = product[...]
+    if direct:
+        mirror = jnp.concatenate(ordered(core, far_tail[TILE:, :], far_tail_c[TILE:, :]), axis=0)
+        product = jnp.where(ids[...] == (group ^ half), dot(x_all, mirror, NT), product)
     product = product.astype(BF16)
     for p in range(pairs):
         both = [
@@ -391,12 +412,19 @@
         blocks += [across(block) for block in blocks]
     else:
         blocks = [lax.all_gather(half_own, "pairs", axis=0, tiled=False)]
+    tall = shape((pairs * domain, half_rows), F32)
+    product, ids = call(
+        functools.partial(products, len(y_own), item_block.shape[0], pairs),
+        [tall, shape(tall.shape, jnp.int32)],
+        [VM] * (3 + len(y_own) + len(y_far) + len(blocks)),
+        "products",
+    )(lean, far, half_own, *y_own, *y_far, *blocks)
     keep, give = call(
-        functools.partial(partials, len(y_own), item_block.shape[0], pairs),
+        functools.partial(partials, len(y_own), pairs, n_pairs <= DIRECT),
         [shape((pairs * half_rows, domain), BF16)] * 2,
-        [VM] * (5 + len(y_own) + len(y_far) + len(blocks)),
+        [VM] * (6 + len(y_own) + len(y_far)),
         "partials",
-    )(lean, far, far_tail, far_tail_c, half_own, *y_own, *y_far, *blocks)
+    )(lean, far, far_tail, far_tail_c, product, ids, *y_own, *y_far)
     inter = call(joined, shape((pairs * half_rows, domain), BF16), [VM] * 2, "joined")(keep, across(give))
     own_c, far_c = across(lean), across(far)
     if n_pairs <= DIRECT:

time: 37.1 us -> 36.8 us (level)
  waiting for transfers between devices: 9.09 us -> 8.17 us
  starting transfers between devices: 20.6 us -> 21 us
    ppermute x18, waiting for transfers between devices: 7.42 us -> 6.5 us  [exchange(): return lax.ppermute(value, ('pairs', 'ints'), route)]
    ppermute x18, starting transfers between devices: 17.1 us -> 17.5 us  [exchange(): return lax.ppermute(value, ('pairs', 'ints'), route)]
    pallas_call x1 -> x2, Pallas kernels: 0.76 us -> 1.05 us  [the longest x1 0.53 us: body(): call(functools.partial(products, len(y_own), item_block.shape[0], pairs),...]
  transfers between devices with their start and end apart: 21 -> 21, of which waited for: 7 -> 9; matrix products, arithmetic and copies ran while one was open for 0% -> 0% of each run, Pallas kernels for 10% -> 12%
where the time goes in v6:
time: 36.8 us; the launch traced here: 36.7 us
  starting transfers between devices  21 us (57%)
  waiting for transfers between devices  8.17 us (22%)
  Pallas kernels  6.71 us (18%)
  other arithmetic  0.69 us (2%)
    ppermute x18, starting transfers between devices, exchange(): return lax.ppermute(value, ('pairs', 'ints'), route)  17.5 us
    ppermute x18, waiting for transfers between devices, exchange(): return lax.ppermute(value, ('pairs', 'ints'), route)  6.5 us
    ppermute x3, starting transfers between devices, family_exchange(): return lax.ppermute(value, ('pairs', 'ints'), route)  3.49 us
    pallas_call x1, Pallas kernels, body(): call(functools.partial(factors, planned, pairs), [shape((n_units * wide,...  2.3 us
    ppermute x3, waiting for transfers between devices, family_exchange(): return lax.ppermute(value, ('pairs', 'ints'), route)  1.67 us
    pallas_call x1, Pallas kernels, body(): call(prepare, [shape((rows + TILE, domain), BF16), shape((half_rows, doma...  1.39 us
    pallas_call x1, Pallas kernels, body(): call(near_factors, [shape((pairs, domain, domain), F32), shape((pairs, he...  0.93 us
  transfers between devices with their start and end apart: 21, of which 9 were waited for; matrix products, arithmetic and copies ran while one was open for 0% of the time, Pallas kernels for 12%

profile of v6, /device:TPU:0, one launch (start us, length us, event | category | flops | bytes accessed | tf_op | source)
XLA Modules:
  0.0 36.7 jit_solution(11284918334491504844)
XLA Ops:
  0.0 1.4 %prepare.1 = (bf16[144,256]{1,0:T(8,128)(2,1)S(1)}, bf16[128,256]{1,0:T(8,128)(2,1)S(1)}, bf16[80,256]{1,0:T(8,128)(2,1)S(1)}, bf16[128,256]{1,0:T(8,128)(2,1)S(1)}) custom-call(f32[2,64,256]{2,1,0:T(8,128)} %amps.1, bf16[1,256,256]{2,1,0:T(8,128)(2,1)} %block.1, f32[2,64,256]{2,1,0:T(8,128)} %resid.3, f32[2,256]{1,0:T(2,128)} %virt.1, f32[2]{0:T(128)} %pair.1, ...), custom_call_target="tpu_custom_call" | custom-call | tf_op jit(solution)/shard_map/prepare/pallas_call | solution.py:381
  1.4 4.1 %collective-permute-start.1 = (bf16[144,256]{1,0:T(8,128)(2,1)S(1)}, bf16[144,256]{1,0:T(8,128)(2,1)S(1)}, u32[]{:S(2)}, u32[]{:S(2)}) collective-permute-start(bf16[144,256]{1,0:T(8,128)(2,1)S(1)} %get-tuple-element.27.own), channel_id=1, source_target_pairs={{0,16},{1,17},{2,18},{3,19},{4,20},{5,21},{6,22},{7,23},{8,24},{9,... | collective-permute-start | bytes 221192 | tf_op jit(solution)/shard_map/ppermute | solution.py:31
  5.5 1.5 %collective-permute-start.6 = (bf16[144,256]{1,0:T(8,128)(2,1)S(1)}, bf16[144,256]{1,0:T(8,128)(2,1)S(1)}, u32[]{:S(2)}, u32[]{:S(2)}) collective-permute-start(bf16[144,256]{1,0:T(8,128)(2,1)S(1)} %get-tuple-element.27.own), channel_id=1, source_target_pairs={{0,2},{1,3},{2,0},{3,1},{4,6},{5,7},{6,4},{7,5},{8,10},{9,11},{10,... | collective-permute-start | bytes 221192 | tf_op jit(solution)/shard_map/ppermute | solution.py:31
  7.0 1.5 %collective-permute-start.8 = (bf16[128,256]{1,0:T(8,128)(2,1)S(1)}, bf16[128,256]{1,0:T(8,128)(2,1)S(1)}, u32[]{:S(2)}, u32[]{:S(2)}) collective-permute-start(bf16[128,256]{1,0:T(8,128)(2,1)S(1)} %get-tuple-element.33.half_own), channel_id=1, source_target_pairs={{0,4},{1,21},{2,6},{3,23},{4,0},{5,17},{6,2},{7,19},{8,12},{9,29},... | collective-permute-start | bytes 196616 | tf_op jit(solution)/shard_map/ppermute | solution.py:40
  8.5 1.6 %collective-permute-start.9 = (bf16[128,256]{1,0:T(8,128)(2,1)S(1)}, bf16[128,256]{1,0:T(8,128)(2,1)S(1)}, u32[]{:S(2)}, u32[]{:S(2)}) collective-permute-start(bf16[128,256]{1,0:T(8,128)(2,1)S(1)} %get-tuple-element.33.half_own), channel_id=1, source_target_pairs={{0,8},{1,25},{2,10},{3,27},{4,12},{5,29},{6,14},{7,31},{8,0},{9,17... | collective-permute-start | bytes 196616 | tf_op jit(solution)/shard_map/ppermute | solution.py:40
  10.1 0.4 %collective-permute-start.10 = (bf16[128,256]{1,0:T(8,128)(2,1)S(1)}, bf16[128,256]{1,0:T(8,128)(2,1)S(1)}, u32[]{:S(2)}, u32[]{:S(2)}) collective-permute-start(bf16[128,256]{1,0:T(8,128)(2,1)S(1)} %get-tuple-element.33.half_own), channel_id=1, source_target_pairs={{0,12},{1,29},{2,14},{3,31},{4,8},{5,25},{6,10},{7,27},{8,4},{9,21... | collective-permute-start | bytes 196616 | tf_op jit(solution)/shard_map/ppermute | solution.py:40
  10.5 0.3 collective-permute-start.3
  10.8 2.1 %collective-permute-start.7 = (bf16[144,256]{1,0:T(8,128)(2,1)S(1)}, bf16[144,256]{1,0:T(8,128)(2,1)S(1)}, u32[]{:S(2)}, u32[]{:S(2)}) collective-permute-start(bf16[144,256]{1,0:T(8,128)(2,1)S(1)} %collective-permute-done.1.far), channel_id=1, source_target_pairs={{0,2},{1,3},{2,0},{3,1},{4,6},{5,7},{6,4},{7,5},{8,10},{9,11},{10,... | collective-permute-start | bytes 221192 | tf_op jit(solution)/shard_map/ppermute | solution.py:31
  13.0 1.0 %collective-permute-start.12 = (bf16[128,256]{1,0:T(8,128)(2,1)S(1)}, bf16[128,256]{1,0:T(8,128)(2,1)S(1)}, u32[]{:S(2)}, u32[]{:S(2)}) collective-permute-start(bf16[128,256]{1,0:T(8,128)(2,1)S(1)} %collective-permute-done.9.refs_3_), channel_id=1, source_target_pairs={{0,1},{1,0},{2,3},{3,2},{4,5},{5,4},{6,7},{7,6},{8,9},{9,8},{10,11... | collective-permute-start | bytes 196616 | tf_op jit(solution)/shard_map/ppermute | solution.py:31
  14.0 1.7 %collective-permute-done.10.refs_4_ = bf16[128,256]{1,0:T(8,128)(2,1)S(1)} collective-permute-done((bf16[128,256]{1,0:T(8,128)(2,1)S(1)}, bf16[128,256]{1,0:T(8,128)(2,1)S(1)}, u32[]{:S(2)}, u32[]{:S(2)}) %collective-permute-start.10) | collective-permute-done | bytes 65568 | tf_op jit(solution)/shard_map/ppermute | solution.py:40
  15.7 0.8 %collective-permute-start.13 = (bf16[128,256]{1,0:T(8,128)(2,1)S(1)}, bf16[128,256]{1,0:T(8,128)(2,1)S(1)}, u32[]{:S(2)}, u32[]{:S(2)}) collective-permute-start(bf16[128,256]{1,0:T(8,128)(2,1)S(1)} %collective-permute-done.10.refs_4_), channel_id=1, source_target_pairs={{0,1},{1,0},{2,3},{3,2},{4,5},{5,4},{6,7},{7,6},{8,9},{9,8},{10,11... | collective-permute-start | bytes 196616 | tf_op jit(solution)/shard_map/ppermute | solution.py:31
  16.5 0.5 %collective-permute-done.3.far_tail = bf16[80,256]{1,0:T(8,128)(2,1)S(1)} collective-permute-done((bf16[80,256]{1,0:T(8,128)(2,1)S(1)}, bf16[80,256]{1,0:T(8,128)(2,1)S(1)}, u32[]{:S(2)}, u32[]{:S(2)}) %collective-permute-start.3) | collective-permute-done | bytes 40992 | tf_op jit(solution)/shard_map/ppermute | solution.py:31
  17.0 0.4 %collective-permute-done.13.refs_7_ = bf16[128,256]{1,0:T(8,128)(2,1)S(1)} collective-permute-done((bf16[128,256]{1,0:T(8,128)(2,1)S(1)}, bf16[128,256]{1,0:T(8,128)(2,1)S(1)}, u32[]{:S(2)}, u32[]{:S(2)}) %collective-permute-start.13) | collective-permute-done | bytes 65568 | tf_op jit(solution)/shard_map/ppermute | solution.py:31
  17.4 0.5 %products.1 = (f32[512,128]{1,0:T(8,128)S(1)}, s32[512,128]{1,0:T(8,128)S(1)}) custom-call(bf16[144,256]{1,0:T(8,128)(2,1)S(1)} %get-tuple-element.27.own, bf16[144,256]{1,0:T(8,128)(2,1)S(1)} %collective-permute-done.1.far, bf16[128,256]{1,0:T(8,128)(2,1)S(1)} %get-tuple-element.33.half_own, bf16[144,256]{1,0:T(8,128)(2,1)S(1)} %collective-permute-done.6.refs_0_, ...), custom_call_target="tpu_custom_call" | custom-call | tf_op jit(solution)/shard_map/products/pallas_call | solution.py:416
  18.2 0.5 %partials.1 = (bf16[256,256]{1,0:T(8,128)(2,1)S(1)}, bf16[256,256]{1,0:T(8,128)(2,1)S(1)}) custom-call(bf16[144,256]{1,0:T(8,128)(2,1)S(1)} %get-tuple-element.27.own, bf16[144,256]{1,0:T(8,128)(2,1)S(1)} %collective-permute-done.1.far, bf16[80,256]{1,0:T(8,128)(2,1)S(1)} %collective-permute-done.3.far_tail, ...), custom_call_target="tpu_custom_call" | custom-call | tf_op jit(solution)/shard_map/partials/pallas_call | solution.py:422
  19.0 1.6 %collective-permute-start.4 = (bf16[128,256]{1,0:T(8,128)(2,1)S(1)}, bf16[128,256]{1,0:T(8,128)(2,1)S(1)}, u32[]{:S(2)}, u32[]{:S(2)}) collective-permute-start(bf16[128,256]{1,0:T(8,128)(2,1)S(1)} %get-tuple-element.29), channel_id=1, source_target_pairs={{0,16},{1,17},{2,18},{3,19},{4,20},{5,21},{6,22},{7,23},{8,24},{9,... | collective-permute-start | bytes 196616 | tf_op jit(solution)/shard_map/ppermute | solution.py:31
  20.6 1.9 %collective-permute-start.15 = (bf16[256,256]{1,0:T(8,128)(2,1)S(1)}, bf16[256,256]{1,0:T(8,128)(2,1)S(1)}, u32[]{:S(2)}, u32[]{:S(2)}) collective-permute-start(bf16[256,256]{1,0:T(8,128)(2,1)S(1)} %joined.1.refs_0_), channel_id=1, source_target_pairs={{0,12},{1,13},{2,14},{3,15},{4,8},{5,9},{6,10},{7,11},{8,4},{9,5},... | collective-permute-start | bytes 393224 | tf_op jit(solution)/shard_map/ppermute | solution.py:31
  22.5 1.1 %collective-permute-start.16 = (bf16[256,256]{1,0:T(8,128)(2,1)S(1)}, bf16[256,256]{1,0:T(8,128)(2,1)S(1)}, u32[]{:S(2)}, u32[]{:S(2)}) collective-permute-start(bf16[256,256]{1,0:T(8,128)(2,1)S(1)} %joined.1.refs_0_), channel_id=1, source_target_pairs={{0,4},{1,5},{2,6},{3,7},{4,0},{5,1},{6,2},{7,3},{8,12},{9,13},{10,... | collective-permute-start | bytes 393224 | tf_op jit(solution)/shard_map/ppermute | solution.py:31
  23.6 0.5 %collective-permute-start.17 = (bf16[256,256]{1,0:T(8,128)(2,1)S(1)}, bf16[256,256]{1,0:T(8,128)(2,1)S(1)}, u32[]{:S(2)}, u32[]{:S(2)}) collective-permute-start(bf16[256,256]{1,0:T(8,128)(2,1)S(1)} %joined.1.refs_0_), channel_id=1, source_target_pairs={{0,8},{1,9},{2,10},{3,11},{4,12},{5,13},{6,14},{7,15},{8,0},{9,1},... | collective-permute-start | bytes 393224 | tf_op jit(solution)/shard_map/ppermute | solution.py:31
  24.2 1.6 %collective-permute-done.4.resid_far = bf16[128,256]{1,0:T(8,128)(2,1)S(1)} collective-permute-done((bf16[128,256]{1,0:T(8,128)(2,1)S(1)}, bf16[128,256]{1,0:T(8,128)(2,1)S(1)}, u32[]{:S(2)}, u32[]{:S(2)}) %collective-permute-start.4) | collective-permute-done | bytes 65568 | tf_op jit(solution)/shard_map/ppermute | solution.py:31
  25.7 0.9 %near_factors.1 = (f32[2,256,256]{2,1,0:T(8,128)S(1)}, f32[2,64,256]{2,1,0:T(8,128)S(1)}) custom-call(f32[2,64,256]{2,1,0:T(8,128)} %resid.3, bf16[80,256]{1,0:T(8,128)(2,1)S(1)} %get-tuple-element.28.tail.own), custom_call_target="tpu_custom_call" | custom-call | flops 1000000000 | tf_op jit(solution)/shard_map/near_factors/pallas_call | solution.py:394
  26.7 0.3 collective-permute-done.2.far_c
  27.0 2.3 %factors.1 = (bf16[1024,512]{1,0:T(8,128)(2,1)S(1)}, bf16[512,1024]{1,0:T(8,128)(2,1)S(1)}, f32[2,256,256]{2,1,0:T(8,128)S(1)}, f32[2,256,256]{2,1,0:T(8,128)S(1)}, s32[2,8,128]{2,1,0:T(8,128)S(1)}) custom-call(bf16[144,256]{1,0:T(8,128)(2,1)S(1)} %get-tuple-element.27.own, bf16[144,256]{1,0:T(8,128)(2,1)S(1)} %collective-permute-done.own_c, ...), custom_call_target="tpu_custom_call" | custom-call | tf_op jit(solution)/shard_map/factors/pallas_call | solution.py:439
  29.3 0.5 %cycle_first.1 = (f32[256,512]{1,0:T(8,128)S(1)}, f32[512,256]{1,0:T(8,128)S(1)}) custom-call(bf16[144,256]{1,0:T(8,128)(2,1)S(1)} %get-tuple-element.27.own, bf16[144,256]{1,0:T(8,128)(2,1)S(1)} %collective-permute-done.own_c, bf16[144,256]{1,0:T(8,128)(2,1)S(1)} %collective-permute-done.1.far, bf16[144,256]{1,0:T(8,128)(2,1)S(1)} %collective-permute-done.2.far_c, ...), custom_call_target="tpu_custom_call" | custom-call | tf_op jit(solution)/shard_map/cycle_first/pallas_call | solution.py:455
  29.8 0.4 %collective-permute-done.16.refs_0_ = bf16[256,256]{1,0:T(8,128)(2,1)S(1)} collective-permute-done((bf16[256,256]{1,0:T(8,128)(2,1)S(1)}, bf16[256,256]{1,0:T(8,128)(2,1)S(1)}, u32[]{:S(2)}, u32[]{:S(2)}) %collective-permute-start.16) | collective-permute-done | bytes 131104 | tf_op jit(solution)/shard_map/ppermute | solution.py:31
  30.2 0.6 %cycle_last.1 = (f32[2,64,256]{2,1,0:T(8,128)S(1)}, bf16[2,64,256]{2,1,0:T(8,128)(2,1)S(1)}, bf16[2,64,256]{2,1,0:T(8,128)(2,1)S(1)}, bf16[2,64,256]{2,1,0:T(8,128)(2,1)S(1)}) custom-call(bf16[1024,512]{1,0:T(8,128)(2,1)S(1)} %get-tuple-element.30.z, bf16[512,1024]{1,0:T(8,128)(2,1)S(1)} %get-tuple-element.31.zt, f32[256,512]{1,0:T(8,128)S(1)} %get-tuple-element.39.near, ...), custom_call_target="tpu_custom_call" | custom-call | tf_op jit(solution)/shard_map/cycle_last/pallas_call | solution.py:461
  30.8 0.8 %collective-permute-start.18 = (bf16[2,64,256]{2,1,0:T(8,128)(2,1)S(1)}, bf16[2,64,256]{2,1,0:T(8,128)(2,1)S(1)}, u32[]{:S(2)}, u32[]{:S(2)}) collective-permute-start(bf16[2,64,256]{2,1,0:T(8,128)(2,1)S(1)} %get-tuple-element.46), channel_id=1, source_target_pairs={{0,2},{1,3},{2,0},{3,1},{4,6},{5,7},{6,4},{7,5},{8,10},{9,11},{10,... | collective-permute-start | bytes 196616 | tf_op jit(solution)/shard_map/ppermute | solution.py:31
  31.6 0.5 %collective-permute-start.19 = (bf16[2,64,256]{2,1,0:T(8,128)(2,1)S(1)}, bf16[2,64,256]{2,1,0:T(8,128)(2,1)S(1)}, u32[]{:S(2)}, u32[]{:S(2)}) collective-permute-start(bf16[2,64,256]{2,1,0:T(8,128)(2,1)S(1)} %get-tuple-element.47), channel_id=1, source_target_pairs={{0,3},{1,2},{2,1},{3,0},{4,7},{5,6},{6,5},{7,4},{8,11},{9,10},{10,... | collective-permute-start | bytes 196616 | tf_op jit(solution)/shard_map/ppermute | solution.py:31
  32.1 0.9 %collective-permute-start.20 = (bf16[2,64,256]{2,1,0:T(8,128)(2,1)S(1)}, bf16[2,64,256]{2,1,0:T(8,128)(2,1)S(1)}, u32[]{:S(2)}, u32[]{:S(2)}) collective-permute-start(bf16[2,64,256]{2,1,0:T(8,128)(2,1)S(1)} %get-tuple-element.48), channel_id=1, source_target_pairs={{0,1},{1,0},{2,3},{3,2},{4,5},{5,4},{6,7},{7,6},{8,9},{9,8},{10,11... | collective-permute-start | bytes 196616 | tf_op jit(solution)/shard_map/ppermute | solution.py:31
  33.0 2.6 %collective-permute-done.18 = bf16[2,64,256]{2,1,0:T(8,128)(2,1)S(1)} collective-permute-done((bf16[2,64,256]{2,1,0:T(8,128)(2,1)S(1)}, bf16[2,64,256]{2,1,0:T(8,128)(2,1)S(1)}, u32[]{:S(2)}, u32[]{:S(2)}) %collective-permute-start.18) | collective-permute-done | bytes 65568 | tf_op jit(solution)/shard_map/ppermute | solution.py:31
  35.6 0.4 %collective-permute-done.19 = bf16[2,64,256]{2,1,0:T(8,128)(2,1)S(1)} collective-permute-done((bf16[2,64,256]{2,1,0:T(8,128)(2,1)S(1)}, bf16[2,64,256]{2,1,0:T(8,128)(2,1)S(1)}, u32[]{:S(2)}, u32[]{:S(2)}) %collective-permute-start.19) | collective-permute-done | bytes 65568 | tf_op jit(solution)/shard_map/ppermute | solution.py:31
  36.0 0.7 %add_multiply_fusion = f32[2,64,256]{2,1,0:T(8,128)} fusion(bf16[2,64,256]{2,1,0:T(8,128)(2,1)S(1)} %collective-permute-done.20, bf16[2,64,256]{2,1,0:T(8,128)(2,1)S(1)} %collective-permute-done.19, f32[2,64,256]{2,1,0:T(8,128)S(1)} %get-tuple-element.45, bf16[2,64,256]{2,1,0:T(8,128)(2,1)S(1)} %collective-permute-done.18), kind=kLoop, calls=%fused_computation | loop fusion | flops 229376 | bytes 458752 | tf_op jit(solution)/shard_map/mul | solution.py:470
  (19 shorter events, 0.6 us)
Async XLA Ops:
  1.4 9.1 %collective-permute-start.1 = (bf16[144,256]{1,0:T(8,128)(2,1)S(1)}, bf16[144,256]{1,0:T(8,128)(2,1)S(1)}, u32[]{:S(2)}, u32[]{:S(2)}) collective-permute-start(bf16[144,256]{1,0:T(8,128)(2,1)S(1)} %get-tuple-element.27.own), channel_id=1, source_target_pairs={{0,16},{1,17},{2,18},{3,19},{4,20},{5,21},{6,22},{7,23},{8,24},{9,... | collective-permute-start | bytes 221192 | tf_op jit(solution)/shard_map/ppermute | solution.py:31
  5.5 5.4 %collective-permute-start.6 = (bf16[144,256]{1,0:T(8,128)(2,1)S(1)}, bf16[144,256]{1,0:T(8,128)(2,1)S(1)}, u32[]{:S(2)}, u32[]{:S(2)}) collective-permute-start(bf16[144,256]{1,0:T(8,128)(2,1)S(1)} %get-tuple-element.27.own), channel_id=1, source_target_pairs={{0,2},{1,3},{2,0},{3,1},{4,6},{5,7},{6,4},{7,5},{8,10},{9,11},{10,... | collective-permute-start | bytes 221192 | tf_op jit(solution)/shard_map/ppermute | solution.py:31
  7.0 6.0 %collective-permute-start.8 = (bf16[128,256]{1,0:T(8,128)(2,1)S(1)}, bf16[128,256]{1,0:T(8,128)(2,1)S(1)}, u32[]{:S(2)}, u32[]{:S(2)}) collective-permute-start(bf16[128,256]{1,0:T(8,128)(2,1)S(1)} %get-tuple-element.33.half_own), channel_id=1, source_target_pairs={{0,4},{1,21},{2,6},{3,23},{4,0},{5,17},{6,2},{7,19},{8,12},{9,29},... | collective-permute-start | bytes 196616 | tf_op jit(solution)/shard_map/ppermute | solution.py:40
  8.5 4.5 %collective-permute-start.9 = (bf16[128,256]{1,0:T(8,128)(2,1)S(1)}, bf16[128,256]{1,0:T(8,128)(2,1)S(1)}, u32[]{:S(2)}, u32[]{:S(2)}) collective-permute-start(bf16[128,256]{1,0:T(8,128)(2,1)S(1)} %get-tuple-element.33.half_own), channel_id=1, source_target_pairs={{0,8},{1,25},{2,10},{3,27},{4,12},{5,29},{6,14},{7,31},{8,0},{9,17... | collective-permute-start | bytes 196616 | tf_op jit(solution)/shard_map/ppermute | solution.py:40
  10.1 5.6 %collective-permute-start.10 = (bf16[128,256]{1,0:T(8,128)(2,1)S(1)}, bf16[128,256]{1,0:T(8,128)(2,1)S(1)}, u32[]{:S(2)}, u32[]{:S(2)}) collective-permute-start(bf16[128,256]{1,0:T(8,128)(2,1)S(1)} %get-tuple-element.33.half_own), channel_id=1, source_target_pairs={{0,12},{1,29},{2,14},{3,31},{4,8},{5,25},{6,10},{7,27},{8,4},{9,21... | collective-permute-start | bytes 196616 | tf_op jit(solution)/shard_map/ppermute | solution.py:40
  10.5 6.5 %collective-permute-start.3 = (bf16[80,256]{1,0:T(8,128)(2,1)S(1)}, bf16[80,256]{1,0:T(8,128)(2,1)S(1)}, u32[]{:S(2)}, u32[]{:S(2)}) collective-permute-start(bf16[80,256]{1,0:T(8,128)(2,1)S(1)} %get-tuple-element.28.tail.own), channel_id=1, source_target_pairs={{0,16},{1,17},{2,18},{3,19},{4,20},{5,21},{6,22},{7,23},{8,24},{9,... | collective-permute-start | bytes 122888 | tf_op jit(solution)/shard_map/ppermute | solution.py:31
  10.8 6.5 %collective-permute-start.7 = (bf16[144,256]{1,0:T(8,128)(2,1)S(1)}, bf16[144,256]{1,0:T(8,128)(2,1)S(1)}, u32[]{:S(2)}, u32[]{:S(2)}) collective-permute-start(bf16[144,256]{1,0:T(8,128)(2,1)S(1)} %collective-permute-done.1.far), channel_id=1, source_target_pairs={{0,2},{1,3},{2,0},{3,1},{4,6},{5,7},{6,4},{7,5},{8,10},{9,11},{10,... | collective-permute-start | bytes 221192 | tf_op jit(solution)/shard_map/ppermute | solution.py:31
  13.0 4.0 %collective-permute-start.11 = (bf16[128,256]{1,0:T(8,128)(2,1)S(1)}, bf16[128,256]{1,0:T(8,128)(2,1)S(1)}, u32[]{:S(2)}, u32[]{:S(2)}) collective-permute-start(bf16[128,256]{1,0:T(8,128)(2,1)S(1)} %collective-permute-done.8.refs_2_), channel_id=1, source_target_pairs={{0,1},{1,0},{2,3},{3,2},{4,5},{5,4},{6,7},{7,6},{8,9},{9,8},{10,11... | collective-permute-start | bytes 196616 | tf_op jit(solution)/shard_map/ppermute | solution.py:31
  13.0 4.0 %collective-permute-start.12 = (bf16[128,256]{1,0:T(8,128)(2,1)S(1)}, bf16[128,256]{1,0:T(8,128)(2,1)S(1)}, u32[]{:S(2)}, u32[]{:S(2)}) collective-permute-start(bf16[128,256]{1,0:T(8,128)(2,1)S(1)} %collective-permute-done.9.refs_3_), channel_id=1, source_target_pairs={{0,1},{1,0},{2,3},{3,2},{4,5},{5,4},{6,7},{7,6},{8,9},{9,8},{10,11... | collective-permute-start | bytes 196616 | tf_op jit(solution)/shard_map/ppermute | solution.py:31
  15.7 1.7 %collective-permute-start.13 = (bf16[128,256]{1,0:T(8,128)(2,1)S(1)}, bf16[128,256]{1,0:T(8,128)(2,1)S(1)}, u32[]{:S(2)}, u32[]{:S(2)}) collective-permute-start(bf16[128,256]{1,0:T(8,128)(2,1)S(1)} %collective-permute-done.10.refs_4_), channel_id=1, source_target_pairs={{0,1},{1,0},{2,3},{3,2},{4,5},{5,4},{6,7},{7,6},{8,9},{9,8},{10,11... | collective-permute-start | bytes 196616 | tf_op jit(solution)/shard_map/ppermute | solution.py:31
  17.0 1.2 %collective-permute-start.5 = (bf16[80,256]{1,0:T(8,128)(2,1)S(1)}, bf16[80,256]{1,0:T(8,128)(2,1)S(1)}, u32[]{:S(2)}, u32[]{:S(2)}) collective-permute-start(bf16[80,256]{1,0:T(8,128)(2,1)S(1)} %collective-permute-done.3.far_tail), channel_id=1, source_target_pairs={{0,1},{1,0},{2,3},{3,2},{4,5},{5,4},{6,7},{7,6},{8,9},{9,8},{10,11... | collective-permute-start | bytes 122888 | tf_op jit(solution)/shard_map/ppermute | solution.py:31
  18.7 1.8 %collective-permute-start.14 = (bf16[256,256]{1,0:T(8,128)(2,1)S(1)}, bf16[256,256]{1,0:T(8,128)(2,1)S(1)}, u32[]{:S(2)}, u32[]{:S(2)}) collective-permute-start(bf16[256,256]{1,0:T(8,128)(2,1)S(1)} %get-tuple-element.38), channel_id=1, source_target_pairs={{0,1},{1,0},{2,3},{3,2},{4,5},{5,4},{6,7},{7,6},{8,9},{9,8},{10,11... | collective-permute-start | bytes 393224 | tf_op jit(solution)/shard_map/ppermute | solution.py:31
  19.0 6.8 %collective-permute-start.4 = (bf16[128,256]{1,0:T(8,128)(2,1)S(1)}, bf16[128,256]{1,0:T(8,128)(2,1)S(1)}, u32[]{:S(2)}, u32[]{:S(2)}) collective-permute-start(bf16[128,256]{1,0:T(8,128)(2,1)S(1)} %get-tuple-element.29), channel_id=1, source_target_pairs={{0,16},{1,17},{2,18},{3,19},{4,20},{5,21},{6,22},{7,23},{8,24},{9,... | collective-permute-start | bytes 196616 | tf_op jit(solution)/shard_map/ppermute | solution.py:31
  20.6 8.7 %collective-permute-start.15 = (bf16[256,256]{1,0:T(8,128)(2,1)S(1)}, bf16[256,256]{1,0:T(8,128)(2,1)S(1)}, u32[]{:S(2)}, u32[]{:S(2)}) collective-permute-start(bf16[256,256]{1,0:T(8,128)(2,1)S(1)} %joined.1.refs_0_), channel_id=1, source_target_pairs={{0,12},{1,13},{2,14},{3,15},{4,8},{5,9},{6,10},{7,11},{8,4},{9,5},... | collective-permute-start | bytes 393224 | tf_op jit(solution)/shard_map/ppermute | solution.py:31
  22.5 7.7 %collective-permute-start.16 = (bf16[256,256]{1,0:T(8,128)(2,1)S(1)}, bf16[256,256]{1,0:T(8,128)(2,1)S(1)}, u32[]{:S(2)}, u32[]{:S(2)}) collective-permute-start(bf16[256,256]{1,0:T(8,128)(2,1)S(1)} %joined.1.refs_0_), channel_id=1, source_target_pairs={{0,4},{1,5},{2,6},{3,7},{4,0},{5,1},{6,2},{7,3},{8,12},{9,13},{10,... | collective-permute-start | bytes 393224 | tf_op jit(solution)/shard_map/ppermute | solution.py:31
  23.6 6.6 %collective-permute-start.17 = (bf16[256,256]{1,0:T(8,128)(2,1)S(1)}, bf16[256,256]{1,0:T(8,128)(2,1)S(1)}, u32[]{:S(2)}, u32[]{:S(2)}) collective-permute-start(bf16[256,256]{1,0:T(8,128)(2,1)S(1)} %joined.1.refs_0_), channel_id=1, source_target_pairs={{0,8},{1,9},{2,10},{3,11},{4,12},{5,13},{6,14},{7,15},{8,0},{9,1},... | collective-permute-start | bytes 393224 | tf_op jit(solution)/shard_map/ppermute | solution.py:31
  24.2 2.5 %collective-permute-start = (bf16[144,256]{1,0:T(8,128)(2,1)S(1)}, bf16[144,256]{1,0:T(8,128)(2,1)S(1)}, u32[]{:S(2)}, u32[]{:S(2)}) collective-permute-start(bf16[144,256]{1,0:T(8,128)(2,1)S(1)} %get-tuple-element.27.own), channel_id=1, source_target_pairs={{0,1},{1,0},{2,3},{3,2},{4,5},{5,4},{6,7},{7,6},{8,9},{9,8},{10,11... | collective-permute-start | bytes 221192 | tf_op jit(solution)/shard_map/ppermute | solution.py:31
  25.7 1.3 %collective-permute-start.2 = (bf16[144,256]{1,0:T(8,128)(2,1)S(1)}, bf16[144,256]{1,0:T(8,128)(2,1)S(1)}, u32[]{:S(2)}, u32[]{:S(2)}) collective-permute-start(bf16[144,256]{1,0:T(8,128)(2,1)S(1)} %collective-permute-done.1.far), channel_id=1, source_target_pairs={{0,1},{1,0},{2,3},{3,2},{4,5},{5,4},{6,7},{7,6},{8,9},{9,8},{10,11... | collective-permute-start | bytes 221192 | tf_op jit(solution)/shard_map/ppermute | solution.py:31
  30.8 4.8 %collective-permute-start.18 = (bf16[2,64,256]{2,1,0:T(8,128)(2,1)S(1)}, bf16[2,64,256]{2,1,0:T(8,128)(2,1)S(1)}, u32[]{:S(2)}, u32[]{:S(2)}) collective-permute-start(bf16[2,64,256]{2,1,0:T(8,128)(2,1)S(1)} %get-tuple-element.46), channel_id=1, source_target_pairs={{0,2},{1,3},{2,0},{3,1},{4,6},{5,7},{6,4},{7,5},{8,10},{9,11},{10,... | collective-permute-start | bytes 196616 | tf_op jit(solution)/shard_map/ppermute | solution.py:31
  31.6 4.4 %collective-permute-start.19 = (bf16[2,64,256]{2,1,0:T(8,128)(2,1)S(1)}, bf16[2,64,256]{2,1,0:T(8,128)(2,1)S(1)}, u32[]{:S(2)}, u32[]{:S(2)}) collective-permute-start(bf16[2,64,256]{2,1,0:T(8,128)(2,1)S(1)} %get-tuple-element.47), channel_id=1, source_target_pairs={{0,3},{1,2},{2,1},{3,0},{4,7},{5,6},{6,5},{7,4},{8,11},{9,10},{10,... | collective-permute-start | bytes 196616 | tf_op jit(solution)/shard_map/ppermute | solution.py:31
  32.1 3.9 %collective-permute-start.20 = (bf16[2,64,256]{2,1,0:T(8,128)(2,1)S(1)}, bf16[2,64,256]{2,1,0:T(8,128)(2,1)S(1)}, u32[]{:S(2)}, u32[]{:S(2)}) collective-permute-start(bf16[2,64,256]{2,1,0:T(8,128)(2,1)S(1)} %get-tuple-element.48), channel_id=1, source_target_pairs={{0,1},{1,0},{2,3},{3,2},{4,5},{5,4},{6,7},{7,6},{8,9},{9,8},{10,11... | collective-permute-start | bytes 196616 | tf_op jit(solution)/shard_map/ppermute | solution.py:31
